TPU v7x, 32 devices: a whole 2x2x4 slice. The times are simulated.
32 devices in a mesh: groups: 2 (over y), expert: 4 (over x, core), narrow: 4 (over z).
Axes of the slice: x: 2, y: 2, z: 4, core: 2. Of those that a mesh axis runs over, the one named last changes fastest.
Arguments:
- tokens: bfloat16 [512, 3584], P(('groups', 'expert', 'narrow')), parts along dimension 0, may hold values from -6 to 6
- expert_ids: int32 [512, 8], P(('groups', 'expert')), parts along dimension 0, may hold values from 0 to 15, all different within a row; in each aligned block of 64 rows (0 to 63, 64 to 127, ...) at most 48 rows name the same one
- route_weights: float32 [512, 8], P(('groups', 'expert')), parts along dimension 0, may hold values from 0.05 to 0.4
- pair_flags: int32 [256], P(('groups', 'expert', 'narrow')), parts along dimension 0, may hold values 0 or 1
- shared_gate_up: bfloat16 [3584, 2, 2048], P(None, None, 'narrow'), may hold values from -0.09375 to 0.09375
- shared_down: bfloat16 [2048, 3584], P('narrow'), may hold values from -0.125 to 0.125
- expert_gate_up: bfloat16 [16, 3584, 2, 2048], P('expert', None, None, 'narrow'), may hold values from -0.09375 to 0.09375
- expert_down: bfloat16 [16, 2048, 3584], P('expert', 'narrow'), may hold values from -0.125 to 0.125
- readout: float32 [3584], replicated, may hold values from -0.09375 to 0.09375
Outputs:
- mixed: bfloat16 [512, 3584], P(('groups', 'expert', 'narrow')), parts along dimension 0
- pmi_scores: float32 [256], P(('groups', 'expert', 'narrow')), parts along dimension 0
There are 2 independent parts, one for each index of `groups`. A program takes and returns all parts, laid end to end along the dimension named above; an argument that names none is the same for every part. Nothing has to cross between parts.
Inputs may be any that keep to these rules, and one draw needn't show every extreme that they name: `expert_ids`: each row names 8 different experts. In each aligned block of 64 rows no expert is named by more than 48 rows, a bound that some block reaches.
All inputs are finite; a program needn't handle non-finite values. Where the computation divides by a largest or mean magnitude, that divisor is 1e-20 or more. No bound on the sum of `pair_flags` on one device may be relied on, other than what follows from the above.
Results may differ from a plain program's by a relative error of at most 0.012.
Values may be sent and summed in bfloat16 or wider, within the bound.
No kernel may reach another device: no remote copies, remote signals or barrier semaphores. Data moves between devices by JAX's collectives and lax.ppermute only.
A program may use at most 192 MiB of HBM per device.

v0:
```python
import math

import jax
import jax.numpy as jnp
from jax import lax
from jax.sharding import PartitionSpec as P

ROT = 128


def sign_matrix():
    row_index = lax.broadcasted_iota(jnp.int32, (ROT, ROT), 0)
    col_index = lax.broadcasted_iota(jnp.int32, (ROT, ROT), 1)
    common = jnp.bitwise_and(row_index, col_index)
    parity = jnp.zeros((ROT, ROT), jnp.int32)
    for shift_bits in range(ROT.bit_length() - 1):
        parity = parity + jnp.bitwise_and(jnp.right_shift(common, shift_bits), 1)
    return (1 - 2 * jnp.bitwise_and(parity, 1)).astype(jnp.bfloat16)


def quantize(member_rows):
    row_count, feature_len = member_rows.shape
    blocks = member_rows.reshape(row_count * (feature_len // ROT), ROT)
    rotated = jnp.dot(blocks, sign_matrix(), preferred_element_type=jnp.float32) * (
        1.0 / math.sqrt(ROT)
    )
    rotated = rotated.reshape(row_count, feature_len // ROT, ROT)
    block_scale = (jnp.max(jnp.abs(rotated), axis=2) + 1e-06).astype(jnp.bfloat16)
    quantized = (rotated / block_scale.astype(jnp.float32)[:, :, None]).astype(jnp.bfloat16)
    return (quantized.reshape(row_count, feature_len), block_scale)


def expert_partial(pieces, gate_up, down):
    quantized, block_scale = pieces
    sources, local_experts, items, feature_len = quantized.shape
    blocks = feature_len // ROT
    restored = (
        quantized.reshape(sources, local_experts, items, blocks, ROT).astype(jnp.float32)
        * block_scale.astype(jnp.float32)[..., None]
    )
    restored = restored.astype(jnp.bfloat16).reshape(sources, local_experts, items, feature_len)
    gate_up_out = jnp.einsum(
        "seid,edgf->seigf", restored, gate_up, preferred_element_type=jnp.float32
    )
    hidden = (jax.nn.silu(gate_up_out[:, :, :, 0]) * gate_up_out[:, :, :, 1]).astype(jnp.bfloat16)
    return jnp.einsum("seif,efd->seid", hidden, down, preferred_element_type=jnp.float32).astype(
        jnp.bfloat16
    )


def per_device(
    tokens,
    expert_ids,
    route_weights,
    pair_flags,
    shared_gate_up,
    shared_down,
    expert_gate_up,
    expert_down,
    readout,
):
    group_rows = lax.all_gather(tokens, "narrow", axis=0, tiled=True)
    rows_e, feature_len = group_rows.shape
    top_count = expert_ids.shape[1]
    exp_dev = expert_gate_up.shape[0]
    expert_count = lax.axis_size("expert")
    experts = exp_dev * expert_count
    capacity = min(rows_e, 3 * top_count * rows_e // (2 * experts))
    blocks = feature_len // ROT
    shared_both = jnp.einsum(
        "rd,dgf->rgf", group_rows, shared_gate_up, preferred_element_type=jnp.float32
    )
    shared_hidden = (jax.nn.silu(shared_both[:, 0]) * shared_both[:, 1]).astype(jnp.bfloat16)
    shared_part = jnp.dot(shared_hidden, shared_down, preferred_element_type=jnp.float32)
    quantized, block_scale = quantize(group_rows)
    flat_ids = expert_ids.reshape(-1)
    columns = lax.broadcasted_iota(jnp.int32, (1, experts), 1)
    onehot = (flat_ids[:, None] == columns).astype(jnp.int32)
    position = jnp.sum((jnp.cumsum(onehot, axis=0) - 1) * onehot, axis=1)
    slot_index = flat_ids * capacity + position
    entry_token = lax.broadcasted_iota(jnp.int32, (rows_e * top_count,), 0) // top_count
    token_of = jnp.full((experts * capacity,), rows_e, jnp.int32).at[slot_index].set(entry_token)
    quant_pad = jnp.concatenate([quantized, jnp.zeros((1, feature_len), jnp.bfloat16)], axis=0)
    scale_pad = jnp.concatenate([block_scale, jnp.zeros((1, blocks), jnp.bfloat16)], axis=0)
    outgoing = quant_pad[token_of].reshape(expert_count, exp_dev, capacity, feature_len)
    out_scale = scale_pad[token_of].reshape(expert_count, exp_dev, capacity, blocks)
    partial_value = expert_partial(
        (
            lax.all_to_all(outgoing, "expert", split_axis=0, concat_axis=0, tiled=True),
            lax.all_to_all(out_scale, "expert", split_axis=0, concat_axis=0, tiled=True),
        ),
        expert_gate_up,
        expert_down,
    )
    weights = route_weights.reshape(-1)
    returned = lax.all_to_all(partial_value, "expert", split_axis=0, concat_axis=0, tiled=True)
    picked = (
        returned.reshape(experts * capacity, feature_len)[slot_index].astype(jnp.float32)
        * weights[:, None]
    )
    routed = jnp.sum(picked.reshape(rows_e, top_count, feature_len), axis=1)
    total_sum = lax.psum_scatter(
        (shared_part + routed).astype(jnp.bfloat16), "narrow", scatter_dimension=0, tiled=True
    ).astype(jnp.float32)
    mixed = total_sum.astype(jnp.bfloat16)
    row_score = jnp.sum(total_sum * readout[None, :], axis=1) / jnp.sqrt(
        jnp.mean(total_sum * total_sum, axis=1) + 1e-06
    )
    paired = row_score.reshape(-1, 2)
    pmi_scores = (paired[:, 0] - paired[:, 1]) * (1 - 2 * pair_flags).astype(jnp.float32)
    return (mixed, pmi_scores)


def solution(mesh):
    in_specs = (
        P(("groups", "expert", "narrow"), None),
        P(("groups", "expert"), None),
        P(("groups", "expert"), None),
        P(("groups", "expert", "narrow")),
        P(None, None, "narrow"),
        P("narrow", None),
        P("expert", None, None, "narrow"),
        P("expert", "narrow", None),
        P(),
    )
    out_specs = (P(("groups", "expert", "narrow"), None), P(("groups", "expert", "narrow")))
    return jax.shard_map(
        per_device, mesh=mesh, in_specs=in_specs, out_specs=out_specs, check_vma=False
    )
```

profile of v0, /device:TPU:0, one launch (start us, length us, event | category | flops | bytes accessed | tf_op | source)
XLA Modules:
  0.0 260.1 jit_solution(3863930255259067022)
XLA Ops:
  7.2 0.7 broadcast_multiply_fusion
  7.9 0.8 copy.31
  8.6 0.1 eq.25
  8.7 0.1 eq.29
  8.8 17.0 %all_gather.3 = bf16[64,3584]{1,0:T(8,128)(2,1)S(1)} all-gather(bf16[16,3584]{1,0:T(8,128)(2,1)} %param.9), channel_id=1, replica_groups=mesh['groups'=2,'expert'=4,'narrow'=4] {'narrow'}, dimensions={0}, use_global_device_ids=true | all-gather | bytes 573440 | tf_op jit(solution)/shard_map/all_gather | solution.py:62
  25.8 0.6 reshape.107
  26.4 0.4 abs_reduce_fusion
  26.8 0.1 convert_element_type.72
  26.9 0.1 copy.30
  27.0 0.1 mul.90
  27.1 1.2 reduce-window.6
  28.2 0.2 slice_reduce_fusion
  28.5 0.1 fusion.35
  28.6 2.4 scatter_custom_fusion
  31.1 1.9 gather_fusion.1
  33.0 0.2 copy.34
  33.2 0.8 reshape.156
  34.0 3.3 %all-to-all-start.1 = ((bf16[4,2,2688]{2,1,0:T(2,128)(2,1)}), bf16[4,2,2688]{2,1,0:T(2,128)(2,1)S(1)}, u32[]{:S(2)}, u32[]{:S(2)}) async-start(bf16[4,2,2688]{2,1,0:T(2,128)(2,1)} %reshape.156), calls=%async_computation.1 | async-start | bytes 86016 | tf_op jit(solution)/shard_map/all_to_all | solution.py:90
  37.3 0.3 copy.29
  37.6 0.1 reshape.108
  37.7 0.3 div.36
  38.0 0.7 fusion.24
  38.8 5.4 %gather_fusion = bf16[768,3584]{1,0:T(8,128)(2,1)} fusion(bf16[65,3584]{1,0:T(8,128)(2,1)S(1)} %concatenate.6, s32[1024]{0:T(1024)S(1)} %pad_clamp_fusion.1), kind=kCustom, calls=%fused_computation | custom fusion | bytes 11013120 | tf_op jit(solution)/shard_map/gather | solution.py:85
  44.2 0.0 all-to-all-done.1
  44.2 5.3 %all-to-all-start = ((bf16[4,4,48,3584]{3,2,1,0:T(8,128)(2,1)}), bf16[4,4,48,3584]{3,2,1,0:T(8,128)(2,1)}, u32[]{:S(2)}, u32[]{:S(2)}) async-start(bf16[4,4,48,3584]{3,2,1,0:T(8,128)(2,1)} %bitcast.81), calls=%async_computation | async-start | bytes 11010048 | tf_op jit(solution)/shard_map/all_to_all | solution.py:89
  49.5 0.2 reshape.157
  49.6 0.2 copy.35
  49.8 7.1 %mul.92 = f32[4,4,48,28,128]{4,3,2,1,0:T(8,128)} broadcast(f32[4,4,48,28]{3,2,1,0:T(8,128)S(1)} %copy.35), dimensions={0,1,2,3} | broadcast | bytes 11096064 | tf_op jit(solution)/shard_map/mul | solution.py:38
  57.0 13.2 %mul.93 = f32[4,4,48,3584]{3,2,1,0:T(8,128)} reshape(f32[4,4,48,28,128]{4,3,2,1,0:T(8,128)} %mul.92) | data formatting | bytes 22020096 | tf_op jit(solution)/shard_map/mul | solution.py:38
  70.2 41.5 %all-to-all-done = bf16[4,4,48,3584]{3,2,1,0:T(8,128)(2,1)} async-done(((bf16[4,4,48,3584]{3,2,1,0:T(8,128)(2,1)}), bf16[4,4,48,3584]{3,2,1,0:T(8,128)(2,1)}, u32[]{:S(2)}, u32[]{:S(2)}) %all-to-all-start) | async-done | bytes 5505056 | tf_op jit(solution)/shard_map/all_to_all | solution.py:89
  111.7 20.1 %fusion.17 = f32[4,4,48,2,512]{4,2,3,0,1:T(8,128)} fusion(bf16[4,3584,2,512,1]{3,2,1,0,4:T(2,128)(2,1)} %bitcast.89, f32[4,4,48,3584]{3,2,1,0:T(8,128)} %mul.93, bf16[4,4,48,3584]{3,2,1,0:T(8,128)(2,1)} %all-to-all-done), kind=kOutput, calls=%fused_computation.21 | convolution fusion | flops 5645402112 | bytes 49020928 | tf_op jit(solution)/shard_map/seid,edgf->seigf/dot_general | solution.py:42
  131.8 9.2 %fusion.10 = bf16[4,4,48,3584]{3,2,0,1:T(8,128)(2,1)S(1)} fusion(bf16[4,512,3584]{2,1,0:T(8,128)(2,1)} %param.16, f32[4,4,48,2,512]{4,2,3,0,1:T(8,128)} %fusion.17), kind=kOutput, calls=%fused_computation.14 | convolution fusion | flops 2823684096 | bytes 23330816 | tf_op jit(solution)/shard_map/seif,efd->seid/dot_general | solution.py:46
  141.0 2.9 %copy.39 = bf16[4,4,48,3584]{3,2,1,0:T(8,128)(2,1)} copy(bf16[4,4,48,3584]{3,2,0,1:T(8,128)(2,1)S(1)} %fusion.10) | data formatting | bytes 11010048 | tf_op jit(solution)/shard_map/convert_element_type | solution.py:46
  143.9 5.2 %all-to-all-start.2 = ((bf16[4,4,48,3584]{3,2,1,0:T(8,128)(2,1)}), bf16[4,4,48,3584]{3,2,1,0:T(8,128)(2,1)}, u32[]{:S(2)}, u32[]{:S(2)}) async-start(bf16[4,4,48,3584]{3,2,1,0:T(8,128)(2,1)} %copy.39), calls=%async_computation.2 | async-start | bytes 11010048 | tf_op jit(solution)/shard_map/all_to_all | solution.py:96
  149.1 0.3 reduce-scatter.2.cloned.1.call-start
  149.4 0.1 copy.40
  149.5 4.5 %fusion.5 = f32[64,2,512]{2,0,1:T(8,128)S(1)} fusion(bf16[3584,2,512]{2,1,0:T(2,128)(2,1)} %param.13, bf16[64,3584]{1,0:T(8,128)(2,1)S(1)} %all_gather.3), kind=kOutput, calls=%fused_computation.11 | convolution fusion | flops 469762048 | bytes 8060928 | tf_op jit(solution)/shard_map/rd,dgf->rgf/dot_general | solution.py:70
  153.9 57.4 %all-to-all-done.2 = bf16[4,4,48,3584]{3,2,1,0:T(8,128)(2,1)} async-done(((bf16[4,4,48,3584]{3,2,1,0:T(8,128)(2,1)}), bf16[4,4,48,3584]{3,2,1,0:T(8,128)(2,1)}, u32[]{:S(2)}, u32[]{:S(2)}) %all-to-all-start.2) | async-done | bytes 5505056 | tf_op jit(solution)/shard_map/all_to_all | solution.py:96
  211.4 11.2 %gather_fusion.2 = bf16[512,3584]{1,0:T(8,128)(2,1)} fusion(bf16[768,3584]{1,0:T(8,128)(2,1)} %bitcast.17, s32[1024]{0:T(1024)S(1)} %pad_clamp_fusion), kind=kCustom, calls=%fused_computation.2 | custom fusion | bytes 7342080 | tf_op jit(solution)/shard_map/gather | solution.py:98
  222.6 5.2 %fusion.4 = f32[64,3584]{1,0:T(8,128)S(1)} fusion(bf16[512,3584]{1,0:T(8,128)(2,1)} %gather_fusion.2, f32[64,8]{1,0:T(8,128)S(1)} %copy.40), kind=kLoop, calls=%fused_computation.10 | loop fusion | flops 5275648 | bytes 4589568 | tf_op jit(solution)/shard_map/reduce_sum | solution.py:101
  227.9 1.5 fusion.15
  229.4 0.0 reduce-scatter.2.cloned.1.call-update
  229.4 22.0 %reduce-scatter.2.cloned.1.call-done = bf16[16,3584]{1,0:T(8,128)(2,1)} async-done(((bf16[64,3584]{1,0:T(8,128)(2,1)}), bf16[16,3584]{1,0:T(8,128)(2,1)}) %reduce-scatter.2.cloned.1.call-update) | async-done | bytes 114704 | tf_op jit(solution)/shard_map/reduce_scatter | solution.py:102
  251.4 0.0 copy-done.1
  251.4 1.0 fusion.29
  252.5 0.1 div.44
  252.6 0.2 subtract_reduce_fusion
  252.8 0.5 convert_multiply_fusion.3
  (19 shorter events, 0.1 us)
Async XLA Ops:
  34.0 10.2 %all-to-all-start.1 = ((bf16[4,2,2688]{2,1,0:T(2,128)(2,1)}), bf16[4,2,2688]{2,1,0:T(2,128)(2,1)S(1)}, u32[]{:S(2)}, u32[]{:S(2)}) async-start(bf16[4,2,2688]{2,1,0:T(2,128)(2,1)} %reshape.156), calls=%async_computation.1 | async-start | bytes 86016 | tf_op jit(solution)/shard_map/all_to_all | solution.py:90
  44.2 67.5 %all-to-all-start = ((bf16[4,4,48,3584]{3,2,1,0:T(8,128)(2,1)}), bf16[4,4,48,3584]{3,2,1,0:T(8,128)(2,1)}, u32[]{:S(2)}, u32[]{:S(2)}) async-start(bf16[4,4,48,3584]{3,2,1,0:T(8,128)(2,1)} %bitcast.81), calls=%async_computation | async-start | bytes 11010048 | tf_op jit(solution)/shard_map/all_to_all | solution.py:89
  143.9 5.5 %copy-start.2 = (f32[64,8]{0,1:T(8,128)S(1)}, f32[64,8]{0,1:T(8,128)}, u32[]{:S(2)}) copy-start(f32[64,8]{0,1:T(8,128)} %param.11) | copy-start | bytes 6148
  143.9 67.5 %all-to-all-start.2 = ((bf16[4,4,48,3584]{3,2,1,0:T(8,128)(2,1)}), bf16[4,4,48,3584]{3,2,1,0:T(8,128)(2,1)}, u32[]{:S(2)}, u32[]{:S(2)}) async-start(bf16[4,4,48,3584]{3,2,1,0:T(8,128)(2,1)} %copy.39), calls=%async_computation.2 | async-start | bytes 11010048 | tf_op jit(solution)/shard_map/all_to_all | solution.py:96
  149.1 102.3 %reduce-scatter.2.cloned.1.call-start = ((), (), s32[]{:S(2)}) async-start(), calls=%async_computation.4 | async-start | bytes 573440 | tf_op jit(solution)/shard_map/reduce_scatter | solution.py:102
  222.6 5.2 %copy-start = (bf16[512,3584]{1,0:T(8,128)(2,1)S(1)}, bf16[512,3584]{1,0:T(8,128)(2,1)}, u32[]{:S(2)}) copy-start(bf16[512,3584]{1,0:T(8,128)(2,1)} %param.14) | copy-start | bytes 11010052
  222.6 28.8 %copy-start.1 = (f32[3584]{0:T(1024)S(1)}, f32[3584]{0:T(1024)}, u32[]{:S(2)}) copy-start(f32[3584]{0:T(1024)} %param.17) | copy-start | bytes 43012
  222.6 30.1 %copy-start.3 = (s32[8]{0:T(128)S(1)}, s32[8]{0:T(128)}, u32[]{:S(2)}) copy-start(s32[8]{0:T(128)} %param.12) | copy-start | bytes 100
Sparse Core Ops, SparseCore 0:
  229.5 21.8 reduce-scatter.1
where the time goes:
time: 261 us; the launch traced here: 260 us
  waiting for transfers between devices  121 us (46%)
  local copies, waits for them, and re-layouts  48.6 us (19%)
  matrix products  35.6 us (14%)
  blocking collectives  17 us (7%)
  between operations  14.2 us (5%)
  starting transfers between devices  14 us (5%)
  other arithmetic  9.64 us (4%)
    all_to_all x1, waiting for transfers between devices, per_device(): lax.all_to_all(partial_value, 'expert', split_axis=0, concat_axis=0, tile...  57.4 us
    all_to_all x1, waiting for transfers between devices, per_device(): lax.all_to_all(outgoing, 'expert', split_axis=0, concat_axis=0, tiled=True)  41.5 us
    reduce_scatter x1, waiting for transfers between devices, per_device(): lax.psum_scatter((shared_part + routed).astype(jnp.bfloat16), 'narrow', s...  22 us
    mul x2, local copies, waits for them, and re-layouts, expert_partial(): quantized.reshape(sources, local_experts, items, blocks, ROT)  20.3 us
    dot_general x1, matrix products, expert_partial(): jnp.einsum('seid,edgf->seigf', restored, gate_up, preferred_element_type=...  20.1 us
    all_gather x1, blocking collectives, per_device(): group_rows = lax.all_gather(tokens, 'narrow', axis=0, tiled=True)  17 us
    gather x1, local copies, waits for them, and re-layouts, per_device(): returned.reshape(experts * capacity, feature_len)[slot_index]  11.2 us
    dot_general x1, matrix products, expert_partial(): jnp.einsum('seif,efd->seid', hidden, down, preferred_element_type=jnp.flo...  9.17 us
  transfers between devices with their start and end apart: 4, of which 3 were waited for; matrix products, arithmetic and copies ran while one was open for 12% of the time, Pallas kernels for 0%

commit v1 on v0

v1 whole, which is shorter than its diff:
```python
import functools
import math

import jax
import jax.numpy as jnp
from jax import lax
from jax.experimental import pallas as pl
from jax.experimental.pallas import tpu as pltpu
from jax.sharding import PartitionSpec as P

ROT = 128
CORES = 2
VMEM_BYTES = 30 * 1024 * 1024
SCATTER_CHUNKS = 2


def sign_matrix(copies):
    size = copies * ROT
    row_index = lax.broadcasted_iota(jnp.int32, (size, size), 0)
    col_index = lax.broadcasted_iota(jnp.int32, (size, size), 1)
    common = jnp.bitwise_and(row_index % ROT, col_index % ROT)
    parity = jnp.zeros((size, size), jnp.int32)
    for shift_bits in range(ROT.bit_length() - 1):
        parity = parity + jnp.bitwise_and(jnp.right_shift(common, shift_bits), 1)
    signs = 1 - 2 * jnp.bitwise_and(parity, 1)
    return jnp.where(row_index // ROT == col_index // ROT, signs, 0).astype(jnp.bfloat16)


def hidden_kernel(n_pieces, n_tiles, n_local, *refs):
    pieces = refs[:n_pieces]
    select, signs, gate_up, shared, hidden, shared_hidden, rows_s, deq_s, combine_s = refs[n_pieces:]
    step = pl.program_id(0)
    feature_len = deq_s.shape[1]
    width = signs.shape[0]

    @pl.when(step == 0)
    def _():
        base = 0
        for piece in pieces:
            count = piece.shape[0]
            rows_s[base : base + count, :] = piece[:, :feature_len]
            combine_s[base : base + count, :] = piece[:, feature_len:].astype(jnp.float32)
            base += count

        def block(index, carry):
            at = pl.ds(pl.multiple_of(index * width, width), width)
            rotated = jnp.dot(
                rows_s[:, at], signs[...], preferred_element_type=jnp.float32
            ) * (1.0 / math.sqrt(ROT))
            parts = []
            for piece_at in range(0, width, ROT):
                part = rotated[:, piece_at : piece_at + ROT]
                scale = (jnp.max(jnp.abs(part), axis=1, keepdims=True) + 1e-06).astype(jnp.bfloat16)
                scale = scale.astype(jnp.float32)
                quantized = (part / scale).astype(jnp.bfloat16)
                parts.append((quantized.astype(jnp.float32) * scale).astype(jnp.bfloat16))
            deq_s[:, at] = jnp.concatenate(parts, axis=1)
            return carry

        lax.fori_loop(0, feature_len // width, block, 0)
        gate = jnp.dot(rows_s[...], shared[0], preferred_element_type=jnp.float32)
        up = jnp.dot(rows_s[...], shared[1], preferred_element_type=jnp.float32)
        shared_hidden[...] = (gate / (1.0 + jnp.exp(-gate)) * up).astype(jnp.bfloat16)

    gate = jnp.dot(deq_s[...], gate_up[0, 0], preferred_element_type=jnp.float32)
    up = jnp.dot(deq_s[...], gate_up[0, 1], preferred_element_type=jnp.float32)
    local = step // (n_tiles // n_local)
    weight = jnp.sum(combine_s[...] * select[pl.ds(local, 1), :], axis=1, keepdims=True)
    hidden[...] = (gate / (1.0 + jnp.exp(-gate)) * up * weight).astype(jnp.bfloat16)


def hidden_rows(pieces, select, gate_up, shared):
    n_local, _, feature_len, inner = gate_up.shape
    rows = sum(piece.shape[0] for piece in pieces)
    signs = sign_matrix(2 if feature_len % (2 * ROT) == 0 else 1)
    tile = min(inner, 256)
    per = inner // tile
    whole = pl.BlockSpec(memory_space=pltpu.VMEM)
    return pl.pallas_call(
        functools.partial(hidden_kernel, len(pieces), n_local * per, n_local),
        grid=(n_local * per,),
        in_specs=[whole] * (len(pieces) + 2)
        + [pl.BlockSpec((1, 2, feature_len, tile), lambda s: (s // per, 0, 0, s % per)), whole],
        out_specs=[pl.BlockSpec((rows, tile), lambda s: (0, s)), whole],
        out_shape=[
            jax.ShapeDtypeStruct((rows, n_local * inner), jnp.bfloat16),
            jax.ShapeDtypeStruct((rows, shared.shape[2]), jnp.bfloat16),
        ],
        scratch_shapes=[
            pltpu.VMEM((rows, feature_len), jnp.bfloat16),
            pltpu.VMEM((rows, feature_len), jnp.bfloat16),
            pltpu.VMEM((rows, select.shape[1]), jnp.float32),
        ],
        compiler_params=pltpu.CompilerParams(vmem_limit_bytes=VMEM_BYTES),
        name="hidden_rows",
    )(*pieces, select, signs, gate_up, shared)


def down_kernel(hidden, shared_hidden, down, shared_down, out):
    out[...] = (
        jnp.dot(hidden[...], down[...], preferred_element_type=jnp.float32)
        + jnp.dot(shared_hidden[...], shared_down[...], preferred_element_type=jnp.float32)
    ).astype(out.dtype)


def down_rows(hidden, shared_hidden, down, shared_down, start, stop):
    rows = hidden.shape[0]
    inner = down.shape[0]
    tile = math.gcd(512, math.gcd(start, stop - start))
    first = start // tile
    whole = pl.BlockSpec(memory_space=pltpu.VMEM)
    return pl.pallas_call(
        down_kernel,
        grid=((stop - start) // tile,),
        in_specs=[
            whole,
            whole,
            pl.BlockSpec((inner, tile), lambda s: (0, first + s)),
            pl.BlockSpec((shared_down.shape[0], tile), lambda s: (0, first + s)),
        ],
        out_specs=pl.BlockSpec((rows, tile), lambda s: (0, s)),
        out_shape=jax.ShapeDtypeStruct((rows, stop - start), jnp.bfloat16),
        compiler_params=pltpu.CompilerParams(vmem_limit_bytes=VMEM_BYTES),
        name="down_rows",
    )(hidden, shared_hidden, down, shared_down)


def exchange(value, axis, flip):
    return lax.ppermute(value, axis, [(i, i ^ flip) for i in range(lax.axis_size(axis))])


def per_device(
    tokens,
    expert_ids,
    route_weights,
    pair_flags,
    shared_gate_up,
    shared_down,
    expert_gate_up,
    expert_down,
    readout,
):
    own_rows, feature_len = tokens.shape
    n_local, _, _, inner = expert_gate_up.shape
    expert_count = lax.axis_size("expert")
    narrow_count = lax.axis_size("narrow")
    chips = expert_count // CORES
    experts = n_local * expert_count
    expert_at = lax.axis_index("expert")
    narrow_at = lax.axis_index("narrow")

    ids = lax.dynamic_slice_in_dim(expert_ids, narrow_at * own_rows, own_rows, 0)
    chosen = lax.dynamic_slice_in_dim(route_weights, narrow_at * own_rows, own_rows, 0)
    named = lax.broadcasted_iota(jnp.int32, (1, 1, experts), 2)
    combine = jnp.sum(jnp.where(ids[:, :, None] == named, chosen[:, :, None], 0.0), axis=1)
    high = combine.astype(jnp.bfloat16)
    low = (combine - high.astype(jnp.float32)).astype(jnp.bfloat16)
    columns = -(-2 * experts // 128) * 128
    lanes = jnp.pad(jnp.concatenate([high, low], axis=1), ((0, 0), (0, columns - 2 * experts)))
    sent = jnp.concatenate([tokens, lanes], axis=1)
    local_ids = expert_at * n_local + lax.broadcasted_iota(jnp.int32, (n_local, columns), 0)
    column = lax.broadcasted_iota(jnp.int32, (n_local, columns), 1)
    select = ((column == local_ids) | (column == local_ids + experts)).astype(jnp.float32)

    along_z = jnp.concatenate(
        [sent] + [exchange(sent, "narrow", flip) for flip in range(1, narrow_count)], axis=0
    )
    chip_parts = [along_z] + [
        exchange(along_z, "expert", flip * CORES) for flip in range(1, chips)
    ]
    core_parts = [exchange(part, "expert", 1) for part in chip_parts]

    shared_len = shared_down.shape[0]
    part_len = shared_len // expert_count
    gate_up = jnp.transpose(expert_gate_up, (0, 2, 1, 3))
    if part_len % 128 == 0:
        shared_in = lax.dynamic_slice_in_dim(shared_gate_up, expert_at * part_len, part_len, 2)
        shared_out = lax.dynamic_slice_in_dim(shared_down, expert_at * part_len, part_len, 0)
    else:
        mine = lax.broadcasted_iota(jnp.int32, (shared_len, 1), 0) // part_len == expert_at
        shared_in = shared_gate_up
        shared_out = jnp.where(mine, shared_down, jnp.zeros_like(shared_down))
    shared_in = jnp.transpose(shared_in, (1, 0, 2))

    hidden, shared_hidden = hidden_rows(chip_parts + core_parts, select, gate_up, shared_in)
    down = expert_down.reshape(n_local * inner, feature_len)

    half = own_rows * narrow_count * chips
    totals = []
    width = feature_len // SCATTER_CHUNKS
    for chunk in range(SCATTER_CHUNKS):
        part = down_rows(
            hidden, shared_hidden, down, shared_out, chunk * width, (chunk + 1) * width
        )
        near = exchange(part[half:], "expert", 1)
        by_core = part[:half].astype(jnp.float32) + near.astype(jnp.float32)
        by_core = by_core.reshape(chips, narrow_count * own_rows, width)
        by_chip = by_core[0]
        for flip in range(1, chips):
            by_chip = by_chip + exchange(
                by_core[flip].astype(jnp.bfloat16), "expert", flip * CORES
            ).astype(jnp.float32)
        by_chip = by_chip.reshape(narrow_count, own_rows, width)
        total = by_chip[0]
        for flip in range(1, narrow_count):
            total = total + exchange(
                by_chip[flip].astype(jnp.bfloat16), "narrow", flip
            ).astype(jnp.float32)
        totals.append(total)
    total_sum = jnp.concatenate(totals, axis=1)
    mixed = total_sum.astype(jnp.bfloat16)
    row_score = jnp.sum(total_sum * readout[None, :], axis=1) / jnp.sqrt(
        jnp.mean(total_sum * total_sum, axis=1) + 1e-06
    )
    paired = row_score.reshape(-1, 2)
    pmi_scores = (paired[:, 0] - paired[:, 1]) * (1 - 2 * pair_flags).astype(jnp.float32)
    return (mixed, pmi_scores)


def solution(mesh):
    in_specs = (
        P(("groups", "expert", "narrow"), None),
        P(("groups", "expert"), None),
        P(("groups", "expert"), None),
        P(("groups", "expert", "narrow")),
        P(None, None, "narrow"),
        P("narrow", None),
        P("expert", None, None, "narrow"),
        P("expert", "narrow", None),
        P(),
    )
    out_specs = (P(("groups", "expert", "narrow"), None), P(("groups", "expert", "narrow")))
    return jax.shard_map(
        per_device, mesh=mesh, in_specs=in_specs, out_specs=out_specs, check_vma=False
    )
```

time: 261 us -> 112 us (0.43)
  waiting for transfers between devices: 121 us -> 24.1 us
  matrix products: 35.6 us -> 0 us
  Pallas kernels: 0 us -> 28.8 us
  local copies, waits for them, and re-layouts: 48.6 us -> 31.6 us
  blocking collectives: 17 us -> 0 us
  between operations: 14.2 us -> 0.96 us
  starting transfers between devices: 14 us -> 21.2 us
  other arithmetic: 9.64 us -> 4.96 us
    all_to_all x3 -> x0, waiting for transfers between devices: 99 us -> none  [the longest x1 57.4 us: per_device(): lax.all_to_all(partial_value, 'expert', split_axis=0, concat_axis=0, tile...]
    dot_general x5 -> x0, matrix products: 35.6 us -> none  [the longest x1 20.1 us: expert_partial(): jnp.einsum('seid,edgf->seigf', restored, gate_up, preferred_element_type=...]
    pallas_call x0 -> x3, Pallas kernels: none -> 28.8 us  [the longest x1 21 us: hidden_rows(): pl.pallas_call(functools.partial(hidden_kernel, len(pieces), n_local * pe...]
    unnamed x12 -> x36, local copies, waits for them, and re-layouts: 1.83 us -> 26.1 us
    ppermute x0 -> x16, waiting for transfers between devices: none -> 24.1 us  [exchange(): lax.ppermute(value, axis, [(i, i ^ flip) for i in range(lax.axis_size(axi...]
    reduce_scatter x1 -> x0, waiting for transfers between devices: 22 us -> none  [per_device(): lax.psum_scatter((shared_part + routed).astype(jnp.bfloat16), 'narrow', s...]
    ppermute x0 -> x16, starting transfers between devices: none -> 21.2 us  [exchange(): lax.ppermute(value, axis, [(i, i ^ flip) for i in range(lax.axis_size(axi...]
    mul x5 -> x0, local copies, waits for them, and re-layouts: 20.8 us -> none  [the longest x2 20.3 us: expert_partial(): quantized.reshape(sources, local_experts, items, blocks, ROT)]
  transfers between devices with their start and end apart: 4 -> 16, of which waited for: 3 -> 7; matrix products, arithmetic and copies ran while one was open for 12% -> 24% of each run, Pallas kernels for 0% -> 4%
where the time goes in v1:
time: 112 us
  local copies, waits for them, and re-layouts  31.6 us (28%)
  Pallas kernels  28.8 us (26%)
  waiting for transfers between devices  24.1 us (22%)
  starting transfers between devices  21.2 us (19%)
  other arithmetic  4.96 us (4%)
    unnamed x36, local copies, waits for them, and re-layouts  26.1 us
    ppermute x16, waiting for transfers between devices, exchange(): lax.ppermute(value, axis, [(i, i ^ flip) for i in range(lax.axis_size(axi...  24.1 us
    ppermute x16, starting transfers between devices, exchange(): lax.ppermute(value, axis, [(i, i ^ flip) for i in range(lax.axis_size(axi...  21.2 us
    pallas_call x1, Pallas kernels, hidden_rows(): pl.pallas_call(functools.partial(hidden_kernel, len(pieces), n_local * pe...  21 us
    pallas_call x2, Pallas kernels, down_rows(): pl.pallas_call(down_kernel, grid=((stop - start) // tile,), in_specs=[who...  7.83 us
    dynamic_slice x1, local copies, waits for them, and re-layouts, per_device(): lax.dynamic_slice_in_dim(shared_gate_up, expert_at * part_len, part_len, 2)  3.06 us
  transfers between devices with their start and end apart: 16, of which 7 were waited for; matrix products, arithmetic and copies ran while one was open for 24% of the time, Pallas kernels for 4%

profile of v1, /device:TPU:0, one launch (start us, length us, event | category | flops | bytes accessed | tf_op | source)
XLA Modules:
  0.0 111.7 jit_solution(13810940999341143032)
XLA Ops:
  0.7 0.7 copy-done
  1.4 0.1 copy.19
  1.5 0.8 constant_dynamic-slice_fusion.2
  2.2 0.1 copy.20
  2.3 0.1 select_reduce_fusion
  2.4 0.1 fusion.7
  2.5 0.9 pad_maximum_fusion.2
  3.4 3.1 %collective-permute-start = (bf16[16,3712]{1,0:T(8,128)(2,1)S(1)}, bf16[16,3712]{1,0:T(8,128)(2,1)S(1)}, u32[]{:S(2)}, u32[]{:S(2)}) collective-permute-start(bf16[16,3712]{1,0:T(8,128)(2,1)S(1)} %pad_maximum_fusion.2), channel_id=1, source_target_pairs={{0,1},{1,0},{2,3},{3,2},{4,5},{5,4},{6,7},{7,6},{8,9},{9,8},{10,11... | collective-permute-start | bytes 356360 | tf_op jit(solution)/shard_map/ppermute | solution.py:129
  6.5 2.6 %collective-permute-start.1 = (bf16[16,3712]{1,0:T(8,128)(2,1)S(1)}, bf16[16,3712]{1,0:T(8,128)(2,1)S(1)}, u32[]{:S(2)}, u32[]{:S(2)}) collective-permute-start(bf16[16,3712]{1,0:T(8,128)(2,1)S(1)} %pad_maximum_fusion.2), channel_id=1, source_target_pairs={{0,2},{1,3},{2,0},{3,1},{4,6},{5,7},{6,4},{7,5},{8,10},{9,11},{10,... | collective-permute-start | bytes 356360 | tf_op jit(solution)/shard_map/ppermute | solution.py:129
  9.1 1.9 %collective-permute-done = bf16[16,3712]{1,0:T(8,128)(2,1)S(1)} collective-permute-done((bf16[16,3712]{1,0:T(8,128)(2,1)S(1)}, bf16[16,3712]{1,0:T(8,128)(2,1)S(1)}, u32[]{:S(2)}, u32[]{:S(2)}) %collective-permute-start) | collective-permute-done | bytes 118816 | tf_op jit(solution)/shard_map/ppermute | solution.py:129
  11.0 7.5 %collective-permute-done.1 = bf16[16,3712]{1,0:T(8,128)(2,1)S(1)} collective-permute-done((bf16[16,3712]{1,0:T(8,128)(2,1)S(1)}, bf16[16,3712]{1,0:T(8,128)(2,1)S(1)}, u32[]{:S(2)}, u32[]{:S(2)}) %collective-permute-start.1) | collective-permute-done | bytes 118816 | tf_op jit(solution)/shard_map/ppermute | solution.py:129
  18.5 0.9 pad_maximum_fusion.refs_0_
  19.4 1.6 %collective-permute-start.3 = (bf16[64,3712]{1,0:T(8,128)(2,1)S(1)}, bf16[64,3712]{1,0:T(8,128)(2,1)}, u32[]{:S(2)}, u32[]{:S(2)}) collective-permute-start(bf16[64,3712]{1,0:T(8,128)(2,1)S(1)} %pad_maximum_fusion.refs_0_), channel_id=1, source_target_pairs={{0,8},{4,12},{8,0},{12,4},{1,9},{5,13},{9,1},{13,5},{2,10},{6,14},... | collective-permute-start | bytes 1425416 | tf_op jit(solution)/shard_map/ppermute | solution.py:129
  21.0 1.0 select_convert_fusion.refs_5_
  22.0 3.1 %constant_dynamic-slice_fusion.1 = bf16[3584,2,128]{2,1,0:T(2,128)(2,1)S(1)} fusion(bf16[3584,2,512]{2,1,0:T(2,128)(2,1)} %param.13, s32[]{:T(128)S(6)} %select_n.42), kind=kLoop, calls=%fused_computation.40 | loop fusion | bytes 3670020 | tf_op jit(solution)/shard_map/dynamic_slice | solution.py:177
  25.0 0.1 collective-permute-start.4
  25.1 4.8 %collective-permute-done.3.refs_1_ = bf16[64,3712]{1,0:T(8,128)(2,1)} collective-permute-done((bf16[64,3712]{1,0:T(8,128)(2,1)S(1)}, bf16[64,3712]{1,0:T(8,128)(2,1)}, u32[]{:S(2)}, u32[]{:S(2)}) %collective-permute-start.3) | collective-permute-done | bytes 475168 | tf_op jit(solution)/shard_map/ppermute | solution.py:129
  30.0 0.2 copy.27
  30.2 20.4 %copy.26 = bf16[4,3584,2,512]{3,1,2,0:T(8,128)(2,1)} copy(bf16[4,3584,2,512]{3,2,1,0:T(2,128)(2,1)} %param.15) | data formatting | bytes 58720256 | tf_op args[6]
  50.7 1.2 %constant_dynamic-slice_fusion.shared_down = bf16[128,3584]{1,0:T(8,128)(2,1)S(1)} fusion(bf16[512,3584]{1,0:T(8,128)(2,1)} %param.14, s32[]{:T(128)S(6)} %select_n.42), kind=kLoop, calls=%fused_computation.39 | loop fusion | bytes 1835012 | tf_op jit(solution)/shard_map/dynamic_slice | solution.py:178
  52.0 1.0 copy-done.4
  53.0 21.0 %hidden_rows.1 = (bf16[256,2048]{1,0:T(8,128)(2,1)S(1)}, bf16[256,128]{1,0:T(8,128)(2,1)S(1)}) custom-call(bf16[64,3712]{1,0:T(8,128)(2,1)S(1)} %pad_maximum_fusion.refs_0_, bf16[64,3712]{1,0:T(8,128)(2,1)} %collective-permute-done.3.refs_1_, bf16[64,3712]{1,0:T(8,128)(2,1)} %collective-permute-done.4.refs_2_, ...), custom_call_target="tpu_custom_call" | custom-call | tf_op jit(solution)/shard_map/hidden_rows/pallas_call | solution.py:79
  74.1 1.0 copy-done.2
  75.0 0.6 copy-done.5
  75.7 1.2 %copy-done.3 = bf16[256,2048]{1,0:T(8,128)(2,1)S(1)} copy-done((bf16[256,2048]{1,0:T(8,128)(2,1)S(1)}, bf16[256,2048]{1,0:T(8,128)(2,1)}, u32[]{:S(2)}) %copy-start.3) | copy-done | bytes 1048600
  76.9 0.8 copy-done.6
  77.7 3.9 %down_rows.2 = bf16[256,1792]{1,0:T(8,128)(2,1)S(1)} custom-call(bf16[256,2048]{1,0:T(8,128)(2,1)S(1)} %copy-done.3, bf16[256,128]{1,0:T(8,128)(2,1)S(1)} %copy-done.6, bf16[2048,3584]{1,0:T(8,128)(2,1)S(1)} %bitcast.9, bf16[128,3584]{1,0:T(8,128)(2,1)S(1)} %constant_dynamic-slice_fusion.shared_down), custom_call_target="tpu_custom_call" | custom-call | tf_op jit(solution)/shard_map/down_rows/pallas_call | solution.py:112
  81.7 0.6 collective-permute-start.6
  82.3 3.9 %down_rows.3 = bf16[256,1792]{1,0:T(8,128)(2,1)S(1)} custom-call(bf16[256,2048]{1,0:T(8,128)(2,1)S(1)} %copy-done.3, bf16[256,128]{1,0:T(8,128)(2,1)S(1)} %copy-done.6, bf16[2048,3584]{1,0:T(8,128)(2,1)S(1)} %bitcast.12, bf16[128,3584]{1,0:T(8,128)(2,1)S(1)} %constant_dynamic-slice_fusion.shared_down), custom_call_target="tpu_custom_call" | custom-call | tf_op jit(solution)/shard_map/down_rows/pallas_call | solution.py:112
  86.3 0.1 collective-permute-start.11
  86.4 0.1 convert_add_fusion.1
  86.5 1.6 %collective-permute-start.7 = (bf16[64,1792]{1,0:T(8,128)(2,1)S(1)}, bf16[64,1792]{1,0:T(8,128)(2,1)S(1)}, u32[]{:S(2)}, u32[]{:S(2)}) collective-permute-start(bf16[64,1792]{1,0:T(8,128)(2,1)S(1)} %slice.127), channel_id=1, source_target_pairs={{0,8},{4,12},{8,0},{12,4},{1,9},{5,13},{9,1},{13,5},{2,10},{6,14},... | collective-permute-start | bytes 688136 | tf_op jit(solution)/shard_map/ppermute | solution.py:129
  88.1 0.1 collective-permute-done.11
  88.2 0.1 convert_add_fusion
  88.3 1.6 %collective-permute-start.12 = (bf16[64,1792]{1,0:T(8,128)(2,1)S(1)}, bf16[64,1792]{1,0:T(8,128)(2,1)S(1)}, u32[]{:S(2)}, u32[]{:S(2)}) collective-permute-start(bf16[64,1792]{1,0:T(8,128)(2,1)S(1)} %slice.126), channel_id=1, source_target_pairs={{0,8},{4,12},{8,0},{12,4},{1,9},{5,13},{9,1},{13,5},{2,10},{6,14},... | collective-permute-start | bytes 688136 | tf_op jit(solution)/shard_map/ppermute | solution.py:129
  89.9 5.1 %collective-permute-done.7 = bf16[64,1792]{1,0:T(8,128)(2,1)S(1)} collective-permute-done((bf16[64,1792]{1,0:T(8,128)(2,1)S(1)}, bf16[64,1792]{1,0:T(8,128)(2,1)S(1)}, u32[]{:S(2)}, u32[]{:S(2)}) %collective-permute-start.7) | collective-permute-done | bytes 229408 | tf_op jit(solution)/shard_map/ppermute | solution.py:129
  95.1 2.6 %collective-permute-start.10 = (bf16[16,1792]{1,0:T(8,128)(2,1)S(1)}, bf16[16,1792]{1,0:T(8,128)(2,1)S(1)}, u32[]{:S(2)}, u32[]{:S(2)}) collective-permute-start(bf16[16,1792]{1,0:T(8,128)(2,1)S(1)} %get-tuple-element.15), channel_id=1, source_target_pairs={{0,3},{1,2},{2,1},{3,0},{4,7},{5,6},{6,5},{7,4},{8,11},{9,10},{10,... | collective-permute-start | bytes 172040 | tf_op jit(solution)/shard_map/ppermute | solution.py:129
  97.7 2.2 %collective-permute-start.8 = (bf16[16,1792]{1,0:T(8,128)(2,1)S(1)}, bf16[16,1792]{1,0:T(8,128)(2,1)S(1)}, u32[]{:S(2)}, u32[]{:S(2)}) collective-permute-start(bf16[16,1792]{1,0:T(8,128)(2,1)S(1)} %get-tuple-element.14), channel_id=1, source_target_pairs={{0,1},{1,0},{2,3},{3,2},{4,5},{5,4},{6,7},{7,6},{8,9},{9,8},{10,11... | collective-permute-start | bytes 172040 | tf_op jit(solution)/shard_map/ppermute | solution.py:129
  100.0 2.4 %collective-permute-start.13 = (bf16[16,1792]{1,0:T(8,128)(2,1)S(1)}, bf16[16,1792]{1,0:T(8,128)(2,1)S(1)}, u32[]{:S(2)}, u32[]{:S(2)}) collective-permute-start(bf16[16,1792]{1,0:T(8,128)(2,1)S(1)} %get-tuple-element.17), channel_id=1, source_target_pairs={{0,1},{1,0},{2,3},{3,2},{4,5},{5,4},{6,7},{7,6},{8,9},{9,8},{10,11... | collective-permute-start | bytes 172040 | tf_op jit(solution)/shard_map/ppermute | solution.py:129
  102.4 1.5 %collective-permute-start.14 = (bf16[16,1792]{1,0:T(8,128)(2,1)S(1)}, bf16[16,1792]{1,0:T(8,128)(2,1)S(1)}, u32[]{:S(2)}, u32[]{:S(2)}) collective-permute-start(bf16[16,1792]{1,0:T(8,128)(2,1)S(1)} %get-tuple-element.19), channel_id=1, source_target_pairs={{0,2},{1,3},{2,0},{3,1},{4,6},{5,7},{6,4},{7,5},{8,10},{9,11},{10,... | collective-permute-start | bytes 172040 | tf_op jit(solution)/shard_map/ppermute | solution.py:129
  103.9 1.4 %collective-permute-start.15 = (bf16[16,1792]{1,0:T(8,128)(2,1)S(1)}, bf16[16,1792]{1,0:T(8,128)(2,1)S(1)}, u32[]{:S(2)}, u32[]{:S(2)}) collective-permute-start(bf16[16,1792]{1,0:T(8,128)(2,1)S(1)} %get-tuple-element.18), channel_id=1, source_target_pairs={{0,3},{1,2},{2,1},{3,0},{4,7},{5,6},{6,5},{7,4},{8,11},{9,10},{10,... | collective-permute-start | bytes 172040 | tf_op jit(solution)/shard_map/ppermute | solution.py:129
  105.4 3.9 %collective-permute-done.14 = bf16[16,1792]{1,0:T(8,128)(2,1)S(1)} collective-permute-done((bf16[16,1792]{1,0:T(8,128)(2,1)S(1)}, bf16[16,1792]{1,0:T(8,128)(2,1)S(1)}, u32[]{:S(2)}, u32[]{:S(2)}) %collective-permute-start.14) | collective-permute-done | bytes 57376 | tf_op jit(solution)/shard_map/ppermute | solution.py:129
  109.2 0.8 collective-permute-done.15
  110.0 0.7 fusion
  110.7 0.2 multiply_reduce_fusion
  110.9 0.1 div.24
  111.0 0.2 subtract_reduce_fusion
  111.2 0.5 convert_multiply_fusion
  (60 shorter events, 0.6 us)
Async XLA Ops:
  0.6 0.7 copy-start
  3.4 7.6 %collective-permute-start = (bf16[16,3712]{1,0:T(8,128)(2,1)S(1)}, bf16[16,3712]{1,0:T(8,128)(2,1)S(1)}, u32[]{:S(2)}, u32[]{:S(2)}) collective-permute-start(bf16[16,3712]{1,0:T(8,128)(2,1)S(1)} %pad_maximum_fusion.2), channel_id=1, source_target_pairs={{0,1},{1,0},{2,3},{3,2},{4,5},{5,4},{6,7},{7,6},{8,9},{9,8},{10,11... | collective-permute-start | bytes 356360 | tf_op jit(solution)/shard_map/ppermute | solution.py:129
  6.5 12.0 %collective-permute-start.1 = (bf16[16,3712]{1,0:T(8,128)(2,1)S(1)}, bf16[16,3712]{1,0:T(8,128)(2,1)S(1)}, u32[]{:S(2)}, u32[]{:S(2)}) collective-permute-start(bf16[16,3712]{1,0:T(8,128)(2,1)S(1)} %pad_maximum_fusion.2), channel_id=1, source_target_pairs={{0,2},{1,3},{2,0},{3,1},{4,6},{5,7},{6,4},{7,5},{8,10},{9,11},{10,... | collective-permute-start | bytes 356360 | tf_op jit(solution)/shard_map/ppermute | solution.py:129
  9.1 9.4 %collective-permute-start.2 = (bf16[16,3712]{1,0:T(8,128)(2,1)S(1)}, bf16[16,3712]{1,0:T(8,128)(2,1)S(1)}, u32[]{:S(2)}, u32[]{:S(2)}) collective-permute-start(bf16[16,3712]{1,0:T(8,128)(2,1)S(1)} %pad_maximum_fusion.2), channel_id=1, source_target_pairs={{0,3},{1,2},{2,1},{3,0},{4,7},{5,6},{6,5},{7,4},{8,11},{9,10},{10,... | collective-permute-start | bytes 356360 | tf_op jit(solution)/shard_map/ppermute | solution.py:129
  19.4 10.5 %collective-permute-start.3 = (bf16[64,3712]{1,0:T(8,128)(2,1)S(1)}, bf16[64,3712]{1,0:T(8,128)(2,1)}, u32[]{:S(2)}, u32[]{:S(2)}) collective-permute-start(bf16[64,3712]{1,0:T(8,128)(2,1)S(1)} %pad_maximum_fusion.refs_0_), channel_id=1, source_target_pairs={{0,8},{4,12},{8,0},{12,4},{1,9},{5,13},{9,1},{13,5},{2,10},{6,14},... | collective-permute-start | bytes 1425416 | tf_op jit(solution)/shard_map/ppermute | solution.py:129
  25.0 26.9 %collective-permute-start.4 = (bf16[64,3712]{1,0:T(8,128)(2,1)S(1)}, bf16[64,3712]{1,0:T(8,128)(2,1)}, u32[]{:S(2)}, u32[]{:S(2)}) collective-permute-start(bf16[64,3712]{1,0:T(8,128)(2,1)S(1)} %pad_maximum_fusion.refs_0_), channel_id=1, source_target_pairs={{0,4},{4,0},{8,12},{12,8},{1,5},{5,1},{9,13},{13,9},{2,6},{6,2},{1... | collective-permute-start | bytes 1425416 | tf_op jit(solution)/shard_map/ppermute | solution.py:129
  29.9 22.0 %collective-permute-start.5 = (bf16[64,3712]{1,0:T(8,128)(2,1)}, bf16[64,3712]{1,0:T(8,128)(2,1)}, u32[]{:S(2)}, u32[]{:S(2)}) collective-permute-start(bf16[64,3712]{1,0:T(8,128)(2,1)} %collective-permute-done.3.refs_1_), channel_id=1, source_target_pairs={{0,4},{4,0},{8,12},{12,8},{1,5},{5,1},{9,13},{13,9},{2,6},{6,2},{1... | collective-permute-start | bytes 1425416 | tf_op jit(solution)/shard_map/ppermute | solution.py:129
  51.9 23.7 %slice-start = ((s8[14680064]{0:T(1024)(128)(4,1)}), s8[4194304]{0:T(1024)(128)(4,1)S(1)}, s32[]{:S(2)}) async-start(s8[14680064]{0:T(1024)(128)(4,1)} %bitcast.7), calls=%async_computation | async-start | bytes 8388608
  51.9 1.1 copy-start.4
  53.0 22.6 %slice-start.1 = ((s8[14680064]{0:T(1024)(128)(4,1)}), s8[4194304]{0:T(1024)(128)(4,1)S(1)}, s32[]{:S(2)}) async-start(s8[14680064]{0:T(1024)(128)(4,1)} %bitcast.7), calls=%async_computation.1 | async-start | bytes 8388608
  53.0 22.6 %slice-start.2 = ((s8[14680064]{0:T(1024)(128)(4,1)}), s8[4194304]{0:T(1024)(128)(4,1)S(1)}, s32[]{:S(2)}) async-start(s8[14680064]{0:T(1024)(128)(4,1)} %bitcast.7), calls=%async_computation.2 | async-start | bytes 8388608
  53.0 22.7 %slice-start.3 = ((s8[14680064]{0:T(1024)(128)(4,1)}), s8[2097152]{0:T(1024)(128)(4,1)S(1)}, s32[]{:S(2)}) async-start(s8[14680064]{0:T(1024)(128)(4,1)} %bitcast.7), calls=%async_computation.3 | async-start | bytes 4194304
  53.0 29.2 %slice-start.4 = ((s8[14680064]{0:T(1024)(128)(4,1)}), s8[2097152]{0:T(1024)(128)(4,1)S(1)}, s32[]{:S(2)}) async-start(s8[14680064]{0:T(1024)(128)(4,1)} %bitcast.10), calls=%async_computation.4 | async-start | bytes 4194304
  53.0 29.2 %slice-start.5 = ((s8[14680064]{0:T(1024)(128)(4,1)}), s8[4194304]{0:T(1024)(128)(4,1)S(1)}, s32[]{:S(2)}) async-start(s8[14680064]{0:T(1024)(128)(4,1)} %bitcast.10), calls=%async_computation.5 | async-start | bytes 8388608
  53.0 29.2 %slice-start.6 = ((s8[14680064]{0:T(1024)(128)(4,1)}), s8[4194304]{0:T(1024)(128)(4,1)S(1)}, s32[]{:S(2)}) async-start(s8[14680064]{0:T(1024)(128)(4,1)} %bitcast.10), calls=%async_computation.6 | async-start | bytes 8388608
  74.0 1.0 copy-start.2
  75.0 0.6 copy-start.5
  75.7 1.2 %copy-start.3 = (bf16[256,2048]{1,0:T(8,128)(2,1)S(1)}, bf16[256,2048]{1,0:T(8,128)(2,1)}, u32[]{:S(2)}) copy-start(bf16[256,2048]{1,0:T(8,128)(2,1)} %copy-done.2) | copy-start | bytes 3145732
  76.9 0.8 copy-start.6
  77.7 4.5 %slice-start.7 = ((s8[14680064]{0:T(1024)(128)(4,1)}), s8[4194304]{0:T(1024)(128)(4,1)S(1)}, s32[]{:S(2)}) async-start(s8[14680064]{0:T(1024)(128)(4,1)} %bitcast.10), calls=%async_computation.7 | async-start | bytes 8388608
  81.7 4.7 %collective-permute-start.6 = (bf16[128,1792]{1,0:T(8,128)(2,1)S(1)}, bf16[128,1792]{1,0:T(8,128)(2,1)S(1)}, u32[]{:S(2)}, u32[]{:S(2)}) collective-permute-start(bf16[128,1792]{1,0:T(8,128)(2,1)S(1)} %slice.93), channel_id=1, source_target_pairs={{0,4},{4,0},{8,12},{12,8},{1,5},{5,1},{9,13},{13,9},{2,6},{6,2},{1... | collective-permute-start | bytes 1376264 | tf_op jit(solution)/shard_map/ppermute | solution.py:129
  82.3 29.4 %copy-start.1 = (s32[64,8]{0,1:T(8,128)S(1)}, s32[64,8]{0,1:T(8,128)}, u32[]{:S(2)}) copy-start(s32[64,8]{0,1:T(8,128)} %param.10) | copy-start | bytes 6148
  86.2 24.5 %copy-start.7 = (f32[3584]{0:T(1024)S(1)}, f32[3584]{0:T(1024)}, u32[]{:S(2)}) copy-start(f32[3584]{0:T(1024)} %param.17) | copy-start | bytes 43012
  86.2 24.9 %copy-start.8 = (s32[8]{0:T(128)S(1)}, s32[8]{0:T(128)}, u32[]{:S(2)}) copy-start(s32[8]{0:T(128)} %param.12) | copy-start | bytes 100
  86.3 1.9 %collective-permute-start.11 = (bf16[128,1792]{1,0:T(8,128)(2,1)S(1)}, bf16[128,1792]{1,0:T(8,128)(2,1)S(1)}, u32[]{:S(2)}, u32[]{:S(2)}) collective-permute-start(bf16[128,1792]{1,0:T(8,128)(2,1)S(1)} %slice.101), channel_id=1, source_target_pairs={{0,4},{4,0},{8,12},{12,8},{1,5},{5,1},{9,13},{13,9},{2,6},{6,2},{1... | collective-permute-start | bytes 1376264 | tf_op jit(solution)/shard_map/ppermute | solution.py:129
  86.5 8.5 %collective-permute-start.7 = (bf16[64,1792]{1,0:T(8,128)(2,1)S(1)}, bf16[64,1792]{1,0:T(8,128)(2,1)S(1)}, u32[]{:S(2)}, u32[]{:S(2)}) collective-permute-start(bf16[64,1792]{1,0:T(8,128)(2,1)S(1)} %slice.127), channel_id=1, source_target_pairs={{0,8},{4,12},{8,0},{12,4},{1,9},{5,13},{9,1},{13,5},{2,10},{6,14},... | collective-permute-start | bytes 688136 | tf_op jit(solution)/shard_map/ppermute | solution.py:129
  88.3 11.6 %collective-permute-start.12 = (bf16[64,1792]{1,0:T(8,128)(2,1)S(1)}, bf16[64,1792]{1,0:T(8,128)(2,1)S(1)}, u32[]{:S(2)}, u32[]{:S(2)}) collective-permute-start(bf16[64,1792]{1,0:T(8,128)(2,1)S(1)} %slice.126), channel_id=1, source_target_pairs={{0,8},{4,12},{8,0},{12,4},{1,9},{5,13},{9,1},{13,5},{2,10},{6,14},... | collective-permute-start | bytes 688136 | tf_op jit(solution)/shard_map/ppermute | solution.py:129
  95.1 8.8 %collective-permute-start.10 = (bf16[16,1792]{1,0:T(8,128)(2,1)S(1)}, bf16[16,1792]{1,0:T(8,128)(2,1)S(1)}, u32[]{:S(2)}, u32[]{:S(2)}) collective-permute-start(bf16[16,1792]{1,0:T(8,128)(2,1)S(1)} %get-tuple-element.15), channel_id=1, source_target_pairs={{0,3},{1,2},{2,1},{3,0},{4,7},{5,6},{6,5},{7,4},{8,11},{9,10},{10,... | collective-permute-start | bytes 172040 | tf_op jit(solution)/shard_map/ppermute | solution.py:129
  97.7 7.6 %collective-permute-start.8 = (bf16[16,1792]{1,0:T(8,128)(2,1)S(1)}, bf16[16,1792]{1,0:T(8,128)(2,1)S(1)}, u32[]{:S(2)}, u32[]{:S(2)}) collective-permute-start(bf16[16,1792]{1,0:T(8,128)(2,1)S(1)} %get-tuple-element.14), channel_id=1, source_target_pairs={{0,1},{1,0},{2,3},{3,2},{4,5},{5,4},{6,7},{7,6},{8,9},{9,8},{10,11... | collective-permute-start | bytes 172040 | tf_op jit(solution)/shard_map/ppermute | solution.py:129
  99.9 5.4 %collective-permute-start.9 = (bf16[16,1792]{1,0:T(8,128)(2,1)S(1)}, bf16[16,1792]{1,0:T(8,128)(2,1)S(1)}, u32[]{:S(2)}, u32[]{:S(2)}) collective-permute-start(bf16[16,1792]{1,0:T(8,128)(2,1)S(1)} %get-tuple-element.16), channel_id=1, source_target_pairs={{0,2},{1,3},{2,0},{3,1},{4,6},{5,7},{6,4},{7,5},{8,10},{9,11},{10,... | collective-permute-start | bytes 172040 | tf_op jit(solution)/shard_map/ppermute | solution.py:129
  100.0 5.3 %collective-permute-start.13 = (bf16[16,1792]{1,0:T(8,128)(2,1)S(1)}, bf16[16,1792]{1,0:T(8,128)(2,1)S(1)}, u32[]{:S(2)}, u32[]{:S(2)}) collective-permute-start(bf16[16,1792]{1,0:T(8,128)(2,1)S(1)} %get-tuple-element.17), channel_id=1, source_target_pairs={{0,1},{1,0},{2,3},{3,2},{4,5},{5,4},{6,7},{7,6},{8,9},{9,8},{10,11... | collective-permute-start | bytes 172040 | tf_op jit(solution)/shard_map/ppermute | solution.py:129
  102.4 6.8 %collective-permute-start.14 = (bf16[16,1792]{1,0:T(8,128)(2,1)S(1)}, bf16[16,1792]{1,0:T(8,128)(2,1)S(1)}, u32[]{:S(2)}, u32[]{:S(2)}) collective-permute-start(bf16[16,1792]{1,0:T(8,128)(2,1)S(1)} %get-tuple-element.19), channel_id=1, source_target_pairs={{0,2},{1,3},{2,0},{3,1},{4,6},{5,7},{6,4},{7,5},{8,10},{9,11},{10,... | collective-permute-start | bytes 172040 | tf_op jit(solution)/shard_map/ppermute | solution.py:129
  103.9 6.1 %collective-permute-start.15 = (bf16[16,1792]{1,0:T(8,128)(2,1)S(1)}, bf16[16,1792]{1,0:T(8,128)(2,1)S(1)}, u32[]{:S(2)}, u32[]{:S(2)}) collective-permute-start(bf16[16,1792]{1,0:T(8,128)(2,1)S(1)} %get-tuple-element.18), channel_id=1, source_target_pairs={{0,3},{1,2},{2,1},{3,0},{4,7},{5,6},{6,5},{7,4},{8,11},{9,10},{10,... | collective-permute-start | bytes 172040 | tf_op jit(solution)/shard_map/ppermute | solution.py:129

commit v2 on v1

v2 whole, which is shorter than its diff:
```python
import functools
import math

import jax
import jax.numpy as jnp
from jax import lax
from jax.experimental import pallas as pl
from jax.experimental.pallas import tpu as pltpu
from jax.sharding import PartitionSpec as P

ROT = 128
CORES = 2
SMALL_VMEM = 12 * 1024 * 1024
VMEM_BYTES = 16 * 1024 * 1024
SCATTER_CHUNKS = 2


def sign_matrix(copies):
    size = copies * ROT
    row_index = lax.broadcasted_iota(jnp.int32, (size, size), 0)
    col_index = lax.broadcasted_iota(jnp.int32, (size, size), 1)
    common = jnp.bitwise_and(row_index % ROT, col_index % ROT)
    parity = jnp.zeros((size, size), jnp.int32)
    for shift_bits in range(ROT.bit_length() - 1):
        parity = parity + jnp.bitwise_and(jnp.right_shift(common, shift_bits), 1)
    signs = 1 - 2 * jnp.bitwise_and(parity, 1)
    return jnp.where(row_index // ROT == col_index // ROT, signs, 0).astype(jnp.bfloat16)


def in_vmem(value):
    return pltpu.with_memory_space_constraint(value, pltpu.VMEM)


def vmem(shape, dtype):
    return pltpu.VMEM(shape, dtype)


def apart_kernel(rows, chunk, *refs):
    source, out = refs[0], refs[-1]
    step = pl.program_id(0)
    count = 2 * out.shape[2] // 128
    for at in range(0, rows, chunk):
        pairs = source[0, at * count : (at + chunk) * count, :].reshape(chunk, count, 128)
        pairs = jnp.swapaxes(pairs, 0, 1)
        here = pl.ds(pl.multiple_of(step * rows + at, chunk), chunk)
        for q in range(count):
            out[q % 2, here, (q // 2) * 128 : (q // 2 + 1) * 128] = pairs[q]


def apart(packed, expert, feature_len, inner, after):
    count = 2 * inner // 128
    rows = feature_len // 4 if feature_len % 256 == 0 else feature_len
    chunk = 64 if rows % 64 == 0 else rows
    return pl.pallas_call(
        functools.partial(apart_kernel, rows, chunk),
        grid=(feature_len // rows,),
        in_specs=[pl.BlockSpec((1, rows * count, 128), lambda s: (expert, s, 0))]
        + [pl.BlockSpec(memory_space=pl.ANY)] * len(after),
        out_specs=pl.BlockSpec(memory_space=pltpu.VMEM),
        out_shape=vmem((2, feature_len, inner), packed.dtype),
        compiler_params=pltpu.CompilerParams(vmem_limit_bytes=SMALL_VMEM),
        cost_estimate=pl.CostEstimate(flops=0, bytes_accessed=1024, transcendentals=0),
        name="apart",
    )(packed, *after)


def join_kernel(n_pieces, *refs):
    lanes, out = refs[n_pieces], refs[-1]
    feature_len = refs[0].shape[1]
    base = 0
    for piece in refs[:n_pieces]:
        out[base : base + piece.shape[0], :feature_len] = piece[...]
        base += piece.shape[0]
    out[:, feature_len:] = lanes[...]


def join(pieces, lanes, after):
    whole = pl.BlockSpec(memory_space=pltpu.VMEM)
    return pl.pallas_call(
        functools.partial(join_kernel, len(pieces)),
        in_specs=[whole] * (len(pieces) + 1) + [pl.BlockSpec(memory_space=pl.ANY)] * len(after),
        out_specs=whole,
        out_shape=vmem((lanes.shape[0], pieces[0].shape[1] + lanes.shape[1]), lanes.dtype),
        compiler_params=pltpu.CompilerParams(vmem_limit_bytes=SMALL_VMEM),
        cost_estimate=pl.CostEstimate(flops=0, bytes_accessed=1024, transcendentals=0),
        name="join",
    )(*pieces, lanes, *after)


def rotate(source, signs, target, base):
    rows = source.shape[0]
    feature_len = target.shape[1]
    width = signs.shape[0]

    def block(index, carry):
        at = pl.ds(pl.multiple_of(index * width, width), width)
        rotated = jnp.dot(source[:, at], signs[...], preferred_element_type=jnp.float32) * (
            1.0 / math.sqrt(ROT)
        )
        parts = []
        for piece_at in range(0, width, ROT):
            part = rotated[:, piece_at : piece_at + ROT]
            scale = (jnp.max(jnp.abs(part), axis=1, keepdims=True) + 1e-06).astype(jnp.bfloat16)
            scale = scale.astype(jnp.float32)
            quantized = (part / scale).astype(jnp.bfloat16)
            parts.append((quantized.astype(jnp.float32) * scale).astype(jnp.bfloat16))
        target[base : base + rows, at] = jnp.concatenate(parts, axis=1)
        return carry

    lax.fori_loop(0, feature_len // width, block, 0)


def first_kernel(n_pieces, *refs):
    signs, out = refs[n_pieces:]
    base = 0
    for piece in refs[:n_pieces]:
        rotate(piece, signs, out, base)
        base += piece.shape[0]


def first_rows(pieces, signs, feature_len):
    whole = pl.BlockSpec(memory_space=pltpu.VMEM)
    rows = sum(piece.shape[0] for piece in pieces)
    return pl.pallas_call(
        functools.partial(first_kernel, len(pieces)),
        in_specs=[whole] * (len(pieces) + 1),
        out_specs=whole,
        out_shape=vmem((rows, feature_len), jnp.bfloat16),
        compiler_params=pltpu.CompilerParams(vmem_limit_bytes=SMALL_VMEM),
        cost_estimate=pl.CostEstimate(flops=0, bytes_accessed=1024, transcendentals=0),
        name="first_rows",
    )(*pieces, signs)


def rest_kernel(n_first, n_chips, *refs):
    n_pieces = CORES * n_chips
    pieces = refs[:n_pieces]
    signs, first, shared, deq, shared_hidden, combine, rows_s = refs[n_pieces:]
    count = pieces[0].shape[0]
    feature_len = deq.shape[1]
    for core in range(CORES):
        for chip in range(n_chips):
            base = (core * n_chips + chip) * count
            if chip == 0:
                piece = pieces[core]
                deq[base : base + count, :] = first[core * count : (core + 1) * count, :]
            else:
                piece = pieces[CORES + core * (n_chips - 1) + chip - 1]
                rotate(piece, signs, deq, base)
            rows_s[base : base + count, :] = piece[:, :feature_len]
            combine[base : base + count, :] = piece[:, feature_len:].astype(jnp.float32)
    part = shared.shape[1] // 2
    both = jnp.dot(rows_s[...], shared[...], preferred_element_type=jnp.float32)
    gate, up = both[:, :part], both[:, part:]
    shared_hidden[...] = (gate / (1.0 + jnp.exp(-gate)) * up).astype(jnp.bfloat16)


def rest_rows(pieces, signs, first, shared, n_chips):
    whole = pl.BlockSpec(memory_space=pltpu.VMEM)
    rows = sum(piece.shape[0] for piece in pieces)
    feature_len = first.shape[1]
    return pl.pallas_call(
        functools.partial(rest_kernel, len(pieces), n_chips),
        in_specs=[whole] * (len(pieces) + 3),
        out_specs=[whole] * 3,
        out_shape=[
            vmem((rows, feature_len), jnp.bfloat16),
            vmem((rows, shared.shape[1] // 2), jnp.bfloat16),
            vmem((rows, pieces[0].shape[1] - feature_len), jnp.float32),
        ],
        scratch_shapes=[pltpu.VMEM((rows, feature_len), jnp.bfloat16)],
        compiler_params=pltpu.CompilerParams(vmem_limit_bytes=SMALL_VMEM),
        name="rest_rows",
    )(*pieces, signs, first, shared)


def hidden_kernel(n_local, *refs):
    deq, combine, select = refs[:3]
    weights, out = refs[3 : 3 + n_local], refs[3 + n_local]
    inner = out.shape[1] // n_local
    for local in range(n_local):
        gate = jnp.dot(deq[...], weights[local][0], preferred_element_type=jnp.float32)
        up = jnp.dot(deq[...], weights[local][1], preferred_element_type=jnp.float32)
        weight = jnp.sum(combine[...] * select[local : local + 1, :], axis=1, keepdims=True)
        out[:, local * inner : (local + 1) * inner] = (
            gate / (1.0 + jnp.exp(-gate)) * up * weight
        ).astype(jnp.bfloat16)


def hidden_rows(deq, combine, select, weights):
    whole = pl.BlockSpec(memory_space=pltpu.VMEM)
    rows = deq.shape[0]
    return pl.pallas_call(
        functools.partial(hidden_kernel, len(weights)),
        in_specs=[whole] * (3 + len(weights)),
        out_specs=whole,
        out_shape=vmem((rows, len(weights) * weights[0].shape[2]), jnp.bfloat16),
        compiler_params=pltpu.CompilerParams(vmem_limit_bytes=SMALL_VMEM),
        name="hidden_rows",
    )(deq, combine, select, *weights)


def down_kernel(hidden, shared_hidden, down, shared_down, out):
    out[...] = (
        jnp.dot(hidden[...], down[...], preferred_element_type=jnp.float32)
        + jnp.dot(shared_hidden[...], shared_down[...], preferred_element_type=jnp.float32)
    ).astype(out.dtype)


def down_rows(hidden, shared_hidden, down, shared_down, start, stop):
    rows = hidden.shape[0]
    inner = down.shape[0]
    tile = math.gcd(512, math.gcd(start, stop - start))
    first = start // tile
    whole = pl.BlockSpec(memory_space=pltpu.VMEM)
    return pl.pallas_call(
        down_kernel,
        grid=((stop - start) // tile,),
        in_specs=[
            whole,
            whole,
            pl.BlockSpec((inner, tile), lambda s: (0, first + s)),
            pl.BlockSpec((shared_down.shape[0], tile), lambda s: (0, first + s)),
        ],
        out_specs=pl.BlockSpec((rows, tile), lambda s: (0, s)),
        out_shape=jax.ShapeDtypeStruct((rows, stop - start), jnp.bfloat16),
        compiler_params=pltpu.CompilerParams(vmem_limit_bytes=VMEM_BYTES),
        name="down_rows",
    )(hidden, shared_hidden, down, shared_down)


def exchange(value, axis, flip):
    return lax.ppermute(value, axis, [(i, i ^ flip) for i in range(lax.axis_size(axis))])


def per_device(
    tokens,
    expert_ids,
    route_weights,
    pair_flags,
    shared_gate_up,
    shared_down,
    expert_gate_up,
    expert_down,
    readout,
):
    own_rows, feature_len = tokens.shape
    n_local, _, _, inner = expert_gate_up.shape
    expert_count = lax.axis_size("expert")
    narrow_count = lax.axis_size("narrow")
    chips = expert_count // CORES
    experts = n_local * expert_count
    expert_at = lax.axis_index("expert")
    narrow_at = lax.axis_index("narrow")

    named = lax.broadcasted_iota(jnp.int32, (1, 1, experts), 2)
    combine = jnp.sum(
        jnp.where(expert_ids[:, :, None] == named, route_weights[:, :, None], 0.0), axis=1
    )
    high = combine.astype(jnp.bfloat16)
    low = (combine - high.astype(jnp.float32)).astype(jnp.bfloat16)
    columns = -(-2 * experts // 128) * 128
    lanes = jnp.pad(jnp.concatenate([high, low], axis=1), ((0, 0), (0, columns - 2 * experts)))
    lanes = lanes.reshape(narrow_count, own_rows, columns)
    order = narrow_at ^ jnp.arange(narrow_count)
    lanes = lanes[order].reshape(narrow_count * own_rows, columns)
    local_ids = expert_at * n_local + lax.broadcasted_iota(jnp.int32, (n_local, columns), 0)
    column = lax.broadcasted_iota(jnp.int32, (n_local, columns), 1)
    select = ((column == local_ids) | (column == local_ids + experts)).astype(jnp.float32)

    shared_len = shared_down.shape[0]
    part_len = shared_len // expert_count
    if part_len % 128 == 0:
        shared_in = lax.dynamic_slice_in_dim(shared_gate_up, expert_at * part_len, part_len, 2)
        shared_out = lax.dynamic_slice_in_dim(shared_down, expert_at * part_len, part_len, 0)
    else:
        mine = lax.broadcasted_iota(jnp.int32, (shared_len, 1), 0) // part_len == expert_at
        shared_in = shared_gate_up
        shared_out = jnp.where(mine, shared_down, jnp.zeros_like(shared_down))
    shared_in = shared_in.reshape(feature_len, -1)
    signs = sign_matrix(2 if feature_len % (2 * ROT) == 0 else 1)

    packed = expert_gate_up.reshape(n_local, feature_len, 2, inner // 128, 128)
    packed = packed.transpose(0, 1, 3, 2, 4).reshape(n_local, -1, 128)
    packed = pltpu.with_memory_space_constraint(packed, pltpu.HBM)

    def prepared(expert, after):
        return apart(packed, expert, feature_len, inner, after)

    early = (n_local + 1) // 2
    from_z = [exchange(tokens, "narrow", flip) for flip in range(1, narrow_count)]
    weights = []
    for expert in range(early):
        weights.append(prepared(expert, weights[-1:]))
    along_z = join([tokens] + from_z, lanes, weights[-1:])
    from_x = [exchange(along_z, "expert", flip * CORES) for flip in range(1, chips)]
    near = exchange(along_z, "expert", 1)
    first = first_rows([along_z, near], signs, feature_len)
    after = [along_z]
    for expert in range(early, n_local):
        weights.append(prepared(expert, after))
        after = weights[-1:]
    from_both = [exchange(part, "expert", 1) for part in from_x]

    deq, shared_hidden, combine = rest_rows(
        [along_z, near] + from_x + from_both, signs, first, shared_in, chips
    )
    hidden = hidden_rows(deq, combine, select, weights)
    down = expert_down.reshape(n_local * inner, feature_len)

    half = own_rows * narrow_count * chips
    totals = []
    width = feature_len // SCATTER_CHUNKS
    for chunk in range(SCATTER_CHUNKS):
        part = down_rows(
            hidden, shared_hidden, down, shared_out, chunk * width, (chunk + 1) * width
        )
        near = exchange(part[half:], "expert", 1)
        by_core = part[:half].astype(jnp.float32) + near.astype(jnp.float32)
        by_core = by_core.reshape(chips, narrow_count * own_rows, width)
        by_chip = by_core[0]
        for flip in range(1, chips):
            by_chip = by_chip + exchange(
                by_core[flip].astype(jnp.bfloat16), "expert", flip * CORES
            ).astype(jnp.float32)
        by_chip = by_chip.reshape(narrow_count, own_rows, width)
        total = by_chip[0]
        for flip in range(1, narrow_count):
            total = total + exchange(
                by_chip[flip].astype(jnp.bfloat16), "narrow", flip
            ).astype(jnp.float32)
        totals.append(total)
    total_sum = jnp.concatenate(totals, axis=1)
    mixed = total_sum.astype(jnp.bfloat16)
    row_score = jnp.sum(total_sum * readout[None, :], axis=1) / jnp.sqrt(
        jnp.mean(total_sum * total_sum, axis=1) + 1e-06
    )
    paired = row_score.reshape(-1, 2)
    pmi_scores = (paired[:, 0] - paired[:, 1]) * (1 - 2 * pair_flags).astype(jnp.float32)
    return (mixed, pmi_scores)


def solution(mesh):
    in_specs = (
        P(("groups", "expert", "narrow"), None),
        P(("groups", "expert"), None),
        P(("groups", "expert"), None),
        P(("groups", "expert", "narrow")),
        P(None, None, "narrow"),
        P("narrow", None),
        P("expert", None, None, "narrow"),
        P("expert", "narrow", None),
        P(),
    )
    out_specs = (P(("groups", "expert", "narrow"), None), P(("groups", "expert", "narrow")))
    return jax.shard_map(
        per_device, mesh=mesh, in_specs=in_specs, out_specs=out_specs, check_vma=False
    )
```

time: 112 us -> 114 us (1.018)
  Pallas kernels: 28.8 us -> 51.6 us
  local copies, waits for them, and re-layouts: 31.6 us -> 19.6 us
  waiting for transfers between devices: 24.1 us -> 16.5 us
  other arithmetic: 4.96 us -> 3.14 us
    pallas_call x1 -> x8, Pallas kernels: 21 us -> 43.8 us  [the longest x4 20.8 us: apart(): pl.pallas_call(functools.partial(apart_kernel, rows, chunk), grid=(featur...]
    unnamed x36 -> x23, local copies, waits for them, and re-layouts: 26.1 us -> 14.4 us
    ppermute x16, waiting for transfers between devices: 24.1 us -> 16.5 us  [exchange(): lax.ppermute(value, axis, [(i, i ^ flip) for i in range(lax.axis_size(axi...]
    concatenate x2 -> x0, other arithmetic: 1.84 us -> none  [the longest x1 0.93 us: per_device(): jnp.concatenate([sent] + [exchange(sent, 'narrow', flip) for flip in rang...]
  transfers between devices with their start and end apart: 16 -> 16, of which waited for: 7 -> 5; matrix products, arithmetic and copies ran while one was open for 24% -> 6% of each run, Pallas kernels for 4% -> 28%
where the time goes in v2:
time: 114 us; the launch traced here: 113 us
  Pallas kernels  51.6 us (45%)
  starting transfers between devices  21.5 us (19%)
  local copies, waits for them, and re-layouts  19.6 us (17%)
  waiting for transfers between devices  16.5 us (14%)
  other arithmetic  3.14 us (3%)
    ppermute x16, starting transfers between devices, exchange(): lax.ppermute(value, axis, [(i, i ^ flip) for i in range(lax.axis_size(axi...  21.5 us
    pallas_call x4, Pallas kernels, apart(): pl.pallas_call(functools.partial(apart_kernel, rows, chunk), grid=(featur...  20.8 us
    ppermute x16, waiting for transfers between devices, exchange(): lax.ppermute(value, axis, [(i, i ^ flip) for i in range(lax.axis_size(axi...  16.5 us
    unnamed x23, local copies, waits for them, and re-layouts  14.4 us
    pallas_call x1, Pallas kernels, rest_rows(): pl.pallas_call(functools.partial(rest_kernel, len(pieces), n_chips), in_s...  7.94 us
    pallas_call x2, Pallas kernels, down_rows(): pl.pallas_call(down_kernel, grid=((stop - start) // tile,), in_specs=[who...  7.85 us
    pallas_call x1, Pallas kernels, hidden_rows(): pl.pallas_call(functools.partial(hidden_kernel, len(weights)), in_specs=[...  7.78 us
    pallas_call x1, Pallas kernels, first_rows(): pl.pallas_call(functools.partial(first_kernel, len(pieces)), in_specs=[wh...  7.15 us
  transfers between devices with their start and end apart: 16, of which 5 were waited for; matrix products, arithmetic and copies ran while one was open for 6% of the time, Pallas kernels for 28%

profile of v2, /device:TPU:0, one launch (start us, length us, event | category | flops | bytes accessed | tf_op | source)
XLA Modules:
  0.0 113.4 jit_solution(6402495827039147121)
XLA Ops:
  0.6 3.1 %collective-permute-start = (bf16[16,3584]{1,0:T(8,128)(2,1)}, bf16[16,3584]{1,0:T(8,128)(2,1)S(1)}, u32[]{:S(2)}, u32[]{:S(2)}) collective-permute-start(bf16[16,3584]{1,0:T(8,128)(2,1)} %refs_0_.1), channel_id=1, source_target_pairs={{0,1},{1,0},{2,3},{3,2},{4,5},{5,4},{6,7},{7,6},{8,9},{9,8},{10,11... | collective-permute-start | bytes 344072 | tf_op jit(solution)/shard_map/ppermute | solution.py:233
  3.7 2.6 %collective-permute-start.1 = (bf16[16,3584]{1,0:T(8,128)(2,1)}, bf16[16,3584]{1,0:T(8,128)(2,1)S(1)}, u32[]{:S(2)}, u32[]{:S(2)}) collective-permute-start(bf16[16,3584]{1,0:T(8,128)(2,1)} %refs_0_.1), channel_id=1, source_target_pairs={{0,2},{1,3},{2,0},{3,1},{4,6},{5,7},{6,4},{7,5},{8,10},{9,11},{10,... | collective-permute-start | bytes 344072 | tf_op jit(solution)/shard_map/ppermute | solution.py:233
  6.3 0.7 select_reduce_fusion
  7.1 0.1 copy.18
  7.2 0.1 pad_maximum_fusion.1
  7.3 4.7 %apart.4.refs_1_.refs_3_ = bf16[2,3584,512]{2,1,0:T(8,128)(2,1)S(1)} custom-call(bf16[4,28672,128]{2,1,0:T(8,128)(2,1)} %bitcast.22), custom_call_target="tpu_custom_call" | custom-call | bytes 1024 | tf_op jit(solution)/shard_map/apart/pallas_call | solution.py:54
  12.0 4.7 %apart.5.refs_5_.refs_4_ = bf16[2,3584,512]{2,1,0:T(8,128)(2,1)S(1)} custom-call(bf16[4,28672,128]{2,1,0:T(8,128)(2,1)} %bitcast.23, bf16[2,3584,512]{2,1,0:T(8,128)(2,1)S(1)} %apart.4.refs_1_.refs_3_), custom_call_target="tpu_custom_call" | custom-call | bytes 1024 | tf_op jit(solution)/shard_map/apart/pallas_call | solution.py:54
  16.7 2.9 %copy-done = bf16[2,3584,512]{2,1,0:T(8,128)(2,1)} copy-done((bf16[2,3584,512]{2,1,0:T(8,128)(2,1)}, bf16[2,3584,512]{2,1,0:T(8,128)(2,1)S(1)}, u32[]{:S(2)}) %copy-start) | copy-done | bytes 7340056
  19.6 3.0 %copy-done.2 = bf16[2,3584,512]{2,1,0:T(8,128)(2,1)} copy-done((bf16[2,3584,512]{2,1,0:T(8,128)(2,1)}, bf16[2,3584,512]{2,1,0:T(8,128)(2,1)S(1)}, u32[]{:S(2)}) %copy-start.2) | copy-done | bytes 7340056
  22.6 0.6 gather_fusion
  23.3 3.1 %copy-done.1 = bf16[2,3584,512]{2,1,0:T(8,128)(2,1)S(1)} copy-done((bf16[2,3584,512]{2,1,0:T(8,128)(2,1)S(1)}, bf16[2,3584,512]{2,1,0:T(8,128)(2,1)}, u32[]{:S(2)}) %copy-start.1) | copy-done | bytes 7340056
  26.4 1.8 %collective-permute-start.4 = (bf16[64,3712]{1,0:T(8,128)(2,1)S(1)}, bf16[64,3712]{1,0:T(8,128)(2,1)S(1)}, u32[]{:S(2)}, u32[]{:S(2)}) collective-permute-start(bf16[64,3712]{1,0:T(8,128)(2,1)S(1)} %join.1.refs_0_.refs_1_), channel_id=1, source_target_pairs={{0,8},{4,12},{8,0},{12,4},{1,9},{5,13},{9,1},{13,5},{2,10},{6,14},... | collective-permute-start | bytes 1425416 | tf_op jit(solution)/shard_map/ppermute | solution.py:233
  28.2 0.3 select_convert_fusion.refs_2_.refs_4_
  28.5 3.1 %constant_dynamic-slice_fusion.1 = bf16[3584,2,128]{2,1,0:T(2,128)(2,1)S(1)} fusion(bf16[3584,2,512]{2,1,0:T(2,128)(2,1)} %param.13, s32[]{:T(128)S(6)} %select_n.58), kind=kLoop, calls=%fused_computation.44 | loop fusion | bytes 3670020 | tf_op jit(solution)/shard_map/dynamic_slice | solution.py:274
  31.6 0.1 collective-permute-start.3
  31.6 6.9 %collective-permute-done.4.refs_2_ = bf16[64,3712]{1,0:T(8,128)(2,1)S(1)} collective-permute-done((bf16[64,3712]{1,0:T(8,128)(2,1)S(1)}, bf16[64,3712]{1,0:T(8,128)(2,1)S(1)}, u32[]{:S(2)}, u32[]{:S(2)}) %collective-permute-start.4) | collective-permute-done | bytes 475168 | tf_op jit(solution)/shard_map/ppermute | solution.py:233
  38.5 0.1 fusion.6.refs_2_
  38.6 0.2 copy.22
  38.8 1.2 %constant_dynamic-slice_fusion.shared_down = bf16[128,3584]{1,0:T(8,128)(2,1)S(1)} fusion(bf16[512,3584]{1,0:T(8,128)(2,1)} %param.14, s32[]{:T(128)S(6)} %select_n.58), kind=kLoop, calls=%fused_computation.43 | loop fusion | bytes 1835012 | tf_op jit(solution)/shard_map/dynamic_slice | solution.py:275
  40.1 6.0 %apart.6.refs_1_.refs_5_ = bf16[2,3584,512]{2,1,0:T(8,128)(2,1)S(1)} custom-call(bf16[4,28672,128]{2,1,0:T(8,128)(2,1)} %bitcast.24, bf16[64,3712]{1,0:T(8,128)(2,1)S(1)} %join.1.refs_0_.refs_1_), custom_call_target="tpu_custom_call" | custom-call | bytes 1024 | tf_op jit(solution)/shard_map/apart/pallas_call | solution.py:54
  46.1 5.5 %apart.7.refs_6_ = bf16[2,3584,512]{2,1,0:T(8,128)(2,1)S(1)} custom-call(bf16[4,28672,128]{2,1,0:T(8,128)(2,1)} %bitcast.25, bf16[2,3584,512]{2,1,0:T(8,128)(2,1)S(1)} %apart.6.refs_1_.refs_5_), custom_call_target="tpu_custom_call" | custom-call | bytes 1024 | tf_op jit(solution)/shard_map/apart/pallas_call | solution.py:54
  51.6 7.1 %first_rows.1.refs_5_ = bf16[128,3584]{1,0:T(8,128)(2,1)S(1)} custom-call(bf16[64,3712]{1,0:T(8,128)(2,1)S(1)} %join.1.refs_0_.refs_1_, bf16[64,3712]{1,0:T(8,128)(2,1)S(1)} %collective-permute-done.3.refs_1_, bf16[256,256]{1,0:T(8,128)(2,1)S(1)} %select_convert_fusion.refs_2_.refs_4_), custom_call_target="tpu_custom_call" | custom-call | bytes 1024 | tf_op jit(solution)/shard_map/first_rows/pallas_call | solution.py:124
  58.8 7.9 %rest_rows.1 = (bf16[256,3584]{1,0:T(8,128)(2,1)S(1)}, bf16[256,128]{1,0:T(8,128)(2,1)S(1)}, f32[256,128]{1,0:T(8,128)S(1)}) custom-call(bf16[64,3712]{1,0:T(8,128)(2,1)S(1)} %join.1.refs_0_.refs_1_, bf16[64,3712]{1,0:T(8,128)(2,1)S(1)} %collective-permute-done.3.refs_1_, bf16[64,3712]{1,0:T(8,128)(2,1)S(1)} %collective-permute-done.4.refs_2_, ...), custom_call_target="tpu_custom_call" | custom-call | tf_op jit(solution)/shard_map/rest_rows/pallas_call | solution.py:162
  66.8 7.8 %hidden_rows.1.hidden = bf16[256,2048]{1,0:T(8,128)(2,1)S(1)} custom-call(bf16[256,3584]{1,0:T(8,128)(2,1)S(1)} %get-tuple-element.5.refs_0_, f32[256,128]{1,0:T(8,128)S(1)} %get-tuple-element.6.refs_1_, f32[4,128]{1,0:T(4,128)S(1)} %fusion.6.refs_2_, bf16[2,3584,512]{2,1,0:T(8,128)(2,1)S(1)} %bitcast.17, bf16[2,3584,512]{2,1,0:T(8,128)(2,1)S(1)} %bitcast.15, ...), custom_call_target="tpu_custom_call" | custom-call | tf_op jit(solution)/shard_map/hidden_rows/pallas_call | solution.py:193
  74.6 5.2 %copy-done.3 = bf16[4,512,3584]{2,1,0:T(8,128)(2,1)S(1)} copy-done((bf16[4,512,3584]{2,1,0:T(8,128)(2,1)S(1)}, bf16[4,512,3584]{2,1,0:T(8,128)(2,1)}, u32[]{:S(2)}) %copy-start.3) | copy-done | bytes 14680088
  79.7 3.9 %down_rows.2 = bf16[256,1792]{1,0:T(8,128)(2,1)S(1)} custom-call(bf16[256,2048]{1,0:T(8,128)(2,1)S(1)} %hidden_rows.1.hidden, bf16[256,128]{1,0:T(8,128)(2,1)S(1)} %get-tuple-element.7.shared_hidden, bf16[2048,3584]{1,0:T(8,128)(2,1)S(1)} %bitcast.18, bf16[128,3584]{1,0:T(8,128)(2,1)S(1)} %constant_dynamic-slice_fusion.shared_down), custom_call_target="tpu_custom_call" | custom-call | tf_op jit(solution)/shard_map/down_rows/pallas_call | solution.py:216
  83.7 0.6 collective-permute-start.6
  84.3 3.9 %down_rows.3 = bf16[256,1792]{1,0:T(8,128)(2,1)S(1)} custom-call(bf16[256,2048]{1,0:T(8,128)(2,1)S(1)} %hidden_rows.1.hidden, bf16[256,128]{1,0:T(8,128)(2,1)S(1)} %get-tuple-element.7.shared_hidden, bf16[2048,3584]{1,0:T(8,128)(2,1)S(1)} %bitcast.19, bf16[128,3584]{1,0:T(8,128)(2,1)S(1)} %constant_dynamic-slice_fusion.shared_down), custom_call_target="tpu_custom_call" | custom-call | tf_op jit(solution)/shard_map/down_rows/pallas_call | solution.py:216
  88.3 0.1 collective-permute-start.11
  88.4 0.1 convert_add_fusion.1
  88.5 1.6 %collective-permute-start.7 = (bf16[64,1792]{1,0:T(8,128)(2,1)S(1)}, bf16[64,1792]{1,0:T(8,128)(2,1)S(1)}, u32[]{:S(2)}, u32[]{:S(2)}) collective-permute-start(bf16[64,1792]{1,0:T(8,128)(2,1)S(1)} %slice.129), channel_id=1, source_target_pairs={{0,8},{4,12},{8,0},{12,4},{1,9},{5,13},{9,1},{13,5},{2,10},{6,14},... | collective-permute-start | bytes 688136 | tf_op jit(solution)/shard_map/ppermute | solution.py:233
  90.1 0.1 collective-permute-done.11
  90.1 0.1 convert_add_fusion
  90.3 1.6 %collective-permute-start.12 = (bf16[64,1792]{1,0:T(8,128)(2,1)S(1)}, bf16[64,1792]{1,0:T(8,128)(2,1)S(1)}, u32[]{:S(2)}, u32[]{:S(2)}) collective-permute-start(bf16[64,1792]{1,0:T(8,128)(2,1)S(1)} %slice.128), channel_id=1, source_target_pairs={{0,8},{4,12},{8,0},{12,4},{1,9},{5,13},{9,1},{13,5},{2,10},{6,14},... | collective-permute-start | bytes 688136 | tf_op jit(solution)/shard_map/ppermute | solution.py:233
  91.8 5.1 %collective-permute-done.7 = bf16[64,1792]{1,0:T(8,128)(2,1)S(1)} collective-permute-done((bf16[64,1792]{1,0:T(8,128)(2,1)S(1)}, bf16[64,1792]{1,0:T(8,128)(2,1)S(1)}, u32[]{:S(2)}, u32[]{:S(2)}) %collective-permute-start.7) | collective-permute-done | bytes 229408 | tf_op jit(solution)/shard_map/ppermute | solution.py:233
  97.0 3.6 %collective-permute-start.10 = (bf16[16,1792]{1,0:T(8,128)(2,1)S(1)}, bf16[16,1792]{1,0:T(8,128)(2,1)S(1)}, u32[]{:S(2)}, u32[]{:S(2)}) collective-permute-start(bf16[16,1792]{1,0:T(8,128)(2,1)S(1)} %get-tuple-element.17), channel_id=1, source_target_pairs={{0,3},{1,2},{2,1},{3,0},{4,7},{5,6},{6,5},{7,4},{8,11},{9,10},{10,... | collective-permute-start | bytes 172040 | tf_op jit(solution)/shard_map/ppermute | solution.py:233
  100.6 0.9 collective-permute-start.9
  101.5 0.1 fusion.11
  101.6 1.2 %collective-permute-start.13 = (bf16[16,1792]{1,0:T(8,128)(2,1)S(1)}, bf16[16,1792]{1,0:T(8,128)(2,1)S(1)}, u32[]{:S(2)}, u32[]{:S(2)}) collective-permute-start(bf16[16,1792]{1,0:T(8,128)(2,1)S(1)} %get-tuple-element.19), channel_id=1, source_target_pairs={{0,1},{1,0},{2,3},{3,2},{4,5},{5,4},{6,7},{7,6},{8,9},{9,8},{10,11... | collective-permute-start | bytes 172040 | tf_op jit(solution)/shard_map/ppermute | solution.py:233
  102.8 2.9 %collective-permute-start.14 = (bf16[16,1792]{1,0:T(8,128)(2,1)S(1)}, bf16[16,1792]{1,0:T(8,128)(2,1)S(1)}, u32[]{:S(2)}, u32[]{:S(2)}) collective-permute-start(bf16[16,1792]{1,0:T(8,128)(2,1)S(1)} %get-tuple-element.21), channel_id=1, source_target_pairs={{0,2},{1,3},{2,0},{3,1},{4,6},{5,7},{6,4},{7,5},{8,10},{9,11},{10,... | collective-permute-start | bytes 172040 | tf_op jit(solution)/shard_map/ppermute | solution.py:233
  105.8 1.5 %collective-permute-start.15 = (bf16[16,1792]{1,0:T(8,128)(2,1)S(1)}, bf16[16,1792]{1,0:T(8,128)(2,1)S(1)}, u32[]{:S(2)}, u32[]{:S(2)}) collective-permute-start(bf16[16,1792]{1,0:T(8,128)(2,1)S(1)} %get-tuple-element.20), channel_id=1, source_target_pairs={{0,3},{1,2},{2,1},{3,0},{4,7},{5,6},{6,5},{7,4},{8,11},{9,10},{10,... | collective-permute-start | bytes 172040 | tf_op jit(solution)/shard_map/ppermute | solution.py:233
  107.3 2.8 %collective-permute-done.14 = bf16[16,1792]{1,0:T(8,128)(2,1)S(1)} collective-permute-done((bf16[16,1792]{1,0:T(8,128)(2,1)S(1)}, bf16[16,1792]{1,0:T(8,128)(2,1)S(1)}, u32[]{:S(2)}, u32[]{:S(2)}) %collective-permute-start.14) | collective-permute-done | bytes 57376 | tf_op jit(solution)/shard_map/ppermute | solution.py:233
  110.1 1.6 %collective-permute-done.15 = bf16[16,1792]{1,0:T(8,128)(2,1)S(1)} collective-permute-done((bf16[16,1792]{1,0:T(8,128)(2,1)S(1)}, bf16[16,1792]{1,0:T(8,128)(2,1)S(1)}, u32[]{:S(2)}, u32[]{:S(2)}) %collective-permute-start.15) | collective-permute-done | bytes 57376 | tf_op jit(solution)/shard_map/ppermute | solution.py:233
  111.8 0.7 fusion
  112.4 0.2 multiply_reduce_fusion
  112.6 0.1 div.26
  112.7 0.2 subtract_reduce_fusion
  112.9 0.5 convert_multiply_fusion
  (53 shorter events, 0.4 us)
Async XLA Ops:
  0.6 22.6 %collective-permute-start = (bf16[16,3584]{1,0:T(8,128)(2,1)}, bf16[16,3584]{1,0:T(8,128)(2,1)S(1)}, u32[]{:S(2)}, u32[]{:S(2)}) collective-permute-start(bf16[16,3584]{1,0:T(8,128)(2,1)} %refs_0_.1), channel_id=1, source_target_pairs={{0,1},{1,0},{2,3},{3,2},{4,5},{5,4},{6,7},{7,6},{8,9},{9,8},{10,11... | collective-permute-start | bytes 344072 | tf_op jit(solution)/shard_map/ppermute | solution.py:233
  3.7 19.5 %collective-permute-start.1 = (bf16[16,3584]{1,0:T(8,128)(2,1)}, bf16[16,3584]{1,0:T(8,128)(2,1)S(1)}, u32[]{:S(2)}, u32[]{:S(2)}) collective-permute-start(bf16[16,3584]{1,0:T(8,128)(2,1)} %refs_0_.1), channel_id=1, source_target_pairs={{0,2},{1,3},{2,0},{3,1},{4,6},{5,7},{6,4},{7,5},{8,10},{9,11},{10,... | collective-permute-start | bytes 344072 | tf_op jit(solution)/shard_map/ppermute | solution.py:233
  6.3 16.9 %collective-permute-start.2 = (bf16[16,3584]{1,0:T(8,128)(2,1)}, bf16[16,3584]{1,0:T(8,128)(2,1)S(1)}, u32[]{:S(2)}, u32[]{:S(2)}) collective-permute-start(bf16[16,3584]{1,0:T(8,128)(2,1)} %refs_0_.1), channel_id=1, source_target_pairs={{0,3},{1,2},{2,1},{3,0},{4,7},{5,6},{6,5},{7,4},{8,11},{9,10},{10,... | collective-permute-start | bytes 344072 | tf_op jit(solution)/shard_map/ppermute | solution.py:233
  12.0 11.3 %copy-start.4 = (bf16[16,3584]{1,0:T(8,128)(2,1)S(1)}, bf16[16,3584]{1,0:T(8,128)(2,1)}, u32[]{:S(2)}) copy-start(bf16[16,3584]{1,0:T(8,128)(2,1)} %refs_0_.1) | copy-start | bytes 344068
  16.7 2.9 %copy-start = (bf16[2,3584,512]{2,1,0:T(8,128)(2,1)}, bf16[2,3584,512]{2,1,0:T(8,128)(2,1)S(1)}, u32[]{:S(2)}) copy-start(bf16[2,3584,512]{2,1,0:T(8,128)(2,1)S(1)} %apart.5.refs_5_.refs_4_) | copy-start | bytes 22020100
  19.6 3.0 %copy-start.2 = (bf16[2,3584,512]{2,1,0:T(8,128)(2,1)}, bf16[2,3584,512]{2,1,0:T(8,128)(2,1)S(1)}, u32[]{:S(2)}) copy-start(bf16[2,3584,512]{2,1,0:T(8,128)(2,1)S(1)} %apart.4.refs_1_.refs_3_) | copy-start | bytes 22020100
  23.3 3.1 %copy-start.1 = (bf16[2,3584,512]{2,1,0:T(8,128)(2,1)S(1)}, bf16[2,3584,512]{2,1,0:T(8,128)(2,1)}, u32[]{:S(2)}) copy-start(bf16[2,3584,512]{2,1,0:T(8,128)(2,1)} %copy-done) | copy-start | bytes 22020100
  26.4 12.1 %collective-permute-start.4 = (bf16[64,3712]{1,0:T(8,128)(2,1)S(1)}, bf16[64,3712]{1,0:T(8,128)(2,1)S(1)}, u32[]{:S(2)}, u32[]{:S(2)}) collective-permute-start(bf16[64,3712]{1,0:T(8,128)(2,1)S(1)} %join.1.refs_0_.refs_1_), channel_id=1, source_target_pairs={{0,8},{4,12},{8,0},{12,4},{1,9},{5,13},{9,1},{13,5},{2,10},{6,14},... | collective-permute-start | bytes 1425416 | tf_op jit(solution)/shard_map/ppermute | solution.py:233
  31.6 20.0 %collective-permute-start.3 = (bf16[64,3712]{1,0:T(8,128)(2,1)S(1)}, bf16[64,3712]{1,0:T(8,128)(2,1)S(1)}, u32[]{:S(2)}, u32[]{:S(2)}) collective-permute-start(bf16[64,3712]{1,0:T(8,128)(2,1)S(1)} %join.1.refs_0_.refs_1_), channel_id=1, source_target_pairs={{0,4},{4,0},{8,12},{12,8},{1,5},{5,1},{9,13},{13,9},{2,6},{6,2},{1... | collective-permute-start | bytes 1425416 | tf_op jit(solution)/shard_map/ppermute | solution.py:233
  38.5 20.2 %collective-permute-start.5 = (bf16[64,3712]{1,0:T(8,128)(2,1)S(1)}, bf16[64,3712]{1,0:T(8,128)(2,1)S(1)}, u32[]{:S(2)}, u32[]{:S(2)}) collective-permute-start(bf16[64,3712]{1,0:T(8,128)(2,1)S(1)} %collective-permute-done.4.refs_2_), channel_id=1, source_target_pairs={{0,4},{4,0},{8,12},{12,8},{1,5},{5,1},{9,13},{13,9},{2,6},{6,2},{1... | collective-permute-start | bytes 1425416 | tf_op jit(solution)/shard_map/ppermute | solution.py:233
  40.1 26.6 %slice-start = ((s8[7340032]{0:T(1024)(128)(4,1)}), s8[4194304]{0:T(1024)(128)(4,1)S(1)}, s32[]{:S(2)}) async-start(s8[7340032]{0:T(1024)(128)(4,1)} %bitcast.14), calls=%async_computation | async-start | bytes 8388608
  40.1 26.6 %slice-start.2 = ((s8[7340032]{0:T(1024)(128)(4,1)}), s8[4194304]{0:T(1024)(128)(4,1)S(1)}, s32[]{:S(2)}) async-start(s8[7340032]{0:T(1024)(128)(4,1)} %bitcast.16), calls=%async_computation.2 | async-start | bytes 8388608
  46.1 20.6 %slice-start.1 = ((s8[7340032]{0:T(1024)(128)(4,1)}), s8[3145728]{0:T(1024)(128)(4,1)S(1)}, s32[]{:S(2)}) async-start(s8[7340032]{0:T(1024)(128)(4,1)} %bitcast.14), calls=%async_computation.1 | async-start | bytes 6291456
  46.1 20.6 %slice-start.3 = ((s8[7340032]{0:T(1024)(128)(4,1)}), s8[3145728]{0:T(1024)(128)(4,1)S(1)}, s32[]{:S(2)}) async-start(s8[7340032]{0:T(1024)(128)(4,1)} %bitcast.16), calls=%async_computation.3 | async-start | bytes 6291456
  74.5 5.2 %copy-start.3 = (bf16[4,512,3584]{2,1,0:T(8,128)(2,1)S(1)}, bf16[4,512,3584]{2,1,0:T(8,128)(2,1)}, u32[]{:S(2)}) copy-start(bf16[4,512,3584]{2,1,0:T(8,128)(2,1)} %param.16) | copy-start | bytes 44040196
  83.7 4.7 %collective-permute-start.6 = (bf16[128,1792]{1,0:T(8,128)(2,1)S(1)}, bf16[128,1792]{1,0:T(8,128)(2,1)S(1)}, u32[]{:S(2)}, u32[]{:S(2)}) collective-permute-start(bf16[128,1792]{1,0:T(8,128)(2,1)S(1)} %slice.95), channel_id=1, source_target_pairs={{0,4},{4,0},{8,12},{12,8},{1,5},{5,1},{9,13},{13,9},{2,6},{6,2},{1... | collective-permute-start | bytes 1376264 | tf_op jit(solution)/shard_map/ppermute | solution.py:233
  88.2 24.2 %copy-start.5 = (f32[3584]{0:T(1024)S(1)}, f32[3584]{0:T(1024)}, u32[]{:S(2)}) copy-start(f32[3584]{0:T(1024)} %param.17) | copy-start | bytes 43012
  88.2 24.7 %copy-start.6 = (s32[8]{0:T(128)S(1)}, s32[8]{0:T(128)}, u32[]{:S(2)}) copy-start(s32[8]{0:T(128)} %param.12) | copy-start | bytes 100
  88.3 1.9 %collective-permute-start.11 = (bf16[128,1792]{1,0:T(8,128)(2,1)S(1)}, bf16[128,1792]{1,0:T(8,128)(2,1)S(1)}, u32[]{:S(2)}, u32[]{:S(2)}) collective-permute-start(bf16[128,1792]{1,0:T(8,128)(2,1)S(1)} %slice.103), channel_id=1, source_target_pairs={{0,4},{4,0},{8,12},{12,8},{1,5},{5,1},{9,13},{13,9},{2,6},{6,2},{1... | collective-permute-start | bytes 1376264 | tf_op jit(solution)/shard_map/ppermute | solution.py:233
  88.5 8.5 %collective-permute-start.7 = (bf16[64,1792]{1,0:T(8,128)(2,1)S(1)}, bf16[64,1792]{1,0:T(8,128)(2,1)S(1)}, u32[]{:S(2)}, u32[]{:S(2)}) collective-permute-start(bf16[64,1792]{1,0:T(8,128)(2,1)S(1)} %slice.129), channel_id=1, source_target_pairs={{0,8},{4,12},{8,0},{12,4},{1,9},{5,13},{9,1},{13,5},{2,10},{6,14},... | collective-permute-start | bytes 688136 | tf_op jit(solution)/shard_map/ppermute | solution.py:233
  90.3 11.2 %collective-permute-start.12 = (bf16[64,1792]{1,0:T(8,128)(2,1)S(1)}, bf16[64,1792]{1,0:T(8,128)(2,1)S(1)}, u32[]{:S(2)}, u32[]{:S(2)}) collective-permute-start(bf16[64,1792]{1,0:T(8,128)(2,1)S(1)} %slice.128), channel_id=1, source_target_pairs={{0,8},{4,12},{8,0},{12,4},{1,9},{5,13},{9,1},{13,5},{2,10},{6,14},... | collective-permute-start | bytes 688136 | tf_op jit(solution)/shard_map/ppermute | solution.py:233
  97.0 8.7 %collective-permute-start.10 = (bf16[16,1792]{1,0:T(8,128)(2,1)S(1)}, bf16[16,1792]{1,0:T(8,128)(2,1)S(1)}, u32[]{:S(2)}, u32[]{:S(2)}) collective-permute-start(bf16[16,1792]{1,0:T(8,128)(2,1)S(1)} %get-tuple-element.17), channel_id=1, source_target_pairs={{0,3},{1,2},{2,1},{3,0},{4,7},{5,6},{6,5},{7,4},{8,11},{9,10},{10,... | collective-permute-start | bytes 172040 | tf_op jit(solution)/shard_map/ppermute | solution.py:233
  100.6 6.6 %collective-permute-start.8 = (bf16[16,1792]{1,0:T(8,128)(2,1)S(1)}, bf16[16,1792]{1,0:T(8,128)(2,1)S(1)}, u32[]{:S(2)}, u32[]{:S(2)}) collective-permute-start(bf16[16,1792]{1,0:T(8,128)(2,1)S(1)} %get-tuple-element.16), channel_id=1, source_target_pairs={{0,1},{1,0},{2,3},{3,2},{4,5},{5,4},{6,7},{7,6},{8,9},{9,8},{10,11... | collective-permute-start | bytes 172040 | tf_op jit(solution)/shard_map/ppermute | solution.py:233
  100.6 6.6 %collective-permute-start.9 = (bf16[16,1792]{1,0:T(8,128)(2,1)S(1)}, bf16[16,1792]{1,0:T(8,128)(2,1)S(1)}, u32[]{:S(2)}, u32[]{:S(2)}) collective-permute-start(bf16[16,1792]{1,0:T(8,128)(2,1)S(1)} %get-tuple-element.18), channel_id=1, source_target_pairs={{0,2},{1,3},{2,0},{3,1},{4,6},{5,7},{6,4},{7,5},{8,10},{9,11},{10,... | collective-permute-start | bytes 172040 | tf_op jit(solution)/shard_map/ppermute | solution.py:233
  101.6 5.8 %collective-permute-start.13 = (bf16[16,1792]{1,0:T(8,128)(2,1)S(1)}, bf16[16,1792]{1,0:T(8,128)(2,1)S(1)}, u32[]{:S(2)}, u32[]{:S(2)}) collective-permute-start(bf16[16,1792]{1,0:T(8,128)(2,1)S(1)} %get-tuple-element.19), channel_id=1, source_target_pairs={{0,1},{1,0},{2,3},{3,2},{4,5},{5,4},{6,7},{7,6},{8,9},{9,8},{10,11... | collective-permute-start | bytes 172040 | tf_op jit(solution)/shard_map/ppermute | solution.py:233
  102.8 7.3 %collective-permute-start.14 = (bf16[16,1792]{1,0:T(8,128)(2,1)S(1)}, bf16[16,1792]{1,0:T(8,128)(2,1)S(1)}, u32[]{:S(2)}, u32[]{:S(2)}) collective-permute-start(bf16[16,1792]{1,0:T(8,128)(2,1)S(1)} %get-tuple-element.21), channel_id=1, source_target_pairs={{0,2},{1,3},{2,0},{3,1},{4,6},{5,7},{6,4},{7,5},{8,10},{9,11},{10,... | collective-permute-start | bytes 172040 | tf_op jit(solution)/shard_map/ppermute | solution.py:233
  105.8 6.0 %collective-permute-start.15 = (bf16[16,1792]{1,0:T(8,128)(2,1)S(1)}, bf16[16,1792]{1,0:T(8,128)(2,1)S(1)}, u32[]{:S(2)}, u32[]{:S(2)}) collective-permute-start(bf16[16,1792]{1,0:T(8,128)(2,1)S(1)} %get-tuple-element.20), channel_id=1, source_target_pairs={{0,3},{1,2},{2,1},{3,0},{4,7},{5,6},{6,5},{7,4},{8,11},{9,10},{10,... | collective-permute-start | bytes 172040 | tf_op jit(solution)/shard_map/ppermute | solution.py:233

commit v3 on v2

--- a/solution.py
+++ b/solution.py
@@ -10,9 +10,9 @@
 
 ROT = 128
 CORES = 2
-SMALL_VMEM = 12 * 1024 * 1024
+SMALL_VMEM = 10 * 1024 * 1024
+HIDDEN_VMEM = 5 * 1024 * 1024
 VMEM_BYTES = 16 * 1024 * 1024
-SCATTER_CHUNKS = 2
 
 
 def sign_matrix(copies):
@@ -35,33 +35,74 @@
     return pltpu.VMEM(shape, dtype)
 
 
-def apart_kernel(rows, chunk, *refs):
-    source, out = refs[0], refs[-1]
-    step = pl.program_id(0)
-    count = 2 * out.shape[2] // 128
-    for at in range(0, rows, chunk):
-        pairs = source[0, at * count : (at + chunk) * count, :].reshape(chunk, count, 128)
-        pairs = jnp.swapaxes(pairs, 0, 1)
-        here = pl.ds(pl.multiple_of(step * rows + at, chunk), chunk)
-        for q in range(count):
-            out[q % 2, here, (q // 2) * 128 : (q // 2 + 1) * 128] = pairs[q]
-
-
-def apart(packed, expert, feature_len, inner, after):
+def apart_kernel(experts, rows, chunk, n_after, *refs):
+    source = refs[0]
+    outs = refs[1 + n_after : 1 + n_after + len(experts)]
+    done, held, sems = refs[1 + n_after + len(experts) :]
+    slots = held.shape[0]
+    count = 2 * outs[0].shape[2] // 128
+    pieces = [(n, step) for n in range(len(experts)) for step in range(outs[0].shape[1] // rows)]
+
+    def copy(at):
+        n, step = pieces[at]
+        return pltpu.make_async_copy(
+            source.at[experts[n], pl.ds(step * rows * count, rows * count)],
+            held.at[at % slots],
+            sems.at[at % slots],
+        )
+
+    for at in range(min(slots, len(pieces))):
+        copy(at).start()
+    for at, (n, step) in enumerate(pieces):
+        copy(at).wait()
+        for row in range(0, rows, chunk):
+            pairs = held[at % slots, row * count : (row + chunk) * count, :]
+            pairs = jnp.swapaxes(pairs.reshape(chunk, count, 128), 0, 1)
+            here = slice(step * rows + row, step * rows + row + chunk)
+            for q in range(count):
+                outs[n][q % 2, here, (q // 2) * 128 : (q // 2 + 1) * 128] = pairs[q]
+        if at + slots < len(pieces):
+            copy(at + slots).start()
+    done[...] = jnp.zeros_like(done)
+
+
+def apart(packed, experts, feature_len, inner, after):
     count = 2 * inner // 128
     rows = feature_len // 4 if feature_len % 256 == 0 else feature_len
     chunk = 64 if rows % 64 == 0 else rows
-    return pl.pallas_call(
-        functools.partial(apart_kernel, rows, chunk),
-        grid=(feature_len // rows,),
-        in_specs=[pl.BlockSpec((1, rows * count, 128), lambda s: (expert, s, 0))]
-        + [pl.BlockSpec(memory_space=pl.ANY)] * len(after),
-        out_specs=pl.BlockSpec(memory_space=pltpu.VMEM),
-        out_shape=vmem((2, feature_len, inner), packed.dtype),
+    whole = pl.BlockSpec(memory_space=pltpu.VMEM)
+    out = pl.pallas_call(
+        functools.partial(apart_kernel, experts, rows, chunk, len(after)),
+        in_specs=[pl.BlockSpec(memory_space=pl.ANY)] * (1 + len(after)),
+        out_specs=[whole] * (len(experts) + 1),
+        out_shape=[vmem((2, feature_len, inner), packed.dtype)] * len(experts)
+        + [jax.ShapeDtypeStruct((8, 128), jnp.float32)],
+        scratch_shapes=[
+            pltpu.VMEM((4, rows * count, 128), packed.dtype),
+            pltpu.SemaphoreType.DMA((4,)),
+        ],
         compiler_params=pltpu.CompilerParams(vmem_limit_bytes=SMALL_VMEM),
         cost_estimate=pl.CostEstimate(flops=0, bytes_accessed=1024, transcendentals=0),
         name="apart",
     )(packed, *after)
+    return out[:-1], out[-1]
+
+
+def pass_kernel(value, *refs):
+    refs[-1][...] = value[...]
+
+
+def pass_on(value, after):
+    return pl.pallas_call(
+        pass_kernel,
+        in_specs=[pl.BlockSpec(memory_space=pltpu.VMEM)]
+        + [pl.BlockSpec(memory_space=pl.ANY)] * len(after),
+        out_specs=pl.BlockSpec(memory_space=pltpu.VMEM),
+        out_shape=vmem(value.shape, value.dtype),
+        compiler_params=pltpu.CompilerParams(vmem_limit_bytes=HIDDEN_VMEM),
+        cost_estimate=pl.CostEstimate(flops=0, bytes_accessed=1024, transcendentals=0),
+        name="pass_on",
+    )(value, *after)
 
 
 def join_kernel(n_pieces, *refs):
@@ -81,41 +122,34 @@
         in_specs=[whole] * (len(pieces) + 1) + [pl.BlockSpec(memory_space=pl.ANY)] * len(after),
         out_specs=whole,
         out_shape=vmem((lanes.shape[0], pieces[0].shape[1] + lanes.shape[1]), lanes.dtype),
-        compiler_params=pltpu.CompilerParams(vmem_limit_bytes=SMALL_VMEM),
+        compiler_params=pltpu.CompilerParams(vmem_limit_bytes=HIDDEN_VMEM),
         cost_estimate=pl.CostEstimate(flops=0, bytes_accessed=1024, transcendentals=0),
         name="join",
     )(*pieces, lanes, *after)
 
 
-def rotate(source, signs, target, base):
-    rows = source.shape[0]
+def rotate(sources, signs, target, bases):
     feature_len = target.shape[1]
     width = signs.shape[0]
-
-    def block(index, carry):
-        at = pl.ds(pl.multiple_of(index * width, width), width)
-        rotated = jnp.dot(source[:, at], signs[...], preferred_element_type=jnp.float32) * (
-            1.0 / math.sqrt(ROT)
-        )
-        parts = []
-        for piece_at in range(0, width, ROT):
-            part = rotated[:, piece_at : piece_at + ROT]
-            scale = (jnp.max(jnp.abs(part), axis=1, keepdims=True) + 1e-06).astype(jnp.bfloat16)
-            scale = scale.astype(jnp.float32)
-            quantized = (part / scale).astype(jnp.bfloat16)
-            parts.append((quantized.astype(jnp.float32) * scale).astype(jnp.bfloat16))
-        target[base : base + rows, at] = jnp.concatenate(parts, axis=1)
-        return carry
-
-    lax.fori_loop(0, feature_len // width, block, 0)
+    for at in range(0, feature_len, width):
+        for source, base in zip(sources, bases):
+            rotated = jnp.dot(
+                source[:, at : at + width], signs[...], preferred_element_type=jnp.float32
+            ) * (1.0 / math.sqrt(ROT))
+            for piece_at in range(0, width, ROT):
+                part = rotated[:, piece_at : piece_at + ROT]
+                scale = jnp.max(jnp.abs(part), axis=1, keepdims=True) + 1e-06
+                scale = scale.astype(jnp.bfloat16).astype(jnp.float32)
+                quantized = (part * (1.0 / scale)).astype(jnp.bfloat16).astype(jnp.float32)
+                target[
+                    base : base + source.shape[0], at + piece_at : at + piece_at + ROT
+                ] = (quantized * scale).astype(jnp.bfloat16)
 
 
 def first_kernel(n_pieces, *refs):
     signs, out = refs[n_pieces:]
-    base = 0
-    for piece in refs[:n_pieces]:
-        rotate(piece, signs, out, base)
-        base += piece.shape[0]
+    pieces = refs[:n_pieces]
+    rotate(pieces, signs, out, [n * pieces[0].shape[0] for n in range(n_pieces)])
 
 
 def first_rows(pieces, signs, feature_len):
@@ -126,7 +160,7 @@
         in_specs=[whole] * (len(pieces) + 1),
         out_specs=whole,
         out_shape=vmem((rows, feature_len), jnp.bfloat16),
-        compiler_params=pltpu.CompilerParams(vmem_limit_bytes=SMALL_VMEM),
+        compiler_params=pltpu.CompilerParams(vmem_limit_bytes=HIDDEN_VMEM),
         cost_estimate=pl.CostEstimate(flops=0, bytes_accessed=1024, transcendentals=0),
         name="first_rows",
     )(*pieces, signs)
@@ -138,6 +172,7 @@
     signs, first, shared, deq, shared_hidden, combine, rows_s = refs[n_pieces:]
     count = pieces[0].shape[0]
     feature_len = deq.shape[1]
+    sources, bases = [], []
     for core in range(CORES):
         for chip in range(n_chips):
             base = (core * n_chips + chip) * count
@@ -146,9 +181,11 @@
                 deq[base : base + count, :] = first[core * count : (core + 1) * count, :]
             else:
                 piece = pieces[CORES + core * (n_chips - 1) + chip - 1]
-                rotate(piece, signs, deq, base)
+                sources.append(piece)
+                bases.append(base)
             rows_s[base : base + count, :] = piece[:, :feature_len]
             combine[base : base + count, :] = piece[:, feature_len:].astype(jnp.float32)
+    rotate(sources, signs, deq, bases)
     part = shared.shape[1] // 2
     both = jnp.dot(rows_s[...], shared[...], preferred_element_type=jnp.float32)
     gate, up = both[:, :part], both[:, part:]
@@ -169,7 +206,7 @@
             vmem((rows, pieces[0].shape[1] - feature_len), jnp.float32),
         ],
         scratch_shapes=[pltpu.VMEM((rows, feature_len), jnp.bfloat16)],
-        compiler_params=pltpu.CompilerParams(vmem_limit_bytes=SMALL_VMEM),
+        compiler_params=pltpu.CompilerParams(vmem_limit_bytes=HIDDEN_VMEM + 2 * rows * feature_len),
         name="rest_rows",
     )(*pieces, signs, first, shared)
 
@@ -195,19 +232,19 @@
         in_specs=[whole] * (3 + len(weights)),
         out_specs=whole,
         out_shape=vmem((rows, len(weights) * weights[0].shape[2]), jnp.bfloat16),
-        compiler_params=pltpu.CompilerParams(vmem_limit_bytes=SMALL_VMEM),
+        compiler_params=pltpu.CompilerParams(vmem_limit_bytes=HIDDEN_VMEM),
         name="hidden_rows",
     )(deq, combine, select, *weights)
 
 
-def down_kernel(hidden, shared_hidden, down, shared_down, out):
+def down_kernel(index, hidden, shared_hidden, down, shared_down, out):
     out[...] = (
         jnp.dot(hidden[...], down[...], preferred_element_type=jnp.float32)
         + jnp.dot(shared_hidden[...], shared_down[...], preferred_element_type=jnp.float32)
     ).astype(out.dtype)
 
 
-def down_rows(hidden, shared_hidden, down, shared_down, start, stop):
+def down_rows(index, hidden, shared_hidden, down, shared_down, start, stop):
     rows = hidden.shape[0]
     inner = down.shape[0]
     tile = math.gcd(512, math.gcd(start, stop - start))
@@ -215,18 +252,21 @@
     whole = pl.BlockSpec(memory_space=pltpu.VMEM)
     return pl.pallas_call(
         down_kernel,
-        grid=((stop - start) // tile,),
-        in_specs=[
-            whole,
-            whole,
-            pl.BlockSpec((inner, tile), lambda s: (0, first + s)),
-            pl.BlockSpec((shared_down.shape[0], tile), lambda s: (0, first + s)),
-        ],
-        out_specs=pl.BlockSpec((rows, tile), lambda s: (0, s)),
+        grid_spec=pltpu.PrefetchScalarGridSpec(
+            num_scalar_prefetch=1,
+            grid=((stop - start) // tile,),
+            in_specs=[
+                whole,
+                whole,
+                pl.BlockSpec((inner, tile), lambda s, at: (0, first + s)),
+                pl.BlockSpec((shared_hidden.shape[1], tile), lambda s, at: (at[0], first + s)),
+            ],
+            out_specs=pl.BlockSpec((rows, tile), lambda s, at: (0, s)),
+        ),
         out_shape=jax.ShapeDtypeStruct((rows, stop - start), jnp.bfloat16),
         compiler_params=pltpu.CompilerParams(vmem_limit_bytes=VMEM_BYTES),
         name="down_rows",
-    )(hidden, shared_hidden, down, shared_down)
+    )(index, hidden, shared_hidden, down, shared_down)
 
 
 def exchange(value, axis, flip):
@@ -272,10 +312,10 @@
     part_len = shared_len // expert_count
     if part_len % 128 == 0:
         shared_in = lax.dynamic_slice_in_dim(shared_gate_up, expert_at * part_len, part_len, 2)
-        shared_out = lax.dynamic_slice_in_dim(shared_down, expert_at * part_len, part_len, 0)
+        shared_out, index = shared_down, expert_at.reshape(1)
     else:
         mine = lax.broadcasted_iota(jnp.int32, (shared_len, 1), 0) // part_len == expert_at
-        shared_in = shared_gate_up
+        shared_in, index = shared_gate_up, jnp.zeros((1,), jnp.int32)
         shared_out = jnp.where(mine, shared_down, jnp.zeros_like(shared_down))
     shared_in = shared_in.reshape(feature_len, -1)
     signs = sign_matrix(2 if feature_len % (2 * ROT) == 0 else 1)
@@ -284,52 +324,59 @@
     packed = packed.transpose(0, 1, 3, 2, 4).reshape(n_local, -1, 128)
     packed = pltpu.with_memory_space_constraint(packed, pltpu.HBM)
 
-    def prepared(expert, after):
-        return apart(packed, expert, feature_len, inner, after)
-
-    early = (n_local + 1) // 2
+    def prepared(experts, after):
+        return apart(packed, experts, feature_len, inner, after)
+
+    early = (n_local + 3) // 4
     from_z = [exchange(tokens, "narrow", flip) for flip in range(1, narrow_count)]
-    weights = []
-    for expert in range(early):
-        weights.append(prepared(expert, weights[-1:]))
-    along_z = join([tokens] + from_z, lanes, weights[-1:])
+    weights, done = prepared(list(range(early)), [lanes, shared_in, select, signs, index])
+    along_z = join([tokens] + from_z, lanes, [done])
     from_x = [exchange(along_z, "expert", flip * CORES) for flip in range(1, chips)]
     near = exchange(along_z, "expert", 1)
+    after = [along_z]
+    if n_local > early:
+        late, done = prepared(list(range(early, n_local)), after)
+        weights = weights + late
+        after = [done]
+    from_x = [pass_on(part, after) for part in from_x]
+    from_both = [exchange(part, "expert", 1) for part in from_x]
     first = first_rows([along_z, near], signs, feature_len)
-    after = [along_z]
-    for expert in range(early, n_local):
-        weights.append(prepared(expert, after))
-        after = weights[-1:]
-    from_both = [exchange(part, "expert", 1) for part in from_x]
 
     deq, shared_hidden, combine = rest_rows(
         [along_z, near] + from_x + from_both, signs, first, shared_in, chips
     )
+    down = pltpu.with_memory_space_constraint(
+        expert_down.reshape(n_local * inner, feature_len), pltpu.HBM
+    )
     hidden = hidden_rows(deq, combine, select, weights)
-    down = expert_down.reshape(n_local * inner, feature_len)
 
     half = own_rows * narrow_count * chips
+    cut = feature_len * 5 // 14 // 256 * 256
+
+    def by_core(start, stop):
+        part = down_rows(index, hidden, shared_hidden, down, shared_out, start, stop)
+        near = exchange(part[half:], "expert", 1)
+        total = part[:half].astype(jnp.float32) + near.astype(jnp.float32)
+        return total.reshape(chips, narrow_count, own_rows, stop - start)
+
+    def add_up(parts, axis, step):
+        total = parts[0]
+        for flip in range(1, len(parts)):
+            part = exchange(parts[flip].astype(jnp.bfloat16), axis, flip * step)
+            total = total + part.astype(jnp.float32)
+        return total
+
     totals = []
-    width = feature_len // SCATTER_CHUNKS
-    for chunk in range(SCATTER_CHUNKS):
-        part = down_rows(
-            hidden, shared_hidden, down, shared_out, chunk * width, (chunk + 1) * width
-        )
-        near = exchange(part[half:], "expert", 1)
-        by_core = part[:half].astype(jnp.float32) + near.astype(jnp.float32)
-        by_core = by_core.reshape(chips, narrow_count * own_rows, width)
-        by_chip = by_core[0]
-        for flip in range(1, chips):
-            by_chip = by_chip + exchange(
-                by_core[flip].astype(jnp.bfloat16), "expert", flip * CORES
-            ).astype(jnp.float32)
-        by_chip = by_chip.reshape(narrow_count, own_rows, width)
-        total = by_chip[0]
-        for flip in range(1, narrow_count):
-            total = total + exchange(
-                by_chip[flip].astype(jnp.bfloat16), "narrow", flip
-            ).astype(jnp.float32)
-        totals.append(total)
+    if cut:
+        parts = by_core(0, cut)
+        parts = add_up(
+            [parts[:, n].reshape(chips * own_rows, cut) for n in range(narrow_count)], "narrow", 1
+        ).reshape(chips, own_rows, cut)
+        totals.append(add_up([parts[c] for c in range(chips)], "expert", CORES))
+    parts = by_core(cut, feature_len).reshape(chips, narrow_count * own_rows, feature_len - cut)
+    parts = add_up([parts[c] for c in range(chips)], "expert", CORES)
+    parts = parts.reshape(narrow_count, own_rows, feature_len - cut)
+    totals.append(add_up([parts[n] for n in range(narrow_count)], "narrow", 1))
     total_sum = jnp.concatenate(totals, axis=1)
     mixed = total_sum.astype(jnp.bfloat16)
     row_score = jnp.sum(total_sum * readout[None, :], axis=1) / jnp.sqrt(

time: 114 us -> 79.3 us (0.70)
  local copies, waits for them, and re-layouts: 19.6 us -> 4.24 us
  Pallas kernels: 51.6 us -> 36.5 us
  waiting for transfers between devices: 16.5 us -> 13.9 us
  starting transfers between devices: 21.5 us -> 20 us
    unnamed x23 -> x10, local copies, waits for them, and re-layouts: 14.4 us -> 0.27 us
    pallas_call x1, Pallas kernels: 7.94 us -> 1.6 us  [rest_rows(): pl.pallas_call(functools.partial(rest_kernel, len(pieces), n_chips), in_s...]
    pallas_call x1, Pallas kernels: 7.15 us -> 1.12 us  [first_rows(): pl.pallas_call(functools.partial(first_kernel, len(pieces)), in_specs=[wh...]
    pallas_call x6 -> x5, Pallas kernels: 28.7 us -> 25.8 us  [the longest x2 14 us: down_rows(): pl.pallas_call(down_kernel, grid_spec=pltpu.PrefetchScalarGridSpec(num_sc...]
    ppermute x16, waiting for transfers between devices: 16.5 us -> 13.9 us  [exchange(): lax.ppermute(value, axis, [(i, i ^ flip) for i in range(lax.axis_size(axi...]
    ppermute x16, starting transfers between devices: 21.5 us -> 20 us  [exchange(): lax.ppermute(value, axis, [(i, i ^ flip) for i in range(lax.axis_size(axi...]
    dynamic_slice x1 -> x0, local copies, waits for them, and re-layouts: 1.25 us -> none  [per_device(): lax.dynamic_slice_in_dim(shared_down, expert_at * part_len, part_len, 0)]
  transfers between devices with their start and end apart: 16 -> 16, of which waited for: 5 -> 8; matrix products, arithmetic and copies ran while one was open for 6% -> 7% of each run, Pallas kernels for 28% -> 28%
where the time goes in v3:
time: 79.3 us; the launch traced here: 78.8 us
  Pallas kernels  36.5 us (46%)
  starting transfers between devices  20 us (25%)
  waiting for transfers between devices  13.9 us (18%)
  local copies, waits for them, and re-layouts  4.24 us (5%)
  other arithmetic  3.16 us (4%)
  between operations  0.96 us (1%)
    ppermute x16, starting transfers between devices, exchange(): lax.ppermute(value, axis, [(i, i ^ flip) for i in range(lax.axis_size(axi...  20 us
    pallas_call x2, Pallas kernels, down_rows(): pl.pallas_call(down_kernel, grid_spec=pltpu.PrefetchScalarGridSpec(num_sc...  14 us
    ppermute x16, waiting for transfers between devices, exchange(): lax.ppermute(value, axis, [(i, i ^ flip) for i in range(lax.axis_size(axi...  13.9 us
    pallas_call x2, Pallas kernels, apart(): pl.pallas_call(functools.partial(apart_kernel, experts, rows, chunk, len(...  11.8 us
    pallas_call x1, Pallas kernels, hidden_rows(): pl.pallas_call(functools.partial(hidden_kernel, len(weights)), in_specs=[...  7.96 us
    dynamic_slice x1, local copies, waits for them, and re-layouts, per_device(): lax.dynamic_slice_in_dim(shared_gate_up, expert_at * part_len, part_len, 2)  3.07 us
    pallas_call x1, Pallas kernels, rest_rows(): pl.pallas_call(functools.partial(rest_kernel, len(pieces), n_chips), in_s...  1.6 us
  transfers between devices with their start and end apart: 16, of which 8 were waited for; matrix products, arithmetic and copies ran while one was open for 7% of the time, Pallas kernels for 28%

profile of v3, /device:TPU:0, one launch (start us, length us, event | category | flops | bytes accessed | tf_op | source)
XLA Modules:
  0.0 78.8 jit_solution(7159278638458161770)
XLA Ops:
  0.6 4.1 %collective-permute-start.1 = (bf16[16,3584]{1,0:T(8,128)(2,1)}, bf16[16,3584]{1,0:T(8,128)(2,1)S(1)}, u32[]{:S(2)}, u32[]{:S(2)}) collective-permute-start(bf16[16,3584]{1,0:T(8,128)(2,1)} %refs_0_.1), channel_id=1, source_target_pairs={{0,2},{1,3},{2,0},{3,1},{4,6},{5,7},{6,4},{7,5},{8,10},{9,11},{10,... | collective-permute-start | bytes 344072 | tf_op jit(solution)/shard_map/ppermute | solution.py:273
  4.7 1.6 %collective-permute-start = (bf16[16,3584]{1,0:T(8,128)(2,1)}, bf16[16,3584]{1,0:T(8,128)(2,1)S(1)}, u32[]{:S(2)}, u32[]{:S(2)}) collective-permute-start(bf16[16,3584]{1,0:T(8,128)(2,1)} %refs_0_.1), channel_id=1, source_target_pairs={{0,1},{1,0},{2,3},{3,2},{4,5},{5,4},{6,7},{7,6},{8,9},{9,8},{10,11... | collective-permute-start | bytes 344072 | tf_op jit(solution)/shard_map/ppermute | solution.py:273
  6.4 0.7 select_reduce_fusion
  7.1 0.1 copy.24
  7.2 3.1 %constant_dynamic-slice_fusion = bf16[3584,2,128]{2,1,0:T(2,128)(2,1)S(1)} fusion(bf16[3584,2,512]{2,1,0:T(2,128)(2,1)} %param.13, s32[]{:T(128)S(6)} %select_n.62), kind=kLoop, calls=%fused_computation.44 | loop fusion | bytes 3670020 | tf_op jit(solution)/shard_map/dynamic_slice | solution.py:314
  10.3 0.2 copy.35
  10.5 0.1 pad_maximum_fusion.1
  10.6 0.6 gather_fusion
  11.2 0.3 select_convert_fusion.refs_4_.refs_2_
  11.5 0.1 fusion.6.refs_3_.refs_2_
  11.6 3.7 %apart.2 = (bf16[2,3584,512]{2,1,0:T(8,128)(2,1)S(1)}, f32[8,128]{1,0:T(8,128)S(1)}) custom-call(bf16[4,28672,128]{2,1,0:T(8,128)(2,1)} %bitcast.29, bf16[64,128]{1,0:T(8,128)(2,1)S(1)} %bitcast.27, bf16[3584,256]{1,0:T(8,128)(2,1)S(1)} %bitcast.25, f32[4,128]{1,0:T(4,128)S(1)} %fusion.6.refs_3_.refs_2_, ...), custom_call_target="tpu_custom_call" | custom-call | bytes 1024 | tf_op jit(solution)/shard_map/apart/pallas_call | solution.py:74
  15.3 0.0 collective-permute-done.refs_1_
  15.4 1.8 %collective-permute-start.4 = (bf16[64,3712]{1,0:T(8,128)(2,1)S(1)}, bf16[64,3712]{1,0:T(8,128)(2,1)S(1)}, u32[]{:S(2)}, u32[]{:S(2)}) collective-permute-start(bf16[64,3712]{1,0:T(8,128)(2,1)S(1)} %join.1.refs_1_.refs_0_), channel_id=1, source_target_pairs={{0,8},{4,12},{8,0},{12,4},{1,9},{5,13},{9,1},{13,5},{2,10},{6,14},... | collective-permute-start | bytes 1425416 | tf_op jit(solution)/shard_map/ppermute | solution.py:273
  17.2 8.1 %apart.3 = (bf16[2,3584,512]{2,1,0:T(8,128)(2,1)S(1)}, bf16[2,3584,512]{2,1,0:T(8,128)(2,1)S(1)}, bf16[2,3584,512]{2,1,0:T(8,128)(2,1)S(1)}, f32[8,128]{1,0:T(8,128)S(1)}) custom-call(bf16[4,28672,128]{2,1,0:T(8,128)(2,1)} %bitcast.30, bf16[64,3712]{1,0:T(8,128)(2,1)S(1)} %join.1.refs_1_.refs_0_), custom_call_target="tpu_custom_call" | custom-call | bytes 1024 | tf_op jit(solution)/shard_map/apart/pallas_call | solution.py:74
  25.3 2.2 %collective-permute-done.4.value = bf16[64,3712]{1,0:T(8,128)(2,1)S(1)} collective-permute-done((bf16[64,3712]{1,0:T(8,128)(2,1)S(1)}, bf16[64,3712]{1,0:T(8,128)(2,1)S(1)}, u32[]{:S(2)}, u32[]{:S(2)}) %collective-permute-start.4) | collective-permute-done | bytes 475168 | tf_op jit(solution)/shard_map/ppermute | solution.py:273
  27.5 0.1 collective-permute-start.5
  27.6 1.1 %first_rows.1.refs_5_ = bf16[128,3584]{1,0:T(8,128)(2,1)S(1)} custom-call(bf16[64,3712]{1,0:T(8,128)(2,1)S(1)} %join.1.refs_1_.refs_0_, bf16[64,3712]{1,0:T(8,128)(2,1)S(1)} %collective-permute-done.3.refs_1_, bf16[256,256]{1,0:T(8,128)(2,1)S(1)} %select_convert_fusion.refs_4_.refs_2_), custom_call_target="tpu_custom_call" | custom-call | bytes 1024 | tf_op jit(solution)/shard_map/first_rows/pallas_call | solution.py:158
  28.8 0.7 collective-permute-done.5.refs_3_
  29.5 1.6 %rest_rows.1 = (bf16[256,3584]{1,0:T(8,128)(2,1)S(1)}, bf16[256,128]{1,0:T(8,128)(2,1)S(1)}, f32[256,128]{1,0:T(8,128)S(1)}) custom-call(bf16[64,3712]{1,0:T(8,128)(2,1)S(1)} %join.1.refs_1_.refs_0_, bf16[64,3712]{1,0:T(8,128)(2,1)S(1)} %collective-permute-done.3.refs_1_, bf16[64,3712]{1,0:T(8,128)(2,1)S(1)} %pass_on.1.refs_2_, ...), custom_call_target="tpu_custom_call" | custom-call | tf_op jit(solution)/shard_map/rest_rows/pallas_call | solution.py:199
  31.1 0.0 copy-start
  31.1 8.0 %hidden_rows.1.hidden = bf16[256,2048]{1,0:T(8,128)(2,1)S(1)} custom-call(bf16[256,3584]{1,0:T(8,128)(2,1)S(1)} %get-tuple-element.13.refs_0_, f32[256,128]{1,0:T(8,128)S(1)} %get-tuple-element.14.refs_1_, f32[4,128]{1,0:T(4,128)S(1)} %fusion.6.refs_3_.refs_2_, bf16[2,3584,512]{2,1,0:T(8,128)(2,1)S(1)} %get-tuple-element.15.refs_3_, ...), custom_call_target="tpu_custom_call" | custom-call | tf_op jit(solution)/shard_map/hidden_rows/pallas_call | solution.py:230
  39.0 5.2 %down_rows.2 = bf16[256,1280]{1,0:T(8,128)(2,1)S(1)} custom-call(s32[1]{0:T(128)} %bitcast.refs_5_.index, bf16[256,2048]{1,0:T(8,128)(2,1)S(1)} %hidden_rows.1.hidden, bf16[256,128]{1,0:T(8,128)(2,1)S(1)} %get-tuple-element.19.shared_hidden, bf16[2048,3584]{1,0:T(8,128)(2,1)} %bitcast.31, bf16[512,3584]{1,0:T(8,128)(2,1)S(1)} %copy-done), custom_call_target="tpu_custom_call" | custom-call | tf_op jit(solution)/shard_map/down_rows/pallas_call | solution.py:253
  44.3 0.2 collective-permute-start.6
  44.5 8.7 %down_rows.3 = bf16[256,2304]{1,0:T(8,128)(2,1)S(1)} custom-call(s32[1]{0:T(128)} %bitcast.refs_5_.index, bf16[256,2048]{1,0:T(8,128)(2,1)S(1)} %hidden_rows.1.hidden, bf16[256,128]{1,0:T(8,128)(2,1)S(1)} %get-tuple-element.19.shared_hidden, bf16[2048,3584]{1,0:T(8,128)(2,1)} %bitcast.32, bf16[512,3584]{1,0:T(8,128)(2,1)S(1)} %copy-done), custom_call_target="tpu_custom_call" | custom-call | tf_op jit(solution)/shard_map/down_rows/pallas_call | solution.py:253
  53.3 0.4 collective-permute-start.11
  53.7 0.1 convert_add_fusion.1
  53.9 3.6 %collective-permute-start.9 = (bf16[32,1280]{1,0:T(8,128)(2,1)S(1)}, bf16[32,1280]{1,0:T(8,128)(2,1)S(1)}, u32[]{:S(2)}, u32[]{:S(2)}) collective-permute-start(bf16[32,1280]{1,0:T(8,128)(2,1)S(1)} %bitcast.39), channel_id=1, source_target_pairs={{0,3},{1,2},{2,1},{3,0},{4,7},{5,6},{6,5},{7,4},{8,11},{9,10},{10,... | collective-permute-start | bytes 245768 | tf_op jit(solution)/shard_map/ppermute | solution.py:273
  57.5 0.5 collective-permute-start.7
  58.0 0.3 collective-permute-start.8
  58.4 0.1 convert_add_fusion
  58.5 0.0 copy-start.2
  58.5 1.6 %collective-permute-start.12 = (bf16[64,2304]{1,0:T(8,128)(2,1)S(1)}, bf16[64,2304]{1,0:T(8,128)(2,1)S(1)}, u32[]{:S(2)}, u32[]{:S(2)}) collective-permute-start(bf16[64,2304]{1,0:T(8,128)(2,1)S(1)} %slice.119), channel_id=1, source_target_pairs={{0,8},{4,12},{8,0},{12,4},{1,9},{5,13},{9,1},{13,5},{2,10},{6,14},... | collective-permute-start | bytes 884744 | tf_op jit(solution)/shard_map/ppermute | solution.py:273
  60.1 0.8 %collective-permute-done.9 = bf16[32,1280]{1,0:T(8,128)(2,1)S(1)} collective-permute-done((bf16[32,1280]{1,0:T(8,128)(2,1)S(1)}, bf16[32,1280]{1,0:T(8,128)(2,1)S(1)}, u32[]{:S(2)}, u32[]{:S(2)}) %collective-permute-start.9) | collective-permute-done | bytes 81952 | tf_op jit(solution)/shard_map/ppermute | solution.py:273
  60.9 1.5 %collective-permute-done.7 = bf16[32,1280]{1,0:T(8,128)(2,1)S(1)} collective-permute-done((bf16[32,1280]{1,0:T(8,128)(2,1)S(1)}, bf16[32,1280]{1,0:T(8,128)(2,1)S(1)}, u32[]{:S(2)}, u32[]{:S(2)}) %collective-permute-start.7) | collective-permute-done | bytes 81952 | tf_op jit(solution)/shard_map/ppermute | solution.py:273
  62.4 3.1 %collective-permute-done.8 = bf16[32,1280]{1,0:T(8,128)(2,1)S(1)} collective-permute-done((bf16[32,1280]{1,0:T(8,128)(2,1)S(1)}, bf16[32,1280]{1,0:T(8,128)(2,1)S(1)}, u32[]{:S(2)}, u32[]{:S(2)}) %collective-permute-start.8) | collective-permute-done | bytes 81952 | tf_op jit(solution)/shard_map/ppermute | solution.py:273
  65.5 0.0 copy-start.3
  65.5 1.6 %collective-permute-start.10 = (bf16[16,1280]{1,0:T(8,128)(2,1)S(1)}, bf16[16,1280]{1,0:T(8,128)(2,1)S(1)}, u32[]{:S(2)}, u32[]{:S(2)}) collective-permute-start(bf16[16,1280]{1,0:T(8,128)(2,1)S(1)} %slice.120), channel_id=1, source_target_pairs={{0,8},{4,12},{8,0},{12,4},{1,9},{5,13},{9,1},{13,5},{2,10},{6,14},... | collective-permute-start | bytes 122888 | tf_op jit(solution)/shard_map/ppermute | solution.py:273
  67.1 0.1 fusion.10
  67.2 1.7 %collective-permute-start.13 = (bf16[16,2304]{1,0:T(8,128)(2,1)S(1)}, bf16[16,2304]{1,0:T(8,128)(2,1)S(1)}, u32[]{:S(2)}, u32[]{:S(2)}) collective-permute-start(bf16[16,2304]{1,0:T(8,128)(2,1)S(1)} %get-tuple-element.29), channel_id=1, source_target_pairs={{0,1},{1,0},{2,3},{3,2},{4,5},{5,4},{6,7},{7,6},{8,9},{9,8},{10,11... | collective-permute-start | bytes 221192 | tf_op jit(solution)/shard_map/ppermute | solution.py:273
  68.9 2.6 %collective-permute-start.15 = (bf16[16,2304]{1,0:T(8,128)(2,1)S(1)}, bf16[16,2304]{1,0:T(8,128)(2,1)S(1)}, u32[]{:S(2)}, u32[]{:S(2)}) collective-permute-start(bf16[16,2304]{1,0:T(8,128)(2,1)S(1)} %get-tuple-element.30), channel_id=1, source_target_pairs={{0,3},{1,2},{2,1},{3,0},{4,7},{5,6},{6,5},{7,4},{8,11},{9,10},{10,... | collective-permute-start | bytes 221192 | tf_op jit(solution)/shard_map/ppermute | solution.py:273
  71.5 1.1 %collective-permute-done.13 = bf16[16,2304]{1,0:T(8,128)(2,1)S(1)} collective-permute-done((bf16[16,2304]{1,0:T(8,128)(2,1)S(1)}, bf16[16,2304]{1,0:T(8,128)(2,1)S(1)}, u32[]{:S(2)}, u32[]{:S(2)}) %collective-permute-start.13) | collective-permute-done | bytes 73760 | tf_op jit(solution)/shard_map/ppermute | solution.py:273
  72.6 2.5 %collective-permute-done.15 = bf16[16,2304]{1,0:T(8,128)(2,1)S(1)} collective-permute-done((bf16[16,2304]{1,0:T(8,128)(2,1)S(1)}, bf16[16,2304]{1,0:T(8,128)(2,1)S(1)}, u32[]{:S(2)}, u32[]{:S(2)}) %collective-permute-start.15) | collective-permute-done | bytes 73760 | tf_op jit(solution)/shard_map/ppermute | solution.py:273
  75.2 2.0 %collective-permute-done.14 = bf16[16,2304]{1,0:T(8,128)(2,1)S(1)} collective-permute-done((bf16[16,2304]{1,0:T(8,128)(2,1)S(1)}, bf16[16,2304]{1,0:T(8,128)(2,1)S(1)}, u32[]{:S(2)}, u32[]{:S(2)}) %collective-permute-start.14) | collective-permute-done | bytes 73760 | tf_op jit(solution)/shard_map/ppermute | solution.py:273
  77.2 0.7 fusion.2
  77.9 0.2 multiply_reduce_fusion
  78.0 0.1 div.28
  78.1 0.2 subtract_reduce_fusion
  78.3 0.5 convert_multiply_fusion
  (37 shorter events, 0.4 us)
Async XLA Ops:
  0.6 14.7 %collective-permute-start.1 = (bf16[16,3584]{1,0:T(8,128)(2,1)}, bf16[16,3584]{1,0:T(8,128)(2,1)S(1)}, u32[]{:S(2)}, u32[]{:S(2)}) collective-permute-start(bf16[16,3584]{1,0:T(8,128)(2,1)} %refs_0_.1), channel_id=1, source_target_pairs={{0,2},{1,3},{2,0},{3,1},{4,6},{5,7},{6,4},{7,5},{8,10},{9,11},{10,... | collective-permute-start | bytes 344072 | tf_op jit(solution)/shard_map/ppermute | solution.py:273
  4.7 10.6 %collective-permute-start = (bf16[16,3584]{1,0:T(8,128)(2,1)}, bf16[16,3584]{1,0:T(8,128)(2,1)S(1)}, u32[]{:S(2)}, u32[]{:S(2)}) collective-permute-start(bf16[16,3584]{1,0:T(8,128)(2,1)} %refs_0_.1), channel_id=1, source_target_pairs={{0,1},{1,0},{2,3},{3,2},{4,5},{5,4},{6,7},{7,6},{8,9},{9,8},{10,11... | collective-permute-start | bytes 344072 | tf_op jit(solution)/shard_map/ppermute | solution.py:273
  6.3 9.0 %collective-permute-start.2 = (bf16[16,3584]{1,0:T(8,128)(2,1)}, bf16[16,3584]{1,0:T(8,128)(2,1)S(1)}, u32[]{:S(2)}, u32[]{:S(2)}) collective-permute-start(bf16[16,3584]{1,0:T(8,128)(2,1)} %refs_0_.1), channel_id=1, source_target_pairs={{0,3},{1,2},{2,1},{3,0},{4,7},{5,6},{6,5},{7,4},{8,11},{9,10},{10,... | collective-permute-start | bytes 344072 | tf_op jit(solution)/shard_map/ppermute | solution.py:273
  11.6 3.7 %copy-start.1 = (bf16[16,3584]{1,0:T(8,128)(2,1)S(1)}, bf16[16,3584]{1,0:T(8,128)(2,1)}, u32[]{:S(2)}) copy-start(bf16[16,3584]{1,0:T(8,128)(2,1)} %refs_0_.1) | copy-start | bytes 344068
  15.4 12.1 %collective-permute-start.4 = (bf16[64,3712]{1,0:T(8,128)(2,1)S(1)}, bf16[64,3712]{1,0:T(8,128)(2,1)S(1)}, u32[]{:S(2)}, u32[]{:S(2)}) collective-permute-start(bf16[64,3712]{1,0:T(8,128)(2,1)S(1)} %join.1.refs_1_.refs_0_), channel_id=1, source_target_pairs={{0,8},{4,12},{8,0},{12,4},{1,9},{5,13},{9,1},{13,5},{2,10},{6,14},... | collective-permute-start | bytes 1425416 | tf_op jit(solution)/shard_map/ppermute | solution.py:273
  17.2 10.5 %collective-permute-start.3 = (bf16[64,3712]{1,0:T(8,128)(2,1)S(1)}, bf16[64,3712]{1,0:T(8,128)(2,1)S(1)}, u32[]{:S(2)}, u32[]{:S(2)}) collective-permute-start(bf16[64,3712]{1,0:T(8,128)(2,1)S(1)} %join.1.refs_1_.refs_0_), channel_id=1, source_target_pairs={{0,4},{4,0},{8,12},{12,8},{1,5},{5,1},{9,13},{13,9},{2,6},{6,2},{1... | collective-permute-start | bytes 1425416 | tf_op jit(solution)/shard_map/ppermute | solution.py:273
  27.5 1.9 %collective-permute-start.5 = (bf16[64,3712]{1,0:T(8,128)(2,1)S(1)}, bf16[64,3712]{1,0:T(8,128)(2,1)S(1)}, u32[]{:S(2)}, u32[]{:S(2)}) collective-permute-start(bf16[64,3712]{1,0:T(8,128)(2,1)S(1)} %pass_on.1.refs_2_), channel_id=1, source_target_pairs={{0,4},{4,0},{8,12},{12,8},{1,5},{5,1},{9,13},{13,9},{2,6},{6,2},{1... | collective-permute-start | bytes 1425416 | tf_op jit(solution)/shard_map/ppermute | solution.py:273
  31.1 8.0 %copy-start = (bf16[512,3584]{1,0:T(8,128)(2,1)S(1)}, bf16[512,3584]{1,0:T(8,128)(2,1)}, u32[]{:S(2)}) copy-start(bf16[512,3584]{1,0:T(8,128)(2,1)} %shared_down.3) | copy-start | bytes 11010052
  44.3 9.4 %collective-permute-start.6 = (bf16[128,1280]{1,0:T(8,128)(2,1)S(1)}, bf16[128,1280]{1,0:T(8,128)(2,1)S(1)}, u32[]{:S(2)}, u32[]{:S(2)}) collective-permute-start(bf16[128,1280]{1,0:T(8,128)(2,1)S(1)} %slice.91), channel_id=1, source_target_pairs={{0,4},{4,0},{8,12},{12,8},{1,5},{5,1},{9,13},{13,9},{2,6},{6,2},{1... | collective-permute-start | bytes 983048 | tf_op jit(solution)/shard_map/ppermute | solution.py:273
  53.3 5.1 %collective-permute-start.11 = (bf16[128,2304]{1,0:T(8,128)(2,1)S(1)}, bf16[128,2304]{1,0:T(8,128)(2,1)S(1)}, u32[]{:S(2)}, u32[]{:S(2)}) collective-permute-start(bf16[128,2304]{1,0:T(8,128)(2,1)S(1)} %slice.99), channel_id=1, source_target_pairs={{0,4},{4,0},{8,12},{12,8},{1,5},{5,1},{9,13},{13,9},{2,6},{6,2},{1... | collective-permute-start | bytes 1769480 | tf_op jit(solution)/shard_map/ppermute | solution.py:273
  53.9 7.0 %collective-permute-start.9 = (bf16[32,1280]{1,0:T(8,128)(2,1)S(1)}, bf16[32,1280]{1,0:T(8,128)(2,1)S(1)}, u32[]{:S(2)}, u32[]{:S(2)}) collective-permute-start(bf16[32,1280]{1,0:T(8,128)(2,1)S(1)} %bitcast.39), channel_id=1, source_target_pairs={{0,3},{1,2},{2,1},{3,0},{4,7},{5,6},{6,5},{7,4},{8,11},{9,10},{10,... | collective-permute-start | bytes 245768 | tf_op jit(solution)/shard_map/ppermute | solution.py:273
  57.5 4.9 %collective-permute-start.7 = (bf16[32,1280]{1,0:T(8,128)(2,1)S(1)}, bf16[32,1280]{1,0:T(8,128)(2,1)S(1)}, u32[]{:S(2)}, u32[]{:S(2)}) collective-permute-start(bf16[32,1280]{1,0:T(8,128)(2,1)S(1)} %bitcast.38), channel_id=1, source_target_pairs={{0,1},{1,0},{2,3},{3,2},{4,5},{5,4},{6,7},{7,6},{8,9},{9,8},{10,11... | collective-permute-start | bytes 245768 | tf_op jit(solution)/shard_map/ppermute | solution.py:273
  58.0 7.4 %collective-permute-start.8 = (bf16[32,1280]{1,0:T(8,128)(2,1)S(1)}, bf16[32,1280]{1,0:T(8,128)(2,1)S(1)}, u32[]{:S(2)}, u32[]{:S(2)}) collective-permute-start(bf16[32,1280]{1,0:T(8,128)(2,1)S(1)} %bitcast.37), channel_id=1, source_target_pairs={{0,2},{1,3},{2,0},{3,1},{4,6},{5,7},{6,4},{7,5},{8,10},{9,11},{10,... | collective-permute-start | bytes 245768 | tf_op jit(solution)/shard_map/ppermute | solution.py:273
  58.5 19.3 %copy-start.2 = (f32[3584]{0:T(1024)S(1)}, f32[3584]{0:T(1024)}, u32[]{:S(2)}) copy-start(f32[3584]{0:T(1024)} %param.17) | copy-start | bytes 43012
  58.5 8.6 %collective-permute-start.12 = (bf16[64,2304]{1,0:T(8,128)(2,1)S(1)}, bf16[64,2304]{1,0:T(8,128)(2,1)S(1)}, u32[]{:S(2)}, u32[]{:S(2)}) collective-permute-start(bf16[64,2304]{1,0:T(8,128)(2,1)S(1)} %slice.119), channel_id=1, source_target_pairs={{0,8},{4,12},{8,0},{12,4},{1,9},{5,13},{9,1},{13,5},{2,10},{6,14},... | collective-permute-start | bytes 884744 | tf_op jit(solution)/shard_map/ppermute | solution.py:273
  65.5 12.8 %copy-start.3 = (s32[8]{0:T(128)S(1)}, s32[8]{0:T(128)}, u32[]{:S(2)}) copy-start(s32[8]{0:T(128)} %param.12) | copy-start | bytes 100
  65.5 5.9 %collective-permute-start.10 = (bf16[16,1280]{1,0:T(8,128)(2,1)S(1)}, bf16[16,1280]{1,0:T(8,128)(2,1)S(1)}, u32[]{:S(2)}, u32[]{:S(2)}) collective-permute-start(bf16[16,1280]{1,0:T(8,128)(2,1)S(1)} %slice.120), channel_id=1, source_target_pairs={{0,8},{4,12},{8,0},{12,4},{1,9},{5,13},{9,1},{13,5},{2,10},{6,14},... | collective-permute-start | bytes 122888 | tf_op jit(solution)/shard_map/ppermute | solution.py:273
  67.2 5.4 %collective-permute-start.13 = (bf16[16,2304]{1,0:T(8,128)(2,1)S(1)}, bf16[16,2304]{1,0:T(8,128)(2,1)S(1)}, u32[]{:S(2)}, u32[]{:S(2)}) collective-permute-start(bf16[16,2304]{1,0:T(8,128)(2,1)S(1)} %get-tuple-element.29), channel_id=1, source_target_pairs={{0,1},{1,0},{2,3},{3,2},{4,5},{5,4},{6,7},{7,6},{8,9},{9,8},{10,11... | collective-permute-start | bytes 221192 | tf_op jit(solution)/shard_map/ppermute | solution.py:273
  68.9 6.3 %collective-permute-start.15 = (bf16[16,2304]{1,0:T(8,128)(2,1)S(1)}, bf16[16,2304]{1,0:T(8,128)(2,1)S(1)}, u32[]{:S(2)}, u32[]{:S(2)}) collective-permute-start(bf16[16,2304]{1,0:T(8,128)(2,1)S(1)} %get-tuple-element.30), channel_id=1, source_target_pairs={{0,3},{1,2},{2,1},{3,0},{4,7},{5,6},{6,5},{7,4},{8,11},{9,10},{10,... | collective-permute-start | bytes 221192 | tf_op jit(solution)/shard_map/ppermute | solution.py:273
  71.5 5.7 %collective-permute-start.14 = (bf16[16,2304]{1,0:T(8,128)(2,1)S(1)}, bf16[16,2304]{1,0:T(8,128)(2,1)S(1)}, u32[]{:S(2)}, u32[]{:S(2)}) collective-permute-start(bf16[16,2304]{1,0:T(8,128)(2,1)S(1)} %get-tuple-element.31), channel_id=1, source_target_pairs={{0,2},{1,3},{2,0},{3,1},{4,6},{5,7},{6,4},{7,5},{8,10},{9,11},{10,... | collective-permute-start | bytes 221192 | tf_op jit(solution)/shard_map/ppermute | solution.py:273

commit v4 on v3

--- a/solution.py
+++ b/solution.py
@@ -12,7 +12,6 @@
 CORES = 2
 SMALL_VMEM = 10 * 1024 * 1024
 HIDDEN_VMEM = 5 * 1024 * 1024
-VMEM_BYTES = 16 * 1024 * 1024
 
 
 def sign_matrix(copies):
@@ -168,8 +167,13 @@
 
 def rest_kernel(n_first, n_chips, *refs):
     n_pieces = CORES * n_chips
-    pieces = refs[:n_pieces]
-    signs, first, shared, deq, shared_hidden, combine, rows_s = refs[n_pieces:]
+    index, pieces = refs[0], refs[1 : 1 + n_pieces]
+    signs, first, shared, shared_down, *outs, rows_s, sem = refs[1 + n_pieces :]
+    deq, shared_hidden, combine, shared_out = outs
+    own = shared_out.shape[0]
+    own = pl.ds(pl.multiple_of(index[0] * own, own), own)
+    copy = pltpu.make_async_copy(shared_down.at[own], shared_out, sem)
+    copy.start()
     count = pieces[0].shape[0]
     feature_len = deq.shape[1]
     sources, bases = [], []
@@ -190,83 +194,112 @@
     both = jnp.dot(rows_s[...], shared[...], preferred_element_type=jnp.float32)
     gate, up = both[:, :part], both[:, part:]
     shared_hidden[...] = (gate / (1.0 + jnp.exp(-gate)) * up).astype(jnp.bfloat16)
-
-
-def rest_rows(pieces, signs, first, shared, n_chips):
+    copy.wait()
+
+
+def rest_rows(index, pieces, signs, first, shared, shared_down, n_chips):
     whole = pl.BlockSpec(memory_space=pltpu.VMEM)
     rows = sum(piece.shape[0] for piece in pieces)
     feature_len = first.shape[1]
     return pl.pallas_call(
         functools.partial(rest_kernel, len(pieces), n_chips),
-        in_specs=[whole] * (len(pieces) + 3),
-        out_specs=[whole] * 3,
+        in_specs=[pl.BlockSpec(memory_space=pltpu.SMEM)]
+        + [whole] * (len(pieces) + 3)
+        + [pl.BlockSpec(memory_space=pl.ANY)],
+        out_specs=[whole] * 4,
         out_shape=[
             vmem((rows, feature_len), jnp.bfloat16),
             vmem((rows, shared.shape[1] // 2), jnp.bfloat16),
             vmem((rows, pieces[0].shape[1] - feature_len), jnp.float32),
+            vmem((shared.shape[1] // 2, feature_len), shared_down.dtype),
         ],
-        scratch_shapes=[pltpu.VMEM((rows, feature_len), jnp.bfloat16)],
+        scratch_shapes=[
+            pltpu.VMEM((rows, feature_len), jnp.bfloat16),
+            pltpu.SemaphoreType.DMA(()),
+        ],
         compiler_params=pltpu.CompilerParams(vmem_limit_bytes=HIDDEN_VMEM + 2 * rows * feature_len),
         name="rest_rows",
-    )(*pieces, signs, first, shared)
-
-
-def hidden_kernel(n_local, *refs):
-    deq, combine, select = refs[:3]
-    weights, out = refs[3 : 3 + n_local], refs[3 + n_local]
-    inner = out.shape[1] // n_local
-    for local in range(n_local):
-        gate = jnp.dot(deq[...], weights[local][0], preferred_element_type=jnp.float32)
-        up = jnp.dot(deq[...], weights[local][1], preferred_element_type=jnp.float32)
+    )(index, *pieces, signs, first, shared, shared_down)
+
+
+def hidden_kernel(experts, *refs):
+    n = len(experts)
+    deq, combine, select, down = refs[:4]
+    weights, out = refs[4 : 4 + n], refs[4 + n]
+    down_out, sems = refs[5 + n : 5 + 2 * n], refs[5 + 2 * n]
+    inner = out.shape[1] // n
+    copies = [
+        pltpu.make_async_copy(down.at[local], down_out[at], sems.at[at])
+        for at, local in enumerate(experts)
+    ]
+    for copy in copies:
+        copy.start()
+    for at, local in enumerate(experts):
+        gate = jnp.dot(deq[...], weights[at][0], preferred_element_type=jnp.float32)
+        up = jnp.dot(deq[...], weights[at][1], preferred_element_type=jnp.float32)
         weight = jnp.sum(combine[...] * select[local : local + 1, :], axis=1, keepdims=True)
-        out[:, local * inner : (local + 1) * inner] = (
+        out[:, at * inner : (at + 1) * inner] = (
             gate / (1.0 + jnp.exp(-gate)) * up * weight
         ).astype(jnp.bfloat16)
-
-
-def hidden_rows(deq, combine, select, weights):
+    for copy in copies:
+        copy.wait()
+
+
+def hidden_rows(deq, combine, select, down, experts, weights):
     whole = pl.BlockSpec(memory_space=pltpu.VMEM)
     rows = deq.shape[0]
-    return pl.pallas_call(
-        functools.partial(hidden_kernel, len(weights)),
-        in_specs=[whole] * (3 + len(weights)),
-        out_specs=whole,
-        out_shape=vmem((rows, len(weights) * weights[0].shape[2]), jnp.bfloat16),
+    n = len(experts)
+    out = pl.pallas_call(
+        functools.partial(hidden_kernel, experts),
+        in_specs=[whole] * 3 + [pl.BlockSpec(memory_space=pl.ANY)] + [whole] * n,
+        out_specs=[whole] * (1 + n),
+        out_shape=[
+            vmem((rows, n * weights[0].shape[2]), jnp.bfloat16),
+            *[vmem(down.shape[1:], down.dtype)] * n,
+        ],
+        scratch_shapes=[pltpu.SemaphoreType.DMA((n,))],
         compiler_params=pltpu.CompilerParams(vmem_limit_bytes=HIDDEN_VMEM),
         name="hidden_rows",
-    )(deq, combine, select, *weights)
-
-
-def down_kernel(index, hidden, shared_hidden, down, shared_down, out):
-    out[...] = (
-        jnp.dot(hidden[...], down[...], preferred_element_type=jnp.float32)
-        + jnp.dot(shared_hidden[...], shared_down[...], preferred_element_type=jnp.float32)
-    ).astype(out.dtype)
-
-
-def down_rows(index, hidden, shared_hidden, down, shared_down, start, stop):
-    rows = hidden.shape[0]
-    inner = down.shape[0]
-    tile = math.gcd(512, math.gcd(start, stop - start))
-    first = start // tile
+    )(deq, combine, select, down, *weights)
+    return out[0], list(out[1:])
+
+
+def down_kernel(start, tile, n_hidden, *refs):
+    hidden, (shared_hidden, shared_down), downs = (
+        refs[:n_hidden],
+        refs[n_hidden : n_hidden + 2],
+        refs[n_hidden + 2 : -1],
+    )
+    out = refs[-1]
+    inner = downs[0].shape[0]
+    per = hidden[0].shape[1] // inner
+    for at in range(0, out.shape[1], tile):
+        columns = slice(start + at, start + at + tile)
+        total = jnp.dot(
+            shared_hidden[...], shared_down[:, columns], preferred_element_type=jnp.float32
+        )
+        for local, down in enumerate(downs):
+            units = slice(local % per * inner, (local % per + 1) * inner)
+            total += jnp.dot(
+                hidden[local // per][:, units],
+                down[:, columns],
+                preferred_element_type=jnp.float32,
+            )
+        out[:, at : at + tile] = total.astype(out.dtype)
+
+
+def down_rows(hidden, shared_hidden, downs, shared_down, start, stop):
+    rows = shared_hidden.shape[0]
+    tile = math.gcd(256, math.gcd(start, stop - start))
     whole = pl.BlockSpec(memory_space=pltpu.VMEM)
     return pl.pallas_call(
-        down_kernel,
-        grid_spec=pltpu.PrefetchScalarGridSpec(
-            num_scalar_prefetch=1,
-            grid=((stop - start) // tile,),
-            in_specs=[
-                whole,
-                whole,
-                pl.BlockSpec((inner, tile), lambda s, at: (0, first + s)),
-                pl.BlockSpec((shared_hidden.shape[1], tile), lambda s, at: (at[0], first + s)),
-            ],
-            out_specs=pl.BlockSpec((rows, tile), lambda s, at: (0, s)),
-        ),
-        out_shape=jax.ShapeDtypeStruct((rows, stop - start), jnp.bfloat16),
-        compiler_params=pltpu.CompilerParams(vmem_limit_bytes=VMEM_BYTES),
+        functools.partial(down_kernel, start, tile, len(hidden)),
+        in_specs=[whole] * (2 + len(hidden) + len(downs)),
+        out_specs=whole,
+        out_shape=vmem((rows, stop - start), jnp.bfloat16),
+        compiler_params=pltpu.CompilerParams(vmem_limit_bytes=HIDDEN_VMEM),
         name="down_rows",
-    )(index, hidden, shared_hidden, down, shared_down)
+    )(*hidden, shared_hidden, shared_down, *downs)
 
 
 def exchange(value, axis, flip):
@@ -342,41 +375,44 @@
     from_both = [exchange(part, "expert", 1) for part in from_x]
     first = first_rows([along_z, near], signs, feature_len)
 
-    deq, shared_hidden, combine = rest_rows(
-        [along_z, near] + from_x + from_both, signs, first, shared_in, chips
-    )
-    down = pltpu.with_memory_space_constraint(
-        expert_down.reshape(n_local * inner, feature_len), pltpu.HBM
-    )
-    hidden = hidden_rows(deq, combine, select, weights)
+    shared_out = pltpu.with_memory_space_constraint(shared_out, pltpu.HBM)
+    deq, shared_hidden, combine, shared_out = rest_rows(
+        index, [along_z, near] + from_x + from_both, signs, first, shared_in, shared_out, chips
+    )
+    down = pltpu.with_memory_space_constraint(expert_down, pltpu.HBM)
+    hidden, downs = [], []
+    for at in range(0, n_local, 2):
+        part, down_part = hidden_rows(
+            deq, combine, select, down, list(range(n_local))[at : at + 2], weights[at : at + 2]
+        )
+        hidden.append(part)
+        downs += down_part
 
     half = own_rows * narrow_count * chips
-    cut = feature_len * 5 // 14 // 256 * 256
+    cut = feature_len // 256 // 2 * 256
 
     def by_core(start, stop):
-        part = down_rows(index, hidden, shared_hidden, down, shared_out, start, stop)
+        part = down_rows(hidden, shared_hidden, downs, shared_out, start, stop)
         near = exchange(part[half:], "expert", 1)
         total = part[:half].astype(jnp.float32) + near.astype(jnp.float32)
         return total.reshape(chips, narrow_count, own_rows, stop - start)
 
+    def halve(parts, axis, step):
+        pairs = parts.reshape(parts.shape[0] // 2, 2, *parts.shape[1:])
+        got = exchange(pairs[:, 1].astype(jnp.bfloat16), axis, step)
+        return pairs[:, 0] + got.astype(jnp.float32)
+
     def add_up(parts, axis, step):
-        total = parts[0]
-        for flip in range(1, len(parts)):
-            part = exchange(parts[flip].astype(jnp.bfloat16), axis, flip * step)
-            total = total + part.astype(jnp.float32)
-        return total
+        while parts.shape[0] > 1:
+            parts, step = halve(parts, axis, step), 2 * step
+        return parts[0]
 
     totals = []
     if cut:
-        parts = by_core(0, cut)
-        parts = add_up(
-            [parts[:, n].reshape(chips * own_rows, cut) for n in range(narrow_count)], "narrow", 1
-        ).reshape(chips, own_rows, cut)
-        totals.append(add_up([parts[c] for c in range(chips)], "expert", CORES))
-    parts = by_core(cut, feature_len).reshape(chips, narrow_count * own_rows, feature_len - cut)
-    parts = add_up([parts[c] for c in range(chips)], "expert", CORES)
-    parts = parts.reshape(narrow_count, own_rows, feature_len - cut)
-    totals.append(add_up([parts[n] for n in range(narrow_count)], "narrow", 1))
+        parts = halve(jnp.swapaxes(by_core(0, cut), 0, 1), "narrow", 1)
+        parts = add_up(jnp.swapaxes(parts, 0, 1), "expert", CORES)
+        totals.append(add_up(parts, "narrow", 2))
+    totals.append(add_up(add_up(by_core(cut, feature_len), "expert", CORES), "narrow", 1))
     total_sum = jnp.concatenate(totals, axis=1)
     mixed = total_sum.astype(jnp.bfloat16)
     row_score = jnp.sum(total_sum * readout[None, :], axis=1) / jnp.sqrt(

time: 79.3 us -> 69 us (0.87)
  Pallas kernels: 36.5 us -> 27.7 us
  waiting for transfers between devices: 13.9 us -> 12.7 us
    pallas_call x3 -> x4, Pallas kernels: 21.9 us -> 12.8 us  [the longest x2 8.18 us: hidden_rows(): pl.pallas_call(functools.partial(hidden_kernel, experts), in_specs=[whole...]
    ppermute x16 -> x14, waiting for transfers between devices: 13.9 us -> 12.7 us  [exchange(): lax.ppermute(value, axis, [(i, i ^ flip) for i in range(lax.axis_size(axi...]
    ppermute x16 -> x14, starting transfers between devices: 20 us -> 20 us  [exchange(): lax.ppermute(value, axis, [(i, i ^ flip) for i in range(lax.axis_size(axi...]
  transfers between devices with their start and end apart: 16 -> 14, of which waited for: 8 -> 6; matrix products, arithmetic and copies ran while one was open for 7% -> 8% of each run, Pallas kernels for 28% -> 22%
where the time goes in v4:
time: 69 us; the launch traced here: 68.7 us
  Pallas kernels  27.7 us (40%)
  starting transfers between devices  20 us (29%)
  waiting for transfers between devices  12.7 us (18%)
  local copies, waits for them, and re-layouts  4.26 us (6%)
  other arithmetic  3.14 us (5%)
  between operations  0.97 us (1%)
    ppermute x14, starting transfers between devices, exchange(): lax.ppermute(value, axis, [(i, i ^ flip) for i in range(lax.axis_size(axi...  20 us
    ppermute x14, waiting for transfers between devices, exchange(): lax.ppermute(value, axis, [(i, i ^ flip) for i in range(lax.axis_size(axi...  12.7 us
    pallas_call x2, Pallas kernels, apart(): pl.pallas_call(functools.partial(apart_kernel, experts, rows, chunk, len(...  11.8 us
    pallas_call x2, Pallas kernels, hidden_rows(): pl.pallas_call(functools.partial(hidden_kernel, experts), in_specs=[whole...  8.18 us
    pallas_call x2, Pallas kernels, down_rows(): pl.pallas_call(functools.partial(down_kernel, start, tile, len(hidden)),...  4.58 us
    dynamic_slice x1, local copies, waits for them, and re-layouts, per_device(): lax.dynamic_slice_in_dim(shared_gate_up, expert_at * part_len, part_len, 2)  3.07 us
    pallas_call x1, Pallas kernels, rest_rows(): pl.pallas_call(functools.partial(rest_kernel, len(pieces), n_chips), in_s...  1.9 us
  transfers between devices with their start and end apart: 14, of which 6 were waited for; matrix products, arithmetic and copies ran while one was open for 8% of the time, Pallas kernels for 22%

profile of v4, /device:TPU:0, one launch (start us, length us, event | category | flops | bytes accessed | tf_op | source)
XLA Modules:
  0.0 68.7 jit_solution(3122111999259732194)
XLA Ops:
  0.6 4.1 %collective-permute-start.1 = (bf16[16,3584]{1,0:T(8,128)(2,1)}, bf16[16,3584]{1,0:T(8,128)(2,1)S(1)}, u32[]{:S(2)}, u32[]{:S(2)}) collective-permute-start(bf16[16,3584]{1,0:T(8,128)(2,1)} %refs_0_.1), channel_id=1, source_target_pairs={{0,2},{1,3},{2,0},{3,1},{4,6},{5,7},{6,4},{7,5},{8,10},{9,11},{10,... | collective-permute-start | bytes 344072 | tf_op jit(solution)/shard_map/ppermute | solution.py:306
  4.7 1.6 %collective-permute-start = (bf16[16,3584]{1,0:T(8,128)(2,1)}, bf16[16,3584]{1,0:T(8,128)(2,1)S(1)}, u32[]{:S(2)}, u32[]{:S(2)}) collective-permute-start(bf16[16,3584]{1,0:T(8,128)(2,1)} %refs_0_.1), channel_id=1, source_target_pairs={{0,1},{1,0},{2,3},{3,2},{4,5},{5,4},{6,7},{7,6},{8,9},{9,8},{10,11... | collective-permute-start | bytes 344072 | tf_op jit(solution)/shard_map/ppermute | solution.py:306
  6.3 0.0 collective-permute-start.2
  6.4 0.7 %select_reduce_fusion = f32[64,16]{0,1:T(8,128)S(1)} fusion(f32[64,8]{0,1:T(8,128)} %param.11, s32[64,8]{0,1:T(8,128)} %param.10), kind=kLoop, calls=%fused_computation.36 | loop fusion | flops 23552 | bytes 8192 | tf_op jit(solution)/shard_map/reduce_sum | solution.py:330
  7.1 0.1 copy.28
  7.2 3.1 %constant_dynamic-slice_fusion = bf16[3584,2,128]{2,1,0:T(2,128)(2,1)S(1)} fusion(bf16[3584,2,512]{2,1,0:T(2,128)(2,1)} %param.13, s32[]{:T(128)S(6)} %select_n.62), kind=kLoop, calls=%fused_computation.62 | loop fusion | bytes 3670020 | tf_op jit(solution)/shard_map/dynamic_slice | solution.py:347
  10.3 0.2 copy.55
  10.5 0.1 pad_maximum_fusion.1
  10.6 0.6 gather_fusion
  11.2 0.3 select_convert_fusion.refs_4_.refs_2_.refs_5_
  11.5 0.1 fusion.18.refs_3_.refs_2_
  11.6 3.7 %apart.2 = (bf16[2,3584,512]{2,1,0:T(8,128)(2,1)S(1)}, f32[8,128]{1,0:T(8,128)S(1)}) custom-call(bf16[4,28672,128]{2,1,0:T(8,128)(2,1)} %bitcast.82, bf16[64,128]{1,0:T(8,128)(2,1)S(1)} %bitcast.80, bf16[3584,256]{1,0:T(8,128)(2,1)S(1)} %bitcast.78, f32[4,128]{1,0:T(4,128)S(1)} %fusion.18.refs_3_.refs_2_, ...), custom_call_target="tpu_custom_call" | custom-call | bytes 1024 | tf_op jit(solution)/shard_map/apart/pallas_call | solution.py:73
  15.3 0.0 collective-permute-done.2.refs_3_
  15.4 1.8 %collective-permute-start.4 = (bf16[64,3712]{1,0:T(8,128)(2,1)S(1)}, bf16[64,3712]{1,0:T(8,128)(2,1)S(1)}, u32[]{:S(2)}, u32[]{:S(2)}) collective-permute-start(bf16[64,3712]{1,0:T(8,128)(2,1)S(1)} %join.1.refs_1_.refs_0_), channel_id=1, source_target_pairs={{0,8},{4,12},{8,0},{12,4},{1,9},{5,13},{9,1},{13,5},{2,10},{6,14},... | collective-permute-start | bytes 1425416 | tf_op jit(solution)/shard_map/ppermute | solution.py:306
  17.2 0.0 collective-permute-start.3
  17.2 8.1 %apart.3 = (bf16[2,3584,512]{2,1,0:T(8,128)(2,1)S(1)}, bf16[2,3584,512]{2,1,0:T(8,128)(2,1)S(1)}, bf16[2,3584,512]{2,1,0:T(8,128)(2,1)S(1)}, f32[8,128]{1,0:T(8,128)S(1)}) custom-call(bf16[4,28672,128]{2,1,0:T(8,128)(2,1)} %bitcast.83, bf16[64,3712]{1,0:T(8,128)(2,1)S(1)} %join.1.refs_1_.refs_0_), custom_call_target="tpu_custom_call" | custom-call | bytes 1024 | tf_op jit(solution)/shard_map/apart/pallas_call | solution.py:73
  25.3 2.2 %collective-permute-done.4.value = bf16[64,3712]{1,0:T(8,128)(2,1)S(1)} collective-permute-done((bf16[64,3712]{1,0:T(8,128)(2,1)S(1)}, bf16[64,3712]{1,0:T(8,128)(2,1)S(1)}, u32[]{:S(2)}, u32[]{:S(2)}) %collective-permute-start.4) | collective-permute-done | bytes 475168 | tf_op jit(solution)/shard_map/ppermute | solution.py:306
  27.5 0.1 collective-permute-start.5
  27.6 0.0 collective-permute-done.3.refs_1_.refs_2_
  27.6 1.1 %first_rows.1.refs_6_ = bf16[128,3584]{1,0:T(8,128)(2,1)S(1)} custom-call(bf16[64,3712]{1,0:T(8,128)(2,1)S(1)} %join.1.refs_1_.refs_0_, bf16[64,3712]{1,0:T(8,128)(2,1)S(1)} %collective-permute-done.3.refs_1_.refs_2_, bf16[256,256]{1,0:T(8,128)(2,1)S(1)} %select_convert_fusion.refs_4_.refs_2_.refs_5_), custom_call_target="tpu_custom_call" | custom-call | bytes 1024 | tf_op jit(solution)/shard_map/first_rows/pallas_call | solution.py:157
  28.8 0.7 %collective-permute-done.5.refs_4_ = bf16[64,3712]{1,0:T(8,128)(2,1)S(1)} collective-permute-done((bf16[64,3712]{1,0:T(8,128)(2,1)S(1)}, bf16[64,3712]{1,0:T(8,128)(2,1)S(1)}, u32[]{:S(2)}, u32[]{:S(2)}) %collective-permute-start.5) | collective-permute-done | bytes 475168 | tf_op jit(solution)/shard_map/ppermute | solution.py:306
  29.5 1.9 %rest_rows.1 = (bf16[256,3584]{1,0:T(8,128)(2,1)S(1)}, bf16[256,128]{1,0:T(8,128)(2,1)S(1)}, f32[256,128]{1,0:T(8,128)S(1)}, bf16[128,3584]{1,0:T(8,128)(2,1)S(1)}) custom-call(s32[1]{0:T(128)} %bitcast.refs_5_.refs_0_, bf16[64,3712]{1,0:T(8,128)(2,1)S(1)} %join.1.refs_1_.refs_0_, bf16[64,3712]{1,0:T(8,128)(2,1)S(1)} %collective-permute-done.3.refs_1_.refs_2_, ...), custom_call_target="tpu_custom_call" | custom-call | tf_op jit(solution)/shard_map/rest_rows/pallas_call | solution.py:204
  31.4 4.2 %hidden_rows.3 = (bf16[256,1024]{1,0:T(8,128)(2,1)S(1)}, bf16[512,3584]{1,0:T(8,128)(2,1)S(1)}, bf16[512,3584]{1,0:T(8,128)(2,1)S(1)}) custom-call(bf16[256,3584]{1,0:T(8,128)(2,1)S(1)} %get-tuple-element.20.refs_0_, f32[256,128]{1,0:T(8,128)S(1)} %get-tuple-element.21.refs_1_, f32[4,128]{1,0:T(4,128)S(1)} %fusion.18.refs_3_.refs_2_, ...), custom_call_target="tpu_custom_call" | custom-call | tf_op jit(solution)/shard_map/hidden_rows/pallas_call | solution.py:252
  35.6 4.0 %hidden_rows.2 = (bf16[256,1024]{1,0:T(8,128)(2,1)S(1)}, bf16[512,3584]{1,0:T(8,128)(2,1)S(1)}, bf16[512,3584]{1,0:T(8,128)(2,1)S(1)}) custom-call(bf16[256,3584]{1,0:T(8,128)(2,1)S(1)} %get-tuple-element.20.refs_0_, f32[256,128]{1,0:T(8,128)S(1)} %get-tuple-element.21.refs_1_, f32[4,128]{1,0:T(4,128)S(1)} %fusion.18.refs_3_.refs_2_, ...), custom_call_target="tpu_custom_call" | custom-call | tf_op jit(solution)/shard_map/hidden_rows/pallas_call | solution.py:252
  39.6 2.3 %down_rows.3 = bf16[256,1792]{1,0:T(8,128)(2,1)S(1)} custom-call(bf16[256,1024]{1,0:T(8,128)(2,1)S(1)} %get-tuple-element.24.refs_0_, bf16[256,1024]{1,0:T(8,128)(2,1)S(1)} %get-tuple-element.27.refs_1_, bf16[256,128]{1,0:T(8,128)(2,1)S(1)} %get-tuple-element.28.refs_2_, bf16[128,3584]{1,0:T(8,128)(2,1)S(1)} %get-tuple-element.29.refs_3_, ...), custom_call_target="tpu_custom_call" | custom-call | tf_op jit(solution)/shard_map/down_rows/pallas_call | solution.py:295
  41.9 0.2 collective-permute-start.10
  42.1 2.3 %down_rows.2 = bf16[256,1792]{1,0:T(8,128)(2,1)S(1)} custom-call(bf16[256,1024]{1,0:T(8,128)(2,1)S(1)} %get-tuple-element.24.refs_0_, bf16[256,1024]{1,0:T(8,128)(2,1)S(1)} %get-tuple-element.27.refs_1_, bf16[256,128]{1,0:T(8,128)(2,1)S(1)} %get-tuple-element.28.refs_2_, bf16[128,3584]{1,0:T(8,128)(2,1)S(1)} %get-tuple-element.29.refs_3_, ...), custom_call_target="tpu_custom_call" | custom-call | tf_op jit(solution)/shard_map/down_rows/pallas_call | solution.py:295
  44.4 0.4 collective-permute-start.6
  44.9 0.1 convert_add_fusion
  45.0 1.6 %collective-permute-start.11 = (bf16[1,4,16,1792]{3,2,1,0:T(8,128)(2,1)S(1)}, bf16[1,4,16,1792]{3,2,1,0:T(8,128)(2,1)S(1)}, u32[]{:S(2)}, u32[]{:S(2)}) collective-permute-start(bf16[1,4,16,1792]{3,2,1,0:T(8,128)(2,1)S(1)} %fusion.4), channel_id=1, source_target_pairs={{0,8},{4,12},{8,0},{12,4},{1,9},{5,13},{9,1},{13,5},{2,10},{6,14},... | collective-permute-start | bytes 688136 | tf_op jit(solution)/shard_map/ppermute | solution.py:306
  46.6 0.0 collective-permute-done.6
  46.6 0.1 convert_add_fusion.1
  46.7 0.0 copy-start.1
  46.7 0.0 copy-start.2
  46.8 1.7 %collective-permute-start.7 = (bf16[2,2,16,1792]{3,2,1,0:T(8,128)(2,1)S(1)}, bf16[2,2,16,1792]{3,2,1,0:T(8,128)(2,1)S(1)}, u32[]{:S(2)}, u32[]{:S(2)}) collective-permute-start(bf16[2,2,16,1792]{3,2,1,0:T(8,128)(2,1)S(1)} %fusion.3), channel_id=1, source_target_pairs={{0,1},{1,0},{2,3},{3,2},{4,5},{5,4},{6,7},{7,6},{8,9},{9,8},{10,11... | collective-permute-start | bytes 688136 | tf_op jit(solution)/shard_map/ppermute | solution.py:306
  48.5 4.2 %collective-permute-done.11 = bf16[1,4,16,1792]{3,2,1,0:T(8,128)(2,1)S(1)} collective-permute-done((bf16[1,4,16,1792]{3,2,1,0:T(8,128)(2,1)S(1)}, bf16[1,4,16,1792]{3,2,1,0:T(8,128)(2,1)S(1)}, u32[]{:S(2)}, u32[]{:S(2)}) %collective-permute-start.11) | collective-permute-done | bytes 229408 | tf_op jit(solution)/shard_map/ppermute | solution.py:306
  52.8 1.7 %collective-permute-start.12 = (bf16[2,16,1792]{2,1,0:T(8,128)(2,1)S(1)}, bf16[2,16,1792]{2,1,0:T(8,128)(2,1)S(1)}, u32[]{:S(2)}, u32[]{:S(2)}) collective-permute-start(bf16[2,16,1792]{2,1,0:T(8,128)(2,1)S(1)} %fusion.10), channel_id=1, source_target_pairs={{0,1},{1,0},{2,3},{3,2},{4,5},{5,4},{6,7},{7,6},{8,9},{9,8},{10,11... | collective-permute-start | bytes 344072 | tf_op jit(solution)/shard_map/ppermute | solution.py:306
  54.6 1.6 %collective-permute-start.8 = (bf16[1,2,16,1792]{3,2,1,0:T(8,128)(2,1)S(1)}, bf16[1,2,16,1792]{3,2,1,0:T(8,128)(2,1)S(1)}, u32[]{:S(2)}, u32[]{:S(2)}) collective-permute-start(bf16[1,2,16,1792]{3,2,1,0:T(8,128)(2,1)S(1)} %fusion.9), channel_id=1, source_target_pairs={{0,8},{4,12},{8,0},{12,4},{1,9},{5,13},{9,1},{13,5},{2,10},{6,14},... | collective-permute-start | bytes 344072 | tf_op jit(solution)/shard_map/ppermute | solution.py:306
  56.1 1.5 %collective-permute-done.12 = bf16[2,16,1792]{2,1,0:T(8,128)(2,1)S(1)} collective-permute-done((bf16[2,16,1792]{2,1,0:T(8,128)(2,1)S(1)}, bf16[2,16,1792]{2,1,0:T(8,128)(2,1)S(1)}, u32[]{:S(2)}, u32[]{:S(2)}) %collective-permute-start.12) | collective-permute-done | bytes 114720 | tf_op jit(solution)/shard_map/ppermute | solution.py:306
  57.7 3.6 %collective-permute-start.13 = (bf16[1,16,1792]{2,1,0:T(8,128)(2,1)S(1)}, bf16[1,16,1792]{2,1,0:T(8,128)(2,1)S(1)}, u32[]{:S(2)}, u32[]{:S(2)}) collective-permute-start(bf16[1,16,1792]{2,1,0:T(8,128)(2,1)S(1)} %fusion.16), channel_id=1, source_target_pairs={{0,2},{1,3},{2,0},{3,1},{4,6},{5,7},{6,4},{7,5},{8,10},{9,11},{10,... | collective-permute-start | bytes 172040 | tf_op jit(solution)/shard_map/ppermute | solution.py:306
  61.3 1.7 %collective-permute-start.9 = (bf16[1,16,1792]{2,1,0:T(8,128)(2,1)S(1)}, bf16[1,16,1792]{2,1,0:T(8,128)(2,1)S(1)}, u32[]{:S(2)}, u32[]{:S(2)}) collective-permute-start(bf16[1,16,1792]{2,1,0:T(8,128)(2,1)S(1)} %fusion.15), channel_id=1, source_target_pairs={{0,2},{1,3},{2,0},{3,1},{4,6},{5,7},{6,4},{7,5},{8,10},{9,11},{10,... | collective-permute-start | bytes 172040 | tf_op jit(solution)/shard_map/ppermute | solution.py:306
  63.0 2.2 %collective-permute-done.13 = bf16[1,16,1792]{2,1,0:T(8,128)(2,1)S(1)} collective-permute-done((bf16[1,16,1792]{2,1,0:T(8,128)(2,1)S(1)}, bf16[1,16,1792]{2,1,0:T(8,128)(2,1)S(1)}, u32[]{:S(2)}, u32[]{:S(2)}) %collective-permute-start.13) | collective-permute-done | bytes 57376 | tf_op jit(solution)/shard_map/ppermute | solution.py:306
  65.2 1.9 %collective-permute-done.9 = bf16[1,16,1792]{2,1,0:T(8,128)(2,1)S(1)} collective-permute-done((bf16[1,16,1792]{2,1,0:T(8,128)(2,1)S(1)}, bf16[1,16,1792]{2,1,0:T(8,128)(2,1)S(1)}, u32[]{:S(2)}, u32[]{:S(2)}) %collective-permute-start.9) | collective-permute-done | bytes 57376 | tf_op jit(solution)/shard_map/ppermute | solution.py:306
  67.1 0.7 fusion.8
  67.7 0.2 multiply_reduce_fusion
  67.9 0.1 div.28
  68.0 0.2 subtract_reduce_fusion
  68.2 0.5 convert_multiply_fusion
  (35 shorter events, 0.5 us)
Async XLA Ops:
  0.6 14.7 %collective-permute-start.1 = (bf16[16,3584]{1,0:T(8,128)(2,1)}, bf16[16,3584]{1,0:T(8,128)(2,1)S(1)}, u32[]{:S(2)}, u32[]{:S(2)}) collective-permute-start(bf16[16,3584]{1,0:T(8,128)(2,1)} %refs_0_.1), channel_id=1, source_target_pairs={{0,2},{1,3},{2,0},{3,1},{4,6},{5,7},{6,4},{7,5},{8,10},{9,11},{10,... | collective-permute-start | bytes 344072 | tf_op jit(solution)/shard_map/ppermute | solution.py:306
  4.7 10.6 %collective-permute-start = (bf16[16,3584]{1,0:T(8,128)(2,1)}, bf16[16,3584]{1,0:T(8,128)(2,1)S(1)}, u32[]{:S(2)}, u32[]{:S(2)}) collective-permute-start(bf16[16,3584]{1,0:T(8,128)(2,1)} %refs_0_.1), channel_id=1, source_target_pairs={{0,1},{1,0},{2,3},{3,2},{4,5},{5,4},{6,7},{7,6},{8,9},{9,8},{10,11... | collective-permute-start | bytes 344072 | tf_op jit(solution)/shard_map/ppermute | solution.py:306
  6.3 9.0 %collective-permute-start.2 = (bf16[16,3584]{1,0:T(8,128)(2,1)}, bf16[16,3584]{1,0:T(8,128)(2,1)S(1)}, u32[]{:S(2)}, u32[]{:S(2)}) collective-permute-start(bf16[16,3584]{1,0:T(8,128)(2,1)} %refs_0_.1), channel_id=1, source_target_pairs={{0,3},{1,2},{2,1},{3,0},{4,7},{5,6},{6,5},{7,4},{8,11},{9,10},{10,... | collective-permute-start | bytes 344072 | tf_op jit(solution)/shard_map/ppermute | solution.py:306
  11.6 3.7 %copy-start = (bf16[16,3584]{1,0:T(8,128)(2,1)S(1)}, bf16[16,3584]{1,0:T(8,128)(2,1)}, u32[]{:S(2)}) copy-start(bf16[16,3584]{1,0:T(8,128)(2,1)} %refs_0_.1) | copy-start | bytes 344068
  15.4 12.1 %collective-permute-start.4 = (bf16[64,3712]{1,0:T(8,128)(2,1)S(1)}, bf16[64,3712]{1,0:T(8,128)(2,1)S(1)}, u32[]{:S(2)}, u32[]{:S(2)}) collective-permute-start(bf16[64,3712]{1,0:T(8,128)(2,1)S(1)} %join.1.refs_1_.refs_0_), channel_id=1, source_target_pairs={{0,8},{4,12},{8,0},{12,4},{1,9},{5,13},{9,1},{13,5},{2,10},{6,14},... | collective-permute-start | bytes 1425416 | tf_op jit(solution)/shard_map/ppermute | solution.py:306
  17.2 10.5 %collective-permute-start.3 = (bf16[64,3712]{1,0:T(8,128)(2,1)S(1)}, bf16[64,3712]{1,0:T(8,128)(2,1)S(1)}, u32[]{:S(2)}, u32[]{:S(2)}) collective-permute-start(bf16[64,3712]{1,0:T(8,128)(2,1)S(1)} %join.1.refs_1_.refs_0_), channel_id=1, source_target_pairs={{0,4},{4,0},{8,12},{12,8},{1,5},{5,1},{9,13},{13,9},{2,6},{6,2},{1... | collective-permute-start | bytes 1425416 | tf_op jit(solution)/shard_map/ppermute | solution.py:306
  27.5 1.9 %collective-permute-start.5 = (bf16[64,3712]{1,0:T(8,128)(2,1)S(1)}, bf16[64,3712]{1,0:T(8,128)(2,1)S(1)}, u32[]{:S(2)}, u32[]{:S(2)}) collective-permute-start(bf16[64,3712]{1,0:T(8,128)(2,1)S(1)} %pass_on.1.refs_3_), channel_id=1, source_target_pairs={{0,4},{4,0},{8,12},{12,8},{1,5},{5,1},{9,13},{13,9},{2,6},{6,2},{1... | collective-permute-start | bytes 1425416 | tf_op jit(solution)/shard_map/ppermute | solution.py:306
  41.9 3.0 %collective-permute-start.10 = (bf16[128,1792]{1,0:T(8,128)(2,1)S(1)}, bf16[128,1792]{1,0:T(8,128)(2,1)S(1)}, u32[]{:S(2)}, u32[]{:S(2)}) collective-permute-start(bf16[128,1792]{1,0:T(8,128)(2,1)S(1)} %slice.89), channel_id=1, source_target_pairs={{0,4},{4,0},{8,12},{12,8},{1,5},{5,1},{9,13},{13,9},{2,6},{6,2},{1... | collective-permute-start | bytes 1376264 | tf_op jit(solution)/shard_map/ppermute | solution.py:306
  44.4 2.1 %collective-permute-start.6 = (bf16[128,1792]{1,0:T(8,128)(2,1)S(1)}, bf16[128,1792]{1,0:T(8,128)(2,1)S(1)}, u32[]{:S(2)}, u32[]{:S(2)}) collective-permute-start(bf16[128,1792]{1,0:T(8,128)(2,1)S(1)} %slice.81), channel_id=1, source_target_pairs={{0,4},{4,0},{8,12},{12,8},{1,5},{5,1},{9,13},{13,9},{2,6},{6,2},{1... | collective-permute-start | bytes 1376264 | tf_op jit(solution)/shard_map/ppermute | solution.py:306
  45.0 7.7 %collective-permute-start.11 = (bf16[1,4,16,1792]{3,2,1,0:T(8,128)(2,1)S(1)}, bf16[1,4,16,1792]{3,2,1,0:T(8,128)(2,1)S(1)}, u32[]{:S(2)}, u32[]{:S(2)}) collective-permute-start(bf16[1,4,16,1792]{3,2,1,0:T(8,128)(2,1)S(1)} %fusion.4), channel_id=1, source_target_pairs={{0,8},{4,12},{8,0},{12,4},{1,9},{5,13},{9,1},{13,5},{2,10},{6,14},... | collective-permute-start | bytes 688136 | tf_op jit(solution)/shard_map/ppermute | solution.py:306
  46.7 21.1 %copy-start.1 = (f32[3584]{0:T(1024)S(1)}, f32[3584]{0:T(1024)}, u32[]{:S(2)}) copy-start(f32[3584]{0:T(1024)} %param.17) | copy-start | bytes 43012
  46.7 21.5 %copy-start.2 = (s32[8]{0:T(128)S(1)}, s32[8]{0:T(128)}, u32[]{:S(2)}) copy-start(s32[8]{0:T(128)} %param.12) | copy-start | bytes 100
  46.8 7.8 %collective-permute-start.7 = (bf16[2,2,16,1792]{3,2,1,0:T(8,128)(2,1)S(1)}, bf16[2,2,16,1792]{3,2,1,0:T(8,128)(2,1)S(1)}, u32[]{:S(2)}, u32[]{:S(2)}) collective-permute-start(bf16[2,2,16,1792]{3,2,1,0:T(8,128)(2,1)S(1)} %fusion.3), channel_id=1, source_target_pairs={{0,1},{1,0},{2,3},{3,2},{4,5},{5,4},{6,7},{7,6},{8,9},{9,8},{10,11... | collective-permute-start | bytes 688136 | tf_op jit(solution)/shard_map/ppermute | solution.py:306
  52.8 4.9 %collective-permute-start.12 = (bf16[2,16,1792]{2,1,0:T(8,128)(2,1)S(1)}, bf16[2,16,1792]{2,1,0:T(8,128)(2,1)S(1)}, u32[]{:S(2)}, u32[]{:S(2)}) collective-permute-start(bf16[2,16,1792]{2,1,0:T(8,128)(2,1)S(1)} %fusion.10), channel_id=1, source_target_pairs={{0,1},{1,0},{2,3},{3,2},{4,5},{5,4},{6,7},{7,6},{8,9},{9,8},{10,11... | collective-permute-start | bytes 344072 | tf_op jit(solution)/shard_map/ppermute | solution.py:306
  54.6 6.7 %collective-permute-start.8 = (bf16[1,2,16,1792]{3,2,1,0:T(8,128)(2,1)S(1)}, bf16[1,2,16,1792]{3,2,1,0:T(8,128)(2,1)S(1)}, u32[]{:S(2)}, u32[]{:S(2)}) collective-permute-start(bf16[1,2,16,1792]{3,2,1,0:T(8,128)(2,1)S(1)} %fusion.9), channel_id=1, source_target_pairs={{0,8},{4,12},{8,0},{12,4},{1,9},{5,13},{9,1},{13,5},{2,10},{6,14},... | collective-permute-start | bytes 344072 | tf_op jit(solution)/shard_map/ppermute | solution.py:306
  57.7 7.5 %collective-permute-start.13 = (bf16[1,16,1792]{2,1,0:T(8,128)(2,1)S(1)}, bf16[1,16,1792]{2,1,0:T(8,128)(2,1)S(1)}, u32[]{:S(2)}, u32[]{:S(2)}) collective-permute-start(bf16[1,16,1792]{2,1,0:T(8,128)(2,1)S(1)} %fusion.16), channel_id=1, source_target_pairs={{0,2},{1,3},{2,0},{3,1},{4,6},{5,7},{6,4},{7,5},{8,10},{9,11},{10,... | collective-permute-start | bytes 172040 | tf_op jit(solution)/shard_map/ppermute | solution.py:306
  61.3 5.8 %collective-permute-start.9 = (bf16[1,16,1792]{2,1,0:T(8,128)(2,1)S(1)}, bf16[1,16,1792]{2,1,0:T(8,128)(2,1)S(1)}, u32[]{:S(2)}, u32[]{:S(2)}) collective-permute-start(bf16[1,16,1792]{2,1,0:T(8,128)(2,1)S(1)} %fusion.15), channel_id=1, source_target_pairs={{0,2},{1,3},{2,0},{3,1},{4,6},{5,7},{6,4},{7,5},{8,10},{9,11},{10,... | collective-permute-start | bytes 172040 | tf_op jit(solution)/shard_map/ppermute | solution.py:306

commit v5 on v4

--- a/solution.py
+++ b/solution.py
@@ -11,6 +11,7 @@
 ROT = 128
 CORES = 2
 SMALL_VMEM = 10 * 1024 * 1024
+EARLY = 2
 HIDDEN_VMEM = 5 * 1024 * 1024
 
 
@@ -34,10 +35,10 @@
     return pltpu.VMEM(shape, dtype)
 
 
-def apart_kernel(experts, rows, chunk, n_after, *refs):
+def apart_kernel(experts, rows, chunk, n_in, *refs):
     source = refs[0]
-    outs = refs[1 + n_after : 1 + n_after + len(experts)]
-    done, held, sems = refs[1 + n_after + len(experts) :]
+    outs = refs[n_in : n_in + len(experts)]
+    done, *own_out, held, sems = refs[n_in + len(experts) :]
     slots = held.shape[0]
     count = 2 * outs[0].shape[2] // 128
     pieces = [(n, step) for n in range(len(experts)) for step in range(outs[0].shape[1] // rows)]
@@ -50,8 +51,14 @@
             sems.at[at % slots],
         )
 
+    own_copies = []
+    for out in own_out:
+        columns = pl.ds(refs[1][0] * out.shape[1], out.shape[1])
+        own_copies.append(pltpu.make_async_copy(refs[2].at[:, columns], out, sems.at[slots]))
     for at in range(min(slots, len(pieces))):
         copy(at).start()
+    for own_copy in own_copies:
+        own_copy.start()
     for at, (n, step) in enumerate(pieces):
         copy(at).wait()
         for row in range(0, rows, chunk):
@@ -62,29 +69,39 @@
                 outs[n][q % 2, here, (q // 2) * 128 : (q // 2 + 1) * 128] = pairs[q]
         if at + slots < len(pieces):
             copy(at + slots).start()
+    for own_copy in own_copies:
+        own_copy.wait()
     done[...] = jnp.zeros_like(done)
 
 
-def apart(packed, experts, feature_len, inner, after):
+def apart(packed, experts, feature_len, inner, after, shared=None):
     count = 2 * inner // 128
     rows = feature_len // 4 if feature_len % 256 == 0 else feature_len
     chunk = 64 if rows % 64 == 0 else rows
     whole = pl.BlockSpec(memory_space=pltpu.VMEM)
+    anywhere = pl.BlockSpec(memory_space=pl.ANY)
+    inputs, specs, own = list(after), [anywhere] * len(after), []
+    if shared is not None:
+        index, columns, units = shared
+        inputs = [index, columns] + inputs
+        specs = [pl.BlockSpec(memory_space=pltpu.SMEM), anywhere] + specs
+        own = [vmem((feature_len, units, 2, 128), columns.dtype)]
     out = pl.pallas_call(
-        functools.partial(apart_kernel, experts, rows, chunk, len(after)),
-        in_specs=[pl.BlockSpec(memory_space=pl.ANY)] * (1 + len(after)),
-        out_specs=[whole] * (len(experts) + 1),
+        functools.partial(apart_kernel, experts, rows, chunk, 1 + len(inputs)),
+        in_specs=[pl.BlockSpec(memory_space=pl.ANY)] + specs,
+        out_specs=[whole] * (len(experts) + 1 + len(own)),
         out_shape=[vmem((2, feature_len, inner), packed.dtype)] * len(experts)
-        + [jax.ShapeDtypeStruct((8, 128), jnp.float32)],
+        + [jax.ShapeDtypeStruct((8, 128), jnp.float32)]
+        + own,
         scratch_shapes=[
             pltpu.VMEM((4, rows * count, 128), packed.dtype),
-            pltpu.SemaphoreType.DMA((4,)),
+            pltpu.SemaphoreType.DMA((5,)),
         ],
         compiler_params=pltpu.CompilerParams(vmem_limit_bytes=SMALL_VMEM),
         cost_estimate=pl.CostEstimate(flops=0, bytes_accessed=1024, transcendentals=0),
         name="apart",
-    )(packed, *after)
-    return out[:-1], out[-1]
+    )(packed, *inputs)
+    return out[: len(experts)], out[len(experts)], out[len(experts) + 1 :]
 
 
 def pass_kernel(value, *refs):
@@ -168,7 +185,7 @@
 def rest_kernel(n_first, n_chips, *refs):
     n_pieces = CORES * n_chips
     index, pieces = refs[0], refs[1 : 1 + n_pieces]
-    signs, first, shared, shared_down, *outs, rows_s, sem = refs[1 + n_pieces :]
+    signs, first, second, shared, shared_down, *outs, rows_s, sem = refs[1 + n_pieces :]
     deq, shared_hidden, combine, shared_out = outs
     own = shared_out.shape[0]
     own = pl.ds(pl.multiple_of(index[0] * own, own), own)
@@ -185,8 +202,11 @@
                 deq[base : base + count, :] = first[core * count : (core + 1) * count, :]
             else:
                 piece = pieces[CORES + core * (n_chips - 1) + chip - 1]
-                sources.append(piece)
-                bases.append(base)
+                if core == 0:
+                    deq[base : base + count, :] = second[(chip - 1) * count : chip * count, :]
+                else:
+                    sources.append(piece)
+                    bases.append(base)
             rows_s[base : base + count, :] = piece[:, :feature_len]
             combine[base : base + count, :] = piece[:, feature_len:].astype(jnp.float32)
     rotate(sources, signs, deq, bases)
@@ -197,14 +217,14 @@
     copy.wait()
 
 
-def rest_rows(index, pieces, signs, first, shared, shared_down, n_chips):
+def rest_rows(index, pieces, signs, first, second, shared, shared_down, n_chips):
     whole = pl.BlockSpec(memory_space=pltpu.VMEM)
     rows = sum(piece.shape[0] for piece in pieces)
     feature_len = first.shape[1]
     return pl.pallas_call(
         functools.partial(rest_kernel, len(pieces), n_chips),
         in_specs=[pl.BlockSpec(memory_space=pltpu.SMEM)]
-        + [whole] * (len(pieces) + 3)
+        + [whole] * (len(pieces) + 4)
         + [pl.BlockSpec(memory_space=pl.ANY)],
         out_specs=[whole] * 4,
         out_shape=[
@@ -219,7 +239,7 @@
         ],
         compiler_params=pltpu.CompilerParams(vmem_limit_bytes=HIDDEN_VMEM + 2 * rows * feature_len),
         name="rest_rows",
-    )(index, *pieces, signs, first, shared, shared_down)
+    )(index, *pieces, signs, first, second, shared, shared_down)
 
 
 def hidden_kernel(experts, *refs):
@@ -302,6 +322,46 @@
     )(*hidden, shared_hidden, shared_down, *downs)
 
 
+def finish_kernel(n_parts, *refs):
+    parts = refs[: 2 * n_parts]
+    readout, flags, mixed, scores = refs[2 * n_parts :]
+    rows, feature_len = mixed.shape
+    pairs = scores.shape[1]
+    at = 0
+    dots = jnp.zeros((rows, 1), jnp.float32)
+    squares = jnp.zeros((rows, 1), jnp.float32)
+    for part, got in zip(parts[::2], parts[1::2]):
+        total = part[...] + got[...].astype(jnp.float32)
+        columns = slice(at, at + total.shape[1])
+        mixed[:, columns] = total.astype(mixed.dtype)
+        dots += jnp.sum(total * readout[:, columns], axis=1, keepdims=True)
+        squares += jnp.sum(total * total, axis=1, keepdims=True)
+        at += total.shape[1]
+    row_score = dots / jnp.sqrt(squares * (1.0 / feature_len) + 1e-06)
+    row = lax.broadcasted_iota(jnp.int32, (rows, pairs), 0)
+    first = 2 * lax.broadcasted_iota(jnp.int32, (rows, pairs), 1)
+    signed = jnp.where(row == first, row_score, jnp.where(row == first + 1, -row_score, 0.0))
+    scores[...] = jnp.sum(signed, axis=0, keepdims=True) * (1 - 2 * flags[...]).astype(jnp.float32)
+
+
+def finish(parts, readout, pair_flags):
+    whole = pl.BlockSpec(memory_space=pltpu.VMEM)
+    rows = parts[0][0].shape[0]
+    flat = [term for part in parts for term in part]
+    mixed, scores = pl.pallas_call(
+        functools.partial(finish_kernel, len(parts)),
+        in_specs=[whole] * (len(flat) + 2),
+        out_specs=[whole] * 2,
+        out_shape=[
+            jax.ShapeDtypeStruct((rows, readout.shape[0]), jnp.bfloat16),
+            jax.ShapeDtypeStruct((1, rows // 2), jnp.float32),
+        ],
+        compiler_params=pltpu.CompilerParams(vmem_limit_bytes=HIDDEN_VMEM),
+        name="finish",
+    )(*flat, readout.reshape(1, -1), pair_flags.reshape(1, -1))
+    return mixed, scores.reshape(-1)
+
+
 def exchange(value, axis, flip):
     return lax.ppermute(value, axis, [(i, i ^ flip) for i in range(lax.axis_size(axis))])
 
@@ -344,40 +404,58 @@
     shared_len = shared_down.shape[0]
     part_len = shared_len // expert_count
     if part_len % 128 == 0:
-        shared_in = lax.dynamic_slice_in_dim(shared_gate_up, expert_at * part_len, part_len, 2)
         shared_out, index = shared_down, expert_at.reshape(1)
+        columns_of = shared_gate_up.reshape(feature_len, 2, shared_len // 128, 128)
+        columns_of = pltpu.with_memory_space_constraint(
+            columns_of.transpose(0, 2, 1, 3), pltpu.HBM
+        )
+        shared = (index, columns_of, part_len // 128)
     else:
         mine = lax.broadcasted_iota(jnp.int32, (shared_len, 1), 0) // part_len == expert_at
-        shared_in, index = shared_gate_up, jnp.zeros((1,), jnp.int32)
+        shared_in, index = shared_gate_up.reshape(feature_len, -1), jnp.zeros((1,), jnp.int32)
         shared_out = jnp.where(mine, shared_down, jnp.zeros_like(shared_down))
-    shared_in = shared_in.reshape(feature_len, -1)
+        shared = None
     signs = sign_matrix(2 if feature_len % (2 * ROT) == 0 else 1)
 
     packed = expert_gate_up.reshape(n_local, feature_len, 2, inner // 128, 128)
     packed = packed.transpose(0, 1, 3, 2, 4).reshape(n_local, -1, 128)
     packed = pltpu.with_memory_space_constraint(packed, pltpu.HBM)
 
-    def prepared(experts, after):
-        return apart(packed, experts, feature_len, inner, after)
-
-    early = (n_local + 3) // 4
+    early = (n_local + EARLY - 1) // EARLY
     from_z = [exchange(tokens, "narrow", flip) for flip in range(1, narrow_count)]
-    weights, done = prepared(list(range(early)), [lanes, shared_in, select, signs, index])
+    weights, done, own = apart(
+        packed, [0], feature_len, inner, [lanes, select, signs, index], shared
+    )
+    for expert in range(1, early):
+        more, done, _ = apart(packed, [expert], feature_len, inner, [done])
+        weights = weights + more
+    if own:
+        shared_in = own[0].transpose(0, 2, 1, 3).reshape(feature_len, -1)
     along_z = join([tokens] + from_z, lanes, [done])
     from_x = [exchange(along_z, "expert", flip * CORES) for flip in range(1, chips)]
     near = exchange(along_z, "expert", 1)
     after = [along_z]
     if n_local > early:
-        late, done = prepared(list(range(early, n_local)), after)
+        late, done, _ = apart(
+            packed, list(range(early, n_local)), feature_len, inner, after + [shared_in]
+        )
         weights = weights + late
         after = [done]
-    from_x = [pass_on(part, after) for part in from_x]
+    first = first_rows([along_z, near], signs, feature_len)
+    from_x = [pass_on(part, after + [first]) for part in from_x]
     from_both = [exchange(part, "expert", 1) for part in from_x]
-    first = first_rows([along_z, near], signs, feature_len)
+    second = first_rows(from_x, signs, feature_len)
 
     shared_out = pltpu.with_memory_space_constraint(shared_out, pltpu.HBM)
     deq, shared_hidden, combine, shared_out = rest_rows(
-        index, [along_z, near] + from_x + from_both, signs, first, shared_in, shared_out, chips
+        index,
+        [along_z, near] + from_x + from_both,
+        signs,
+        first,
+        second,
+        shared_in,
+        shared_out,
+        chips,
     )
     down = pltpu.with_memory_space_constraint(expert_down, pltpu.HBM)
     hidden, downs = [], []
@@ -407,20 +485,16 @@
             parts, step = halve(parts, axis, step), 2 * step
         return parts[0]
 
-    totals = []
-    if cut:
-        parts = halve(jnp.swapaxes(by_core(0, cut), 0, 1), "narrow", 1)
-        parts = add_up(jnp.swapaxes(parts, 0, 1), "expert", CORES)
-        totals.append(add_up(parts, "narrow", 2))
-    totals.append(add_up(add_up(by_core(cut, feature_len), "expert", CORES), "narrow", 1))
-    total_sum = jnp.concatenate(totals, axis=1)
-    mixed = total_sum.astype(jnp.bfloat16)
-    row_score = jnp.sum(total_sum * readout[None, :], axis=1) / jnp.sqrt(
-        jnp.mean(total_sum * total_sum, axis=1) + 1e-06
-    )
-    paired = row_score.reshape(-1, 2)
-    pmi_scores = (paired[:, 0] - paired[:, 1]) * (1 - 2 * pair_flags).astype(jnp.float32)
-    return (mixed, pmi_scores)
+    def last_pair(parts, step):
+        while parts.shape[0] > 2:
+            parts, step = halve(parts, "narrow", step), 2 * step
+        return parts[0], exchange(parts[1].astype(jnp.bfloat16), "narrow", step)
+
+    parts = halve(jnp.swapaxes(by_core(0, cut), 0, 1), "narrow", 1)
+    parts = add_up(jnp.swapaxes(parts, 0, 1), "expert", CORES)
+    left = last_pair(parts, 2)
+    right = last_pair(add_up(by_core(cut, feature_len), "expert", CORES), 1)
+    return finish([left, right], readout, pair_flags)
 
 
 def solution(mesh):

time: 69 us -> 68.6 us (level)
  Pallas kernels: 27.7 us -> 31 us
  local copies, waits for them, and re-layouts: 4.26 us -> 1.1 us
  other arithmetic: 3.14 us -> 1.57 us
  waiting for transfers between devices: 12.7 us -> 14.1 us
    dynamic_slice x1 -> x0, local copies, waits for them, and re-layouts: 3.07 us -> none  [per_device(): lax.dynamic_slice_in_dim(shared_gate_up, expert_at * part_len, part_len, 2)]
    pallas_call x2 -> x4, Pallas kernels: 11.8 us -> 14.2 us  [the longest x3 13.5 us: apart(): pl.pallas_call(functools.partial(apart_kernel, experts, rows, chunk, 1 +...]
    ppermute x14, waiting for transfers between devices: 12.7 us -> 14.1 us  [exchange(): lax.ppermute(value, axis, [(i, i ^ flip) for i in range(lax.axis_size(axi...]
    pallas_call x1 -> x2, Pallas kernels: 1.12 us -> 1.78 us  [first_rows(): pl.pallas_call(functools.partial(first_kernel, len(pieces)), in_specs=[wh...]
  transfers between devices with their start and end apart: 14 -> 14, of which waited for: 6 -> 6; matrix products, arithmetic and copies ran while one was open for 8% -> 4% of each run, Pallas kernels for 22% -> 26%
where the time goes in v5:
time: 68.6 us; the launch traced here: 68.4 us
  Pallas kernels  31 us (45%)
  starting transfers between devices  19.7 us (29%)
  waiting for transfers between devices  14.1 us (21%)
  other arithmetic  1.57 us (2%)
  local copies, waits for them, and re-layouts  1.1 us (2%)
  between operations  0.97 us (1%)
    ppermute x14, starting transfers between devices, exchange(): lax.ppermute(value, axis, [(i, i ^ flip) for i in range(lax.axis_size(axi...  19.7 us
    ppermute x14, waiting for transfers between devices, exchange(): lax.ppermute(value, axis, [(i, i ^ flip) for i in range(lax.axis_size(axi...  14.1 us
    pallas_call x3, Pallas kernels, apart(): pl.pallas_call(functools.partial(apart_kernel, experts, rows, chunk, 1 +...  13.5 us
    pallas_call x2, Pallas kernels, hidden_rows(): pl.pallas_call(functools.partial(hidden_kernel, experts), in_specs=[whole...  8.24 us
    pallas_call x2, Pallas kernels, down_rows(): pl.pallas_call(functools.partial(down_kernel, start, tile, len(hidden)),...  4.68 us
    pallas_call x1, Pallas kernels, rest_rows(): pl.pallas_call(functools.partial(rest_kernel, len(pieces), n_chips), in_s...  2.13 us
    pallas_call x2, Pallas kernels, first_rows(): pl.pallas_call(functools.partial(first_kernel, len(pieces)), in_specs=[wh...  1.78 us
  transfers between devices with their start and end apart: 14, of which 6 were waited for; matrix products, arithmetic and copies ran while one was open for 4% of the time, Pallas kernels for 26%

profile of v5, /device:TPU:0, one launch (start us, length us, event | category | flops | bytes accessed | tf_op | source)
XLA Modules:
  0.0 68.4 jit_solution(14953117759833554955)
XLA Ops:
  0.6 3.1 %collective-permute-start = (bf16[16,3584]{1,0:T(8,128)(2,1)}, bf16[16,3584]{1,0:T(8,128)(2,1)S(1)}, u32[]{:S(2)}, u32[]{:S(2)}) collective-permute-start(bf16[16,3584]{1,0:T(8,128)(2,1)} %refs_0_.1), channel_id=1, source_target_pairs={{0,1},{1,0},{2,3},{3,2},{4,5},{5,4},{6,7},{7,6},{8,9},{9,8},{10,11... | collective-permute-start | bytes 344072 | tf_op jit(solution)/shard_map/ppermute | solution.py:366
  3.7 2.6 %collective-permute-start.1 = (bf16[16,3584]{1,0:T(8,128)(2,1)}, bf16[16,3584]{1,0:T(8,128)(2,1)S(1)}, u32[]{:S(2)}, u32[]{:S(2)}) collective-permute-start(bf16[16,3584]{1,0:T(8,128)(2,1)} %refs_0_.1), channel_id=1, source_target_pairs={{0,2},{1,3},{2,0},{3,1},{4,6},{5,7},{6,4},{7,5},{8,10},{9,11},{10,... | collective-permute-start | bytes 344072 | tf_op jit(solution)/shard_map/ppermute | solution.py:366
  6.3 0.0 collective-permute-start.2
  6.3 0.7 %select_reduce_fusion = f32[64,16]{0,1:T(8,128)S(1)} fusion(f32[64,8]{0,1:T(8,128)} %param.11, s32[64,8]{0,1:T(8,128)} %param.10), kind=kLoop, calls=%fused_computation.27 | loop fusion | flops 23552 | bytes 8192 | tf_op jit(solution)/shard_map/reduce_sum | solution.py:390
  7.1 0.1 copy.28
  7.2 0.1 pad_maximum_fusion
  7.3 0.6 gather_fusion
  7.9 0.3 select_convert_fusion.refs_5_.refs_2_.refs_1_
  8.2 0.1 fusion.12.refs_4_.refs_2_
  8.3 3.8 %apart.3 = (bf16[2,3584,512]{2,1,0:T(8,128)(2,1)S(1)}, f32[8,128]{1,0:T(8,128)S(1)}, bf16[3584,1,2,128]{3,2,1,0:T(2,128)(2,1)S(1)}) custom-call(bf16[4,28672,128]{2,1,0:T(8,128)(2,1)} %bitcast.71, s32[1]{0:T(128)} %bitcast.refs_1_.refs_6_.refs_0_, bf16[3584,4,2,128]{3,2,1,0:T(2,128)(2,1)} %bitcast.74, bf16[64,128]{1,0:T(8,128)(2,1)S(1)} %bitcast.68, ...), custom_call_target="tpu_custom_call" | custom-call | bytes 1024 | tf_op jit(solution)/shard_map/apart/pallas_call | solution.py:89
  12.0 0.0 copy-start
  12.1 3.7 %apart.4 = (bf16[2,3584,512]{2,1,0:T(8,128)(2,1)S(1)}, f32[8,128]{1,0:T(8,128)S(1)}) custom-call(bf16[4,28672,128]{2,1,0:T(8,128)(2,1)} %bitcast.72, f32[8,128]{1,0:T(8,128)S(1)} %get-tuple-element.22.refs_1_), custom_call_target="tpu_custom_call" | custom-call | bytes 1024 | tf_op jit(solution)/shard_map/apart/pallas_call | solution.py:89
  15.8 0.0 collective-permute-done.refs_1_
  15.8 0.0 collective-permute-done.1.refs_2_
  15.8 0.0 collective-permute-done.2.refs_3_
  15.8 0.1 collective-permute-start.3
  15.9 1.8 %collective-permute-start.4 = (bf16[64,3712]{1,0:T(8,128)(2,1)S(1)}, bf16[64,3712]{1,0:T(8,128)(2,1)S(1)}, u32[]{:S(2)}, u32[]{:S(2)}) collective-permute-start(bf16[64,3712]{1,0:T(8,128)(2,1)S(1)} %join.1.refs_1_.refs_0_), channel_id=1, source_target_pairs={{0,8},{4,12},{8,0},{12,4},{1,9},{5,13},{9,1},{13,5},{2,10},{6,14},... | collective-permute-start | bytes 1425416 | tf_op jit(solution)/shard_map/ppermute | solution.py:366
  17.7 0.2 copy.56
  17.9 6.0 %apart.5 = (bf16[2,3584,512]{2,1,0:T(8,128)(2,1)S(1)}, bf16[2,3584,512]{2,1,0:T(8,128)(2,1)S(1)}, f32[8,128]{1,0:T(8,128)S(1)}) custom-call(bf16[4,28672,128]{2,1,0:T(8,128)(2,1)} %bitcast.73, bf16[64,3712]{1,0:T(8,128)(2,1)S(1)} %join.1.refs_1_.refs_0_, bf16[3584,256]{1,0:T(8,128)(2,1)S(1)} %bitcast.65), custom_call_target="tpu_custom_call" | custom-call | bytes 1024 | tf_op jit(solution)/shard_map/apart/pallas_call | solution.py:89
  24.0 1.1 %first_rows.2.refs_1_.refs_6_ = bf16[128,3584]{1,0:T(8,128)(2,1)S(1)} custom-call(bf16[64,3712]{1,0:T(8,128)(2,1)S(1)} %join.1.refs_1_.refs_0_, bf16[64,3712]{1,0:T(8,128)(2,1)S(1)} %collective-permute-done.3.refs_1_.refs_2_, bf16[256,256]{1,0:T(8,128)(2,1)S(1)} %select_convert_fusion.refs_5_.refs_2_.refs_1_), custom_call_target="tpu_custom_call" | custom-call | bytes 1024 | tf_op jit(solution)/shard_map/first_rows/pallas_call | solution.py:174
  25.1 4.1 %collective-permute-done.4.value = bf16[64,3712]{1,0:T(8,128)(2,1)S(1)} collective-permute-done((bf16[64,3712]{1,0:T(8,128)(2,1)S(1)}, bf16[64,3712]{1,0:T(8,128)(2,1)S(1)}, u32[]{:S(2)}, u32[]{:S(2)}) %collective-permute-start.4) | collective-permute-done | bytes 475168 | tf_op jit(solution)/shard_map/ppermute | solution.py:366
  29.2 0.1 collective-permute-start.5
  29.3 0.7 first_rows.3.refs_7_
  30.0 1.2 %collective-permute-done.5.refs_4_ = bf16[64,3712]{1,0:T(8,128)(2,1)S(1)} collective-permute-done((bf16[64,3712]{1,0:T(8,128)(2,1)S(1)}, bf16[64,3712]{1,0:T(8,128)(2,1)S(1)}, u32[]{:S(2)}, u32[]{:S(2)}) %collective-permute-start.5) | collective-permute-done | bytes 475168 | tf_op jit(solution)/shard_map/ppermute | solution.py:366
  31.2 2.1 %rest_rows.1 = (bf16[256,3584]{1,0:T(8,128)(2,1)S(1)}, bf16[256,128]{1,0:T(8,128)(2,1)S(1)}, f32[256,128]{1,0:T(8,128)S(1)}, bf16[128,3584]{1,0:T(8,128)(2,1)S(1)}) custom-call(s32[1]{0:T(128)} %bitcast.refs_1_.refs_6_.refs_0_, bf16[64,3712]{1,0:T(8,128)(2,1)S(1)} %join.1.refs_1_.refs_0_, bf16[64,3712]{1,0:T(8,128)(2,1)S(1)} %collective-permute-done.3.refs_1_.refs_2_, ...), custom_call_target="tpu_custom_call" | custom-call | tf_op jit(solution)/shard_map/rest_rows/pallas_call | solution.py:224
  33.3 4.2 %hidden_rows.2 = (bf16[256,1024]{1,0:T(8,128)(2,1)S(1)}, bf16[512,3584]{1,0:T(8,128)(2,1)S(1)}, bf16[512,3584]{1,0:T(8,128)(2,1)S(1)}) custom-call(bf16[256,3584]{1,0:T(8,128)(2,1)S(1)} %get-tuple-element.26.refs_0_, f32[256,128]{1,0:T(8,128)S(1)} %get-tuple-element.27.refs_1_, f32[4,128]{1,0:T(4,128)S(1)} %fusion.12.refs_4_.refs_2_, ...), custom_call_target="tpu_custom_call" | custom-call | tf_op jit(solution)/shard_map/hidden_rows/pallas_call | solution.py:272
  37.5 4.0 %hidden_rows.3 = (bf16[256,1024]{1,0:T(8,128)(2,1)S(1)}, bf16[512,3584]{1,0:T(8,128)(2,1)S(1)}, bf16[512,3584]{1,0:T(8,128)(2,1)S(1)}) custom-call(bf16[256,3584]{1,0:T(8,128)(2,1)S(1)} %get-tuple-element.26.refs_0_, f32[256,128]{1,0:T(8,128)S(1)} %get-tuple-element.27.refs_1_, f32[4,128]{1,0:T(4,128)S(1)} %fusion.12.refs_4_.refs_2_, ...), custom_call_target="tpu_custom_call" | custom-call | tf_op jit(solution)/shard_map/hidden_rows/pallas_call | solution.py:272
  41.5 0.0 copy-start.2
  41.6 2.3 %down_rows.2 = bf16[256,1792]{1,0:T(8,128)(2,1)S(1)} custom-call(bf16[256,1024]{1,0:T(8,128)(2,1)S(1)} %get-tuple-element.30.refs_0_, bf16[256,1024]{1,0:T(8,128)(2,1)S(1)} %get-tuple-element.33.refs_1_, bf16[256,128]{1,0:T(8,128)(2,1)S(1)} %get-tuple-element.34.refs_2_, bf16[128,3584]{1,0:T(8,128)(2,1)S(1)} %get-tuple-element.35.refs_3_, ...), custom_call_target="tpu_custom_call" | custom-call | tf_op jit(solution)/shard_map/down_rows/pallas_call | solution.py:315
  43.9 0.2 collective-permute-start.6
  44.2 2.3 %down_rows.3 = bf16[256,1792]{1,0:T(8,128)(2,1)S(1)} custom-call(bf16[256,1024]{1,0:T(8,128)(2,1)S(1)} %get-tuple-element.30.refs_0_, bf16[256,1024]{1,0:T(8,128)(2,1)S(1)} %get-tuple-element.33.refs_1_, bf16[256,128]{1,0:T(8,128)(2,1)S(1)} %get-tuple-element.34.refs_2_, bf16[128,3584]{1,0:T(8,128)(2,1)S(1)} %get-tuple-element.35.refs_3_, ...), custom_call_target="tpu_custom_call" | custom-call | tf_op jit(solution)/shard_map/down_rows/pallas_call | solution.py:315
  46.6 0.4 collective-permute-start.10
  47.0 0.0 collective-permute-done.6
  47.0 0.1 convert_add_fusion.1
  47.1 0.0 copy-start.1
  47.1 1.7 %collective-permute-start.7 = (bf16[2,2,16,1792]{3,2,0,1:T(8,128)(2,1)S(1)}, bf16[2,2,16,1792]{3,2,0,1:T(8,128)(2,1)S(1)}, u32[]{:S(2)}, u32[]{:S(2)}) collective-permute-start(bf16[2,2,16,1792]{3,2,0,1:T(8,128)(2,1)S(1)} %fusion.4), channel_id=1, source_target_pairs={{0,1},{1,0},{2,3},{3,2},{4,5},{5,4},{6,7},{7,6},{8,9},{9,8},{10,11... | collective-permute-start | bytes 688136 | tf_op jit(solution)/shard_map/ppermute | solution.py:366
  48.8 0.1 convert_add_fusion
  48.9 1.6 %collective-permute-start.11 = (bf16[1,4,16,1792]{3,2,1,0:T(8,128)(2,1)S(1)}, bf16[1,4,16,1792]{3,2,1,0:T(8,128)(2,1)S(1)}, u32[]{:S(2)}, u32[]{:S(2)}) collective-permute-start(bf16[1,4,16,1792]{3,2,1,0:T(8,128)(2,1)S(1)} %fusion.3), channel_id=1, source_target_pairs={{0,8},{4,12},{8,0},{12,4},{1,9},{5,13},{9,1},{13,5},{2,10},{6,14},... | collective-permute-start | bytes 688136 | tf_op jit(solution)/shard_map/ppermute | solution.py:366
  50.5 4.3 %collective-permute-done.7 = bf16[2,2,16,1792]{3,2,0,1:T(8,128)(2,1)S(1)} collective-permute-done((bf16[2,2,16,1792]{3,2,0,1:T(8,128)(2,1)S(1)}, bf16[2,2,16,1792]{3,2,0,1:T(8,128)(2,1)S(1)}, u32[]{:S(2)}, u32[]{:S(2)}) %collective-permute-start.7) | collective-permute-done | bytes 229408 | tf_op jit(solution)/shard_map/ppermute | solution.py:366
  54.9 1.8 %collective-permute-start.8 = (bf16[1,2,16,1792]{3,2,1,0:T(8,128)(2,1)S(1)}, bf16[1,2,16,1792]{3,2,1,0:T(8,128)(2,1)S(1)}, u32[]{:S(2)}, u32[]{:S(2)}) collective-permute-start(bf16[1,2,16,1792]{3,2,1,0:T(8,128)(2,1)S(1)} %fusion.7), channel_id=1, source_target_pairs={{0,8},{4,12},{8,0},{12,4},{1,9},{5,13},{9,1},{13,5},{2,10},{6,14},... | collective-permute-start | bytes 344072 | tf_op jit(solution)/shard_map/ppermute | solution.py:366
  56.7 0.0 collective-permute-done.11
  56.8 1.5 %collective-permute-start.12 = (bf16[2,16,1792]{2,1,0:T(8,128)(2,1)S(1)}, bf16[2,16,1792]{2,1,0:T(8,128)(2,1)S(1)}, u32[]{:S(2)}, u32[]{:S(2)}) collective-permute-start(bf16[2,16,1792]{2,1,0:T(8,128)(2,1)S(1)} %fusion.8), channel_id=1, source_target_pairs={{0,1},{1,0},{2,3},{3,2},{4,5},{5,4},{6,7},{7,6},{8,9},{9,8},{10,11... | collective-permute-start | bytes 344072 | tf_op jit(solution)/shard_map/ppermute | solution.py:366
  58.2 1.5 %collective-permute-done.8 = bf16[1,2,16,1792]{3,2,1,0:T(8,128)(2,1)S(1)} collective-permute-done((bf16[1,2,16,1792]{3,2,1,0:T(8,128)(2,1)S(1)}, bf16[1,2,16,1792]{3,2,1,0:T(8,128)(2,1)S(1)}, u32[]{:S(2)}, u32[]{:S(2)}) %collective-permute-start.8) | collective-permute-done | bytes 114720 | tf_op jit(solution)/shard_map/ppermute | solution.py:366
  59.8 2.7 %collective-permute-start.9 = (bf16[16,1792]{1,0:T(8,128)(2,1)S(1)}, bf16[16,1792]{1,0:T(8,128)(2,1)S(1)}, u32[]{:S(2)}, u32[]{:S(2)}) collective-permute-start(bf16[16,1792]{1,0:T(8,128)(2,1)S(1)} %fusion.9), channel_id=1, source_target_pairs={{0,2},{1,3},{2,0},{3,1},{4,6},{5,7},{6,4},{7,5},{8,10},{9,11},{10,... | collective-permute-start | bytes 172040 | tf_op jit(solution)/shard_map/ppermute | solution.py:366
  62.6 2.2 %collective-permute-start.13 = (bf16[16,1792]{1,0:T(8,128)(2,1)S(1)}, bf16[16,1792]{1,0:T(8,128)(2,1)S(1)}, u32[]{:S(2)}, u32[]{:S(2)}) collective-permute-start(bf16[16,1792]{1,0:T(8,128)(2,1)S(1)} %fusion.10), channel_id=1, source_target_pairs={{0,2},{1,3},{2,0},{3,1},{4,6},{5,7},{6,4},{7,5},{8,10},{9,11},{10,... | collective-permute-start | bytes 172040 | tf_op jit(solution)/shard_map/ppermute | solution.py:366
  64.8 0.5 collective-permute-done.9.refs_1_
  65.3 2.4 %collective-permute-done.13.refs_3_ = bf16[16,1792]{1,0:T(8,128)(2,1)S(1)} collective-permute-done((bf16[16,1792]{1,0:T(8,128)(2,1)S(1)}, bf16[16,1792]{1,0:T(8,128)(2,1)S(1)}, u32[]{:S(2)}, u32[]{:S(2)}) %collective-permute-start.13) | collective-permute-done | bytes 57376 | tf_op jit(solution)/shard_map/ppermute | solution.py:366
  67.7 0.7 %finish.1 = (bf16[16,3584]{1,0:T(8,128)(2,1)}, f32[1,8]{1,0:T(1,128)}) custom-call(f32[16,1792]{1,0:T(8,128)S(1)} %slice_bitcast_fusion.3.refs_0_, bf16[16,1792]{1,0:T(8,128)(2,1)S(1)} %collective-permute-done.9.refs_1_, f32[16,1792]{1,0:T(8,128)S(1)} %slice_bitcast_fusion.2.refs_2_, bf16[16,1792]{1,0:T(8,128)(2,1)S(1)} %collective-permute-done.13.refs_3_, ...), custom_call_target="tpu_custom_call" | custom-call | tf_op jit(solution)/shard_map/finish/pallas_call | solution.py:351
  (31 shorter events, 0.4 us)
Async XLA Ops:
  0.6 15.1 %collective-permute-start = (bf16[16,3584]{1,0:T(8,128)(2,1)}, bf16[16,3584]{1,0:T(8,128)(2,1)S(1)}, u32[]{:S(2)}, u32[]{:S(2)}) collective-permute-start(bf16[16,3584]{1,0:T(8,128)(2,1)} %refs_0_.1), channel_id=1, source_target_pairs={{0,1},{1,0},{2,3},{3,2},{4,5},{5,4},{6,7},{7,6},{8,9},{9,8},{10,11... | collective-permute-start | bytes 344072 | tf_op jit(solution)/shard_map/ppermute | solution.py:366
  3.7 12.1 %collective-permute-start.1 = (bf16[16,3584]{1,0:T(8,128)(2,1)}, bf16[16,3584]{1,0:T(8,128)(2,1)S(1)}, u32[]{:S(2)}, u32[]{:S(2)}) collective-permute-start(bf16[16,3584]{1,0:T(8,128)(2,1)} %refs_0_.1), channel_id=1, source_target_pairs={{0,2},{1,3},{2,0},{3,1},{4,6},{5,7},{6,4},{7,5},{8,10},{9,11},{10,... | collective-permute-start | bytes 344072 | tf_op jit(solution)/shard_map/ppermute | solution.py:366
  6.3 9.5 %collective-permute-start.2 = (bf16[16,3584]{1,0:T(8,128)(2,1)}, bf16[16,3584]{1,0:T(8,128)(2,1)S(1)}, u32[]{:S(2)}, u32[]{:S(2)}) collective-permute-start(bf16[16,3584]{1,0:T(8,128)(2,1)} %refs_0_.1), channel_id=1, source_target_pairs={{0,3},{1,2},{2,1},{3,0},{4,7},{5,6},{6,5},{7,4},{8,11},{9,10},{10,... | collective-permute-start | bytes 344072 | tf_op jit(solution)/shard_map/ppermute | solution.py:366
  12.0 3.8 %copy-start = (bf16[16,3584]{1,0:T(8,128)(2,1)S(1)}, bf16[16,3584]{1,0:T(8,128)(2,1)}, u32[]{:S(2)}) copy-start(bf16[16,3584]{1,0:T(8,128)(2,1)} %refs_0_.1) | copy-start | bytes 344068
  15.8 8.1 %collective-permute-start.3 = (bf16[64,3712]{1,0:T(8,128)(2,1)S(1)}, bf16[64,3712]{1,0:T(8,128)(2,1)S(1)}, u32[]{:S(2)}, u32[]{:S(2)}) collective-permute-start(bf16[64,3712]{1,0:T(8,128)(2,1)S(1)} %join.1.refs_1_.refs_0_), channel_id=1, source_target_pairs={{0,4},{4,0},{8,12},{12,8},{1,5},{5,1},{9,13},{13,9},{2,6},{6,2},{1... | collective-permute-start | bytes 1425416 | tf_op jit(solution)/shard_map/ppermute | solution.py:366
  15.9 13.3 %collective-permute-start.4 = (bf16[64,3712]{1,0:T(8,128)(2,1)S(1)}, bf16[64,3712]{1,0:T(8,128)(2,1)S(1)}, u32[]{:S(2)}, u32[]{:S(2)}) collective-permute-start(bf16[64,3712]{1,0:T(8,128)(2,1)S(1)} %join.1.refs_1_.refs_0_), channel_id=1, source_target_pairs={{0,8},{4,12},{8,0},{12,4},{1,9},{5,13},{9,1},{13,5},{2,10},{6,14},... | collective-permute-start | bytes 1425416 | tf_op jit(solution)/shard_map/ppermute | solution.py:366
  29.2 1.9 %collective-permute-start.5 = (bf16[64,3712]{1,0:T(8,128)(2,1)S(1)}, bf16[64,3712]{1,0:T(8,128)(2,1)S(1)}, u32[]{:S(2)}, u32[]{:S(2)}) collective-permute-start(bf16[64,3712]{1,0:T(8,128)(2,1)S(1)} %pass_on.1.refs_0_.refs_3_), channel_id=1, source_target_pairs={{0,4},{4,0},{8,12},{12,8},{1,5},{5,1},{9,13},{13,9},{2,6},{6,2},{1... | collective-permute-start | bytes 1425416 | tf_op jit(solution)/shard_map/ppermute | solution.py:366
  41.5 2.6 %copy-start.2 = (f32[3584]{0:T(1024)S(1)}, f32[3584]{0:T(1024)}, u32[]{:S(2)}) copy-start(f32[3584]{0:T(1024)} %param.17) | copy-start | bytes 43012
  43.9 3.0 %collective-permute-start.6 = (bf16[128,1792]{1,0:T(8,128)(2,1)S(1)}, bf16[128,1792]{1,0:T(8,128)(2,1)S(1)}, u32[]{:S(2)}, u32[]{:S(2)}) collective-permute-start(bf16[128,1792]{1,0:T(8,128)(2,1)S(1)} %slice.75), channel_id=1, source_target_pairs={{0,4},{4,0},{8,12},{12,8},{1,5},{5,1},{9,13},{13,9},{2,6},{6,2},{1... | collective-permute-start | bytes 1376264 | tf_op jit(solution)/shard_map/ppermute | solution.py:366
  46.6 2.3 %collective-permute-start.10 = (bf16[128,1792]{1,0:T(8,128)(2,1)S(1)}, bf16[128,1792]{1,0:T(8,128)(2,1)S(1)}, u32[]{:S(2)}, u32[]{:S(2)}) collective-permute-start(bf16[128,1792]{1,0:T(8,128)(2,1)S(1)} %slice.83), channel_id=1, source_target_pairs={{0,4},{4,0},{8,12},{12,8},{1,5},{5,1},{9,13},{13,9},{2,6},{6,2},{1... | collective-permute-start | bytes 1376264 | tf_op jit(solution)/shard_map/ppermute | solution.py:366
  47.1 20.6 %copy-start.1 = (s32[8]{0:T(128)S(1)}, s32[8]{0:T(128)}, u32[]{:S(2)}) copy-start(s32[8]{0:T(128)} %param.12) | copy-start | bytes 100
  47.1 7.7 %collective-permute-start.7 = (bf16[2,2,16,1792]{3,2,0,1:T(8,128)(2,1)S(1)}, bf16[2,2,16,1792]{3,2,0,1:T(8,128)(2,1)S(1)}, u32[]{:S(2)}, u32[]{:S(2)}) collective-permute-start(bf16[2,2,16,1792]{3,2,0,1:T(8,128)(2,1)S(1)} %fusion.4), channel_id=1, source_target_pairs={{0,1},{1,0},{2,3},{3,2},{4,5},{5,4},{6,7},{7,6},{8,9},{9,8},{10,11... | collective-permute-start | bytes 688136 | tf_op jit(solution)/shard_map/ppermute | solution.py:366
  48.9 7.8 %collective-permute-start.11 = (bf16[1,4,16,1792]{3,2,1,0:T(8,128)(2,1)S(1)}, bf16[1,4,16,1792]{3,2,1,0:T(8,128)(2,1)S(1)}, u32[]{:S(2)}, u32[]{:S(2)}) collective-permute-start(bf16[1,4,16,1792]{3,2,1,0:T(8,128)(2,1)S(1)} %fusion.3), channel_id=1, source_target_pairs={{0,8},{4,12},{8,0},{12,4},{1,9},{5,13},{9,1},{13,5},{2,10},{6,14},... | collective-permute-start | bytes 688136 | tf_op jit(solution)/shard_map/ppermute | solution.py:366
  54.9 4.9 %collective-permute-start.8 = (bf16[1,2,16,1792]{3,2,1,0:T(8,128)(2,1)S(1)}, bf16[1,2,16,1792]{3,2,1,0:T(8,128)(2,1)S(1)}, u32[]{:S(2)}, u32[]{:S(2)}) collective-permute-start(bf16[1,2,16,1792]{3,2,1,0:T(8,128)(2,1)S(1)} %fusion.7), channel_id=1, source_target_pairs={{0,8},{4,12},{8,0},{12,4},{1,9},{5,13},{9,1},{13,5},{2,10},{6,14},... | collective-permute-start | bytes 344072 | tf_op jit(solution)/shard_map/ppermute | solution.py:366
  56.8 5.8 %collective-permute-start.12 = (bf16[2,16,1792]{2,1,0:T(8,128)(2,1)S(1)}, bf16[2,16,1792]{2,1,0:T(8,128)(2,1)S(1)}, u32[]{:S(2)}, u32[]{:S(2)}) collective-permute-start(bf16[2,16,1792]{2,1,0:T(8,128)(2,1)S(1)} %fusion.8), channel_id=1, source_target_pairs={{0,1},{1,0},{2,3},{3,2},{4,5},{5,4},{6,7},{7,6},{8,9},{9,8},{10,11... | collective-permute-start | bytes 344072 | tf_op jit(solution)/shard_map/ppermute | solution.py:366
  59.8 5.4 %collective-permute-start.9 = (bf16[16,1792]{1,0:T(8,128)(2,1)S(1)}, bf16[16,1792]{1,0:T(8,128)(2,1)S(1)}, u32[]{:S(2)}, u32[]{:S(2)}) collective-permute-start(bf16[16,1792]{1,0:T(8,128)(2,1)S(1)} %fusion.9), channel_id=1, source_target_pairs={{0,2},{1,3},{2,0},{3,1},{4,6},{5,7},{6,4},{7,5},{8,10},{9,11},{10,... | collective-permute-start | bytes 172040 | tf_op jit(solution)/shard_map/ppermute | solution.py:366
  62.6 5.1 %collective-permute-start.13 = (bf16[16,1792]{1,0:T(8,128)(2,1)S(1)}, bf16[16,1792]{1,0:T(8,128)(2,1)S(1)}, u32[]{:S(2)}, u32[]{:S(2)}) collective-permute-start(bf16[16,1792]{1,0:T(8,128)(2,1)S(1)} %fusion.10), channel_id=1, source_target_pairs={{0,2},{1,3},{2,0},{3,1},{4,6},{5,7},{6,4},{7,5},{8,10},{9,11},{10,... | collective-permute-start | bytes 172040 | tf_op jit(solution)/shard_map/ppermute | solution.py:366

commit v6 on v5

--- a/solution.py
+++ b/solution.py
@@ -11,7 +11,7 @@
 ROT = 128
 CORES = 2
 SMALL_VMEM = 10 * 1024 * 1024
-EARLY = 2
+EARLY = 4
 HIDDEN_VMEM = 5 * 1024 * 1024
 
 
@@ -104,40 +104,69 @@
     return out[: len(experts)], out[len(experts)], out[len(experts) + 1 :]
 
 
-def pass_kernel(value, *refs):
-    refs[-1][...] = value[...]
-
-
-def pass_on(value, after):
+def pass_kernel(n_pieces, *refs):
+    out = refs[-1]
+    base = 0
+    for piece in refs[:n_pieces]:
+        out[base : base + piece.shape[0], :] = piece[...]
+        base += piece.shape[0]
+
+
+def pass_on(pieces, after):
+    rows = sum(piece.shape[0] for piece in pieces)
     return pl.pallas_call(
-        pass_kernel,
-        in_specs=[pl.BlockSpec(memory_space=pltpu.VMEM)]
+        functools.partial(pass_kernel, len(pieces)),
+        in_specs=[pl.BlockSpec(memory_space=pltpu.VMEM)] * len(pieces)
         + [pl.BlockSpec(memory_space=pl.ANY)] * len(after),
         out_specs=pl.BlockSpec(memory_space=pltpu.VMEM),
-        out_shape=vmem(value.shape, value.dtype),
+        out_shape=vmem((rows, pieces[0].shape[1]), pieces[0].dtype),
         compiler_params=pltpu.CompilerParams(vmem_limit_bytes=HIDDEN_VMEM),
         cost_estimate=pl.CostEstimate(flops=0, bytes_accessed=1024, transcendentals=0),
         name="pass_on",
-    )(value, *after)
+    )(*pieces, *after)
+
+
+def pack_kernel(rows, lanes, out):
+    out[:, : rows.shape[1]] = rows[...]
+    out[:, rows.shape[1] :] = lanes[...]
+
+
+def pack(rows, lanes):
+    whole = pl.BlockSpec(memory_space=pltpu.VMEM)
+    return pl.pallas_call(
+        pack_kernel,
+        in_specs=[whole] * 2,
+        out_specs=whole,
+        out_shape=vmem((rows.shape[0], rows.shape[1] + lanes.shape[1]), rows.dtype),
+        compiler_params=pltpu.CompilerParams(vmem_limit_bytes=HIDDEN_VMEM),
+        cost_estimate=pl.CostEstimate(flops=0, bytes_accessed=1024, transcendentals=0),
+        name="pack",
+    )(rows, lanes)
 
 
 def join_kernel(n_pieces, *refs):
-    lanes, out = refs[n_pieces], refs[-1]
+    lanes, out, others = refs[n_pieces], refs[-2], refs[-1]
     feature_len = refs[0].shape[1]
+    own = out.shape[0] - others.shape[0]
     base = 0
     for piece in refs[:n_pieces]:
         out[base : base + piece.shape[0], :feature_len] = piece[...]
+        if base:
+            others[base - own : base - own + piece.shape[0], :feature_len] = piece[...]
         base += piece.shape[0]
     out[:, feature_len:] = lanes[...]
+    others[:, feature_len:] = lanes[own:, :]
 
 
 def join(pieces, lanes, after):
     whole = pl.BlockSpec(memory_space=pltpu.VMEM)
+    rows, own = lanes.shape[0], pieces[0].shape[0]
+    columns = pieces[0].shape[1] + lanes.shape[1]
     return pl.pallas_call(
         functools.partial(join_kernel, len(pieces)),
         in_specs=[whole] * (len(pieces) + 1) + [pl.BlockSpec(memory_space=pl.ANY)] * len(after),
-        out_specs=whole,
-        out_shape=vmem((lanes.shape[0], pieces[0].shape[1] + lanes.shape[1]), lanes.dtype),
+        out_specs=[whole] * 2,
+        out_shape=[vmem((rows, columns), lanes.dtype), vmem((rows - own, columns), lanes.dtype)],
         compiler_params=pltpu.CompilerParams(vmem_limit_bytes=HIDDEN_VMEM),
         cost_estimate=pl.CostEstimate(flops=0, bytes_accessed=1024, transcendentals=0),
         name="join",
@@ -423,16 +452,18 @@
 
     early = (n_local + EARLY - 1) // EARLY
     from_z = [exchange(tokens, "narrow", flip) for flip in range(1, narrow_count)]
+    packed_own = pack(tokens, lanes[:own_rows])
+    own_from_x = [exchange(packed_own, "expert", flip * CORES) for flip in range(1, chips)]
     weights, done, own = apart(
-        packed, [0], feature_len, inner, [lanes, select, signs, index], shared
+        packed, [0], feature_len, inner, [lanes, select, signs, index, packed_own], shared
     )
     for expert in range(1, early):
         more, done, _ = apart(packed, [expert], feature_len, inner, [done])
         weights = weights + more
     if own:
         shared_in = own[0].transpose(0, 2, 1, 3).reshape(feature_len, -1)
-    along_z = join([tokens] + from_z, lanes, [done])
-    from_x = [exchange(along_z, "expert", flip * CORES) for flip in range(1, chips)]
+    along_z, others = join([tokens] + from_z, lanes, [done] + own_from_x)
+    from_x = [exchange(others, "expert", flip * CORES) for flip in range(1, chips)]
     near = exchange(along_z, "expert", 1)
     after = [along_z]
     if n_local > early:
@@ -442,7 +473,7 @@
         weights = weights + late
         after = [done]
     first = first_rows([along_z, near], signs, feature_len)
-    from_x = [pass_on(part, after + [first]) for part in from_x]
+    from_x = [pass_on([own, part], after + [first]) for own, part in zip(own_from_x, from_x)]
     from_both = [exchange(part, "expert", 1) for part in from_x]
     second = first_rows(from_x, signs, feature_len)
 

time: 68.6 us -> 67.1 us (0.978)
  waiting for transfers between devices: 14.1 us -> 11.9 us
  Pallas kernels: 31 us -> 29.6 us
  starting transfers between devices: 19.7 us -> 20.9 us
  local copies, waits for them, and re-layouts: 1.1 us -> 1.99 us
    ppermute x14 -> x15, waiting for transfers between devices: 14.1 us -> 11.9 us  [exchange(): lax.ppermute(value, axis, [(i, i ^ flip) for i in range(lax.axis_size(axi...]
    pallas_call x3 -> x2, Pallas kernels: 13.5 us -> 11.9 us  [apart(): pl.pallas_call(functools.partial(apart_kernel, experts, rows, chunk, 1 +...]
    ppermute x14 -> x15, starting transfers between devices: 19.7 us -> 20.9 us  [exchange(): lax.ppermute(value, axis, [(i, i ^ flip) for i in range(lax.axis_size(axi...]
    unnamed x7 -> x9, local copies, waits for them, and re-layouts: 0.26 us -> 1.15 us
  transfers between devices with their start and end apart: 14 -> 15, of which waited for: 6 -> 7; matrix products, arithmetic and copies ran while one was open for 4% -> 4% of each run, Pallas kernels for 26% -> 24%
where the time goes in v6:
time: 67.1 us; the launch traced here: 66.9 us
  Pallas kernels  29.6 us (44%)
  starting transfers between devices  20.9 us (31%)
  waiting for transfers between devices  11.9 us (18%)
  local copies, waits for them, and re-layouts  1.99 us (3%)
  other arithmetic  1.56 us (2%)
  between operations  0.95 us (1%)
    ppermute x15, starting transfers between devices, exchange(): lax.ppermute(value, axis, [(i, i ^ flip) for i in range(lax.axis_size(axi...  20.9 us
    pallas_call x2, Pallas kernels, apart(): pl.pallas_call(functools.partial(apart_kernel, experts, rows, chunk, 1 +...  11.9 us
    ppermute x15, waiting for transfers between devices, exchange(): lax.ppermute(value, axis, [(i, i ^ flip) for i in range(lax.axis_size(axi...  11.9 us
    pallas_call x2, Pallas kernels, hidden_rows(): pl.pallas_call(functools.partial(hidden_kernel, experts), in_specs=[whole...  8.24 us
    pallas_call x2, Pallas kernels, down_rows(): pl.pallas_call(functools.partial(down_kernel, start, tile, len(hidden)),...  4.7 us
    pallas_call x1, Pallas kernels, rest_rows(): pl.pallas_call(functools.partial(rest_kernel, len(pieces), n_chips), in_s...  2.14 us
    pallas_call x2, Pallas kernels, first_rows(): pl.pallas_call(functools.partial(first_kernel, len(pieces)), in_specs=[wh...  1.76 us
  transfers between devices with their start and end apart: 15, of which 7 were waited for; matrix products, arithmetic and copies ran while one was open for 4% of the time, Pallas kernels for 24%

profile of v6, /device:TPU:0, one launch (start us, length us, event | category | flops | bytes accessed | tf_op | source)
XLA Modules:
  0.0 66.9 jit_solution(512633328955349288)
XLA Ops:
  0.6 3.1 %collective-permute-start = (bf16[16,3584]{1,0:T(8,128)(2,1)}, bf16[16,3584]{1,0:T(8,128)(2,1)S(1)}, u32[]{:S(2)}, u32[]{:S(2)}) collective-permute-start(bf16[16,3584]{1,0:T(8,128)(2,1)} %refs_0_.1), channel_id=1, source_target_pairs={{0,1},{1,0},{2,3},{3,2},{4,5},{5,4},{6,7},{7,6},{8,9},{9,8},{10,11... | collective-permute-start | bytes 344072 | tf_op jit(solution)/shard_map/ppermute | solution.py:395
  3.7 2.6 %collective-permute-start.1 = (bf16[16,3584]{1,0:T(8,128)(2,1)}, bf16[16,3584]{1,0:T(8,128)(2,1)S(1)}, u32[]{:S(2)}, u32[]{:S(2)}) collective-permute-start(bf16[16,3584]{1,0:T(8,128)(2,1)} %refs_0_.1), channel_id=1, source_target_pairs={{0,2},{1,3},{2,0},{3,1},{4,6},{5,7},{6,4},{7,5},{8,10},{9,11},{10,... | collective-permute-start | bytes 344072 | tf_op jit(solution)/shard_map/ppermute | solution.py:395
  6.3 0.7 %select_reduce_fusion = f32[64,16]{0,1:T(8,128)S(1)} fusion(f32[64,8]{0,1:T(8,128)} %param.11, s32[64,8]{0,1:T(8,128)} %param.10), kind=kLoop, calls=%fused_computation.27 | loop fusion | flops 23552 | bytes 8192 | tf_op jit(solution)/shard_map/reduce_sum | solution.py:419
  7.0 0.1 copy.28
  7.2 0.1 pad_maximum_fusion
  7.3 0.6 gather_fusion
  7.8 0.0 copy-start
  7.8 0.9 %copy-done = bf16[16,3584]{1,0:T(8,128)(2,1)S(1)} copy-done((bf16[16,3584]{1,0:T(8,128)(2,1)S(1)}, bf16[16,3584]{1,0:T(8,128)(2,1)}, u32[]{:S(2)}) %copy-start) | copy-done | bytes 114712
  8.7 1.8 %collective-permute-start.3 = (bf16[16,3712]{1,0:T(8,128)(2,1)S(1)}, bf16[16,3712]{1,0:T(8,128)(2,1)S(1)}, u32[]{:S(2)}, u32[]{:S(2)}) collective-permute-start(bf16[16,3712]{1,0:T(8,128)(2,1)S(1)} %pack.1.refs_7_), channel_id=1, source_target_pairs={{0,8},{4,12},{8,0},{12,4},{1,9},{5,13},{9,1},{13,5},{2,10},{6,14},... | collective-permute-start | bytes 356360 | tf_op jit(solution)/shard_map/ppermute | solution.py:395
  10.6 0.3 select_convert_fusion.refs_5_.refs_2_.refs_1_
  10.9 0.1 fusion.12.refs_4_.refs_2_
  11.0 3.8 %apart.2 = (bf16[2,3584,512]{2,1,0:T(8,128)(2,1)S(1)}, f32[8,128]{1,0:T(8,128)S(1)}, bf16[3584,1,2,128]{3,2,1,0:T(2,128)(2,1)S(1)}) custom-call(bf16[4,28672,128]{2,1,0:T(8,128)(2,1)} %bitcast.73, s32[1]{0:T(128)} %bitcast.refs_1_.refs_6_.refs_0_, bf16[3584,4,2,128]{3,2,1,0:T(2,128)(2,1)} %bitcast.75, bf16[64,128]{1,0:T(8,128)(2,1)S(1)} %bitcast.70, ...), custom_call_target="tpu_custom_call" | custom-call | bytes 1024 | tf_op jit(solution)/shard_map/apart/pallas_call | solution.py:89
  14.7 0.0 collective-permute-done.refs_1_
  14.7 0.9 %collective-permute-done.1.refs_2_ = bf16[16,3584]{1,0:T(8,128)(2,1)S(1)} collective-permute-done((bf16[16,3584]{1,0:T(8,128)(2,1)}, bf16[16,3584]{1,0:T(8,128)(2,1)S(1)}, u32[]{:S(2)}, u32[]{:S(2)}) %collective-permute-start.1) | collective-permute-done | bytes 114720 | tf_op jit(solution)/shard_map/ppermute | solution.py:395
  15.6 0.0 collective-permute-done.2.refs_3_
  15.6 0.0 collective-permute-done.3.refs_6_.refs_0_
  15.6 0.1 join.1
  15.7 0.1 collective-permute-start.4
  15.8 1.6 %collective-permute-start.5 = (bf16[48,3712]{1,0:T(8,128)(2,1)S(1)}, bf16[48,3712]{1,0:T(8,128)(2,1)S(1)}, u32[]{:S(2)}, u32[]{:S(2)}) collective-permute-start(bf16[48,3712]{1,0:T(8,128)(2,1)S(1)} %get-tuple-element.25), channel_id=1, source_target_pairs={{0,8},{4,12},{8,0},{12,4},{1,9},{5,13},{9,1},{13,5},{2,10},{6,14},... | collective-permute-start | bytes 1069064 | tf_op jit(solution)/shard_map/ppermute | solution.py:395
  17.4 0.2 copy.56
  17.6 8.2 %apart.3 = (bf16[2,3584,512]{2,1,0:T(8,128)(2,1)S(1)}, bf16[2,3584,512]{2,1,0:T(8,128)(2,1)S(1)}, bf16[2,3584,512]{2,1,0:T(8,128)(2,1)S(1)}, f32[8,128]{1,0:T(8,128)S(1)}) custom-call(bf16[4,28672,128]{2,1,0:T(8,128)(2,1)} %bitcast.74, bf16[64,3712]{1,0:T(8,128)(2,1)S(1)} %get-tuple-element.24.refs_1_.refs_0_, bf16[3584,256]{1,0:T(8,128)(2,1)S(1)} %bitcast.67), custom_call_target="tpu_custom_call" | custom-call | bytes 1024 | tf_op jit(solution)/shard_map/apart/pallas_call | solution.py:89
  25.8 1.1 %first_rows.2.refs_3_.refs_6_ = bf16[128,3584]{1,0:T(8,128)(2,1)S(1)} custom-call(bf16[64,3712]{1,0:T(8,128)(2,1)S(1)} %get-tuple-element.24.refs_1_.refs_0_, bf16[64,3712]{1,0:T(8,128)(2,1)S(1)} %collective-permute-done.4.refs_1_.refs_2_, bf16[256,256]{1,0:T(8,128)(2,1)S(1)} %select_convert_fusion.refs_5_.refs_2_.refs_1_), custom_call_target="tpu_custom_call" | custom-call | bytes 1024 | tf_op jit(solution)/shard_map/first_rows/pallas_call | solution.py:203
  27.0 0.2 collective-permute-start.6
  27.2 0.7 first_rows.3.refs_7_
  27.8 1.0 %collective-permute-done.6.refs_4_ = bf16[64,3712]{1,0:T(8,128)(2,1)S(1)} collective-permute-done((bf16[64,3712]{1,0:T(8,128)(2,1)S(1)}, bf16[64,3712]{1,0:T(8,128)(2,1)S(1)}, u32[]{:S(2)}, u32[]{:S(2)}) %collective-permute-start.6) | collective-permute-done | bytes 475168 | tf_op jit(solution)/shard_map/ppermute | solution.py:395
  28.9 2.1 %rest_rows.1 = (bf16[256,3584]{1,0:T(8,128)(2,1)S(1)}, bf16[256,128]{1,0:T(8,128)(2,1)S(1)}, f32[256,128]{1,0:T(8,128)S(1)}, bf16[128,3584]{1,0:T(8,128)(2,1)S(1)}) custom-call(s32[1]{0:T(128)} %bitcast.refs_1_.refs_6_.refs_0_, bf16[64,3712]{1,0:T(8,128)(2,1)S(1)} %get-tuple-element.24.refs_1_.refs_0_, ...), custom_call_target="tpu_custom_call" | custom-call | tf_op jit(solution)/shard_map/rest_rows/pallas_call | solution.py:253
  31.0 4.2 %hidden_rows.2 = (bf16[256,1024]{1,0:T(8,128)(2,1)S(1)}, bf16[512,3584]{1,0:T(8,128)(2,1)S(1)}, bf16[512,3584]{1,0:T(8,128)(2,1)S(1)}) custom-call(bf16[256,3584]{1,0:T(8,128)(2,1)S(1)} %get-tuple-element.28.refs_0_, f32[256,128]{1,0:T(8,128)S(1)} %get-tuple-element.29.refs_1_, f32[4,128]{1,0:T(4,128)S(1)} %fusion.12.refs_4_.refs_2_, ...), custom_call_target="tpu_custom_call" | custom-call | tf_op jit(solution)/shard_map/hidden_rows/pallas_call | solution.py:301
  35.2 4.0 %hidden_rows.3 = (bf16[256,1024]{1,0:T(8,128)(2,1)S(1)}, bf16[512,3584]{1,0:T(8,128)(2,1)S(1)}, bf16[512,3584]{1,0:T(8,128)(2,1)S(1)}) custom-call(bf16[256,3584]{1,0:T(8,128)(2,1)S(1)} %get-tuple-element.28.refs_0_, f32[256,128]{1,0:T(8,128)S(1)} %get-tuple-element.29.refs_1_, f32[4,128]{1,0:T(4,128)S(1)} %fusion.12.refs_4_.refs_2_, ...), custom_call_target="tpu_custom_call" | custom-call | tf_op jit(solution)/shard_map/hidden_rows/pallas_call | solution.py:301
  39.3 0.0 copy-start.3
  39.3 2.3 %down_rows.2 = bf16[256,1792]{1,0:T(8,128)(2,1)S(1)} custom-call(bf16[256,1024]{1,0:T(8,128)(2,1)S(1)} %get-tuple-element.32.refs_0_, bf16[256,1024]{1,0:T(8,128)(2,1)S(1)} %get-tuple-element.35.refs_1_, bf16[256,128]{1,0:T(8,128)(2,1)S(1)} %get-tuple-element.36.refs_2_, bf16[128,3584]{1,0:T(8,128)(2,1)S(1)} %get-tuple-element.37.refs_3_, ...), custom_call_target="tpu_custom_call" | custom-call | tf_op jit(solution)/shard_map/down_rows/pallas_call | solution.py:344
  41.7 0.2 collective-permute-start.7
  41.9 2.4 %down_rows.3 = bf16[256,1792]{1,0:T(8,128)(2,1)S(1)} custom-call(bf16[256,1024]{1,0:T(8,128)(2,1)S(1)} %get-tuple-element.32.refs_0_, bf16[256,1024]{1,0:T(8,128)(2,1)S(1)} %get-tuple-element.35.refs_1_, bf16[256,128]{1,0:T(8,128)(2,1)S(1)} %get-tuple-element.36.refs_2_, bf16[128,3584]{1,0:T(8,128)(2,1)S(1)} %get-tuple-element.37.refs_3_, ...), custom_call_target="tpu_custom_call" | custom-call | tf_op jit(solution)/shard_map/down_rows/pallas_call | solution.py:344
  44.3 0.4 collective-permute-start.11
  44.7 0.1 convert_add_fusion.1
  44.8 0.0 copy-start.2
  44.9 1.8 %collective-permute-start.8 = (bf16[2,2,16,1792]{3,2,0,1:T(8,128)(2,1)S(1)}, bf16[2,2,16,1792]{3,2,0,1:T(8,128)(2,1)S(1)}, u32[]{:S(2)}, u32[]{:S(2)}) collective-permute-start(bf16[2,2,16,1792]{3,2,0,1:T(8,128)(2,1)S(1)} %fusion.4), channel_id=1, source_target_pairs={{0,1},{1,0},{2,3},{3,2},{4,5},{5,4},{6,7},{7,6},{8,9},{9,8},{10,11... | collective-permute-start | bytes 688136 | tf_op jit(solution)/shard_map/ppermute | solution.py:395
  46.7 0.1 convert_add_fusion
  46.9 1.2 %collective-permute-start.12 = (bf16[1,4,16,1792]{3,2,1,0:T(8,128)(2,1)S(1)}, bf16[1,4,16,1792]{3,2,1,0:T(8,128)(2,1)S(1)}, u32[]{:S(2)}, u32[]{:S(2)}) collective-permute-start(bf16[1,4,16,1792]{3,2,1,0:T(8,128)(2,1)S(1)} %fusion.3), channel_id=1, source_target_pairs={{0,8},{4,12},{8,0},{12,4},{1,9},{5,13},{9,1},{13,5},{2,10},{6,14},... | collective-permute-start | bytes 688136 | tf_op jit(solution)/shard_map/ppermute | solution.py:395
  48.0 4.6 %collective-permute-done.8 = bf16[2,2,16,1792]{3,2,0,1:T(8,128)(2,1)S(1)} collective-permute-done((bf16[2,2,16,1792]{3,2,0,1:T(8,128)(2,1)S(1)}, bf16[2,2,16,1792]{3,2,0,1:T(8,128)(2,1)S(1)}, u32[]{:S(2)}, u32[]{:S(2)}) %collective-permute-start.8) | collective-permute-done | bytes 229408 | tf_op jit(solution)/shard_map/ppermute | solution.py:395
  52.7 1.1 %collective-permute-start.9 = (bf16[1,2,16,1792]{3,2,1,0:T(8,128)(2,1)S(1)}, bf16[1,2,16,1792]{3,2,1,0:T(8,128)(2,1)S(1)}, u32[]{:S(2)}, u32[]{:S(2)}) collective-permute-start(bf16[1,2,16,1792]{3,2,1,0:T(8,128)(2,1)S(1)} %fusion.7), channel_id=1, source_target_pairs={{0,8},{4,12},{8,0},{12,4},{1,9},{5,13},{9,1},{13,5},{2,10},{6,14},... | collective-permute-start | bytes 344072 | tf_op jit(solution)/shard_map/ppermute | solution.py:395
  53.9 0.4 collective-permute-done.12
  54.4 1.8 %collective-permute-start.13 = (bf16[2,16,1792]{2,1,0:T(8,128)(2,1)S(1)}, bf16[2,16,1792]{2,1,0:T(8,128)(2,1)S(1)}, u32[]{:S(2)}, u32[]{:S(2)}) collective-permute-start(bf16[2,16,1792]{2,1,0:T(8,128)(2,1)S(1)} %fusion.8), channel_id=1, source_target_pairs={{0,1},{1,0},{2,3},{3,2},{4,5},{5,4},{6,7},{7,6},{8,9},{9,8},{10,11... | collective-permute-start | bytes 344072 | tf_op jit(solution)/shard_map/ppermute | solution.py:395
  56.2 1.4 %collective-permute-done.9 = bf16[1,2,16,1792]{3,2,1,0:T(8,128)(2,1)S(1)} collective-permute-done((bf16[1,2,16,1792]{3,2,1,0:T(8,128)(2,1)S(1)}, bf16[1,2,16,1792]{3,2,1,0:T(8,128)(2,1)S(1)}, u32[]{:S(2)}, u32[]{:S(2)}) %collective-permute-start.9) | collective-permute-done | bytes 114720 | tf_op jit(solution)/shard_map/ppermute | solution.py:395
  57.6 2.8 %collective-permute-start.10 = (bf16[16,1792]{1,0:T(8,128)(2,1)S(1)}, bf16[16,1792]{1,0:T(8,128)(2,1)S(1)}, u32[]{:S(2)}, u32[]{:S(2)}) collective-permute-start(bf16[16,1792]{1,0:T(8,128)(2,1)S(1)} %fusion.9), channel_id=1, source_target_pairs={{0,2},{1,3},{2,0},{3,1},{4,6},{5,7},{6,4},{7,5},{8,10},{9,11},{10,... | collective-permute-start | bytes 172040 | tf_op jit(solution)/shard_map/ppermute | solution.py:395
  60.5 2.2 %collective-permute-start.14 = (bf16[16,1792]{1,0:T(8,128)(2,1)S(1)}, bf16[16,1792]{1,0:T(8,128)(2,1)S(1)}, u32[]{:S(2)}, u32[]{:S(2)}) collective-permute-start(bf16[16,1792]{1,0:T(8,128)(2,1)S(1)} %fusion.10), channel_id=1, source_target_pairs={{0,2},{1,3},{2,0},{3,1},{4,6},{5,7},{6,4},{7,5},{8,10},{9,11},{10,... | collective-permute-start | bytes 172040 | tf_op jit(solution)/shard_map/ppermute | solution.py:395
  62.7 1.7 %collective-permute-done.10.refs_1_ = bf16[16,1792]{1,0:T(8,128)(2,1)S(1)} collective-permute-done((bf16[16,1792]{1,0:T(8,128)(2,1)S(1)}, bf16[16,1792]{1,0:T(8,128)(2,1)S(1)}, u32[]{:S(2)}, u32[]{:S(2)}) %collective-permute-start.10) | collective-permute-done | bytes 57376 | tf_op jit(solution)/shard_map/ppermute | solution.py:395
  64.4 1.8 %collective-permute-done.14.refs_3_ = bf16[16,1792]{1,0:T(8,128)(2,1)S(1)} collective-permute-done((bf16[16,1792]{1,0:T(8,128)(2,1)S(1)}, bf16[16,1792]{1,0:T(8,128)(2,1)S(1)}, u32[]{:S(2)}, u32[]{:S(2)}) %collective-permute-start.14) | collective-permute-done | bytes 57376 | tf_op jit(solution)/shard_map/ppermute | solution.py:395
  66.2 0.7 %finish.1 = (bf16[16,3584]{1,0:T(8,128)(2,1)}, f32[1,8]{1,0:T(1,128)}) custom-call(f32[16,1792]{1,0:T(8,128)S(1)} %slice_bitcast_fusion.3.refs_0_, bf16[16,1792]{1,0:T(8,128)(2,1)S(1)} %collective-permute-done.10.refs_1_, f32[16,1792]{1,0:T(8,128)S(1)} %slice_bitcast_fusion.2.refs_2_, bf16[16,1792]{1,0:T(8,128)(2,1)S(1)} %collective-permute-done.14.refs_3_, ...), custom_call_target="tpu_custom_call" | custom-call | tf_op jit(solution)/shard_map/finish/pallas_call | solution.py:380
  (36 shorter events, 0.4 us)
Async XLA Ops:
  0.6 14.1 %collective-permute-start = (bf16[16,3584]{1,0:T(8,128)(2,1)}, bf16[16,3584]{1,0:T(8,128)(2,1)S(1)}, u32[]{:S(2)}, u32[]{:S(2)}) collective-permute-start(bf16[16,3584]{1,0:T(8,128)(2,1)} %refs_0_.1), channel_id=1, source_target_pairs={{0,1},{1,0},{2,3},{3,2},{4,5},{5,4},{6,7},{7,6},{8,9},{9,8},{10,11... | collective-permute-start | bytes 344072 | tf_op jit(solution)/shard_map/ppermute | solution.py:395
  3.7 11.9 %collective-permute-start.1 = (bf16[16,3584]{1,0:T(8,128)(2,1)}, bf16[16,3584]{1,0:T(8,128)(2,1)S(1)}, u32[]{:S(2)}, u32[]{:S(2)}) collective-permute-start(bf16[16,3584]{1,0:T(8,128)(2,1)} %refs_0_.1), channel_id=1, source_target_pairs={{0,2},{1,3},{2,0},{3,1},{4,6},{5,7},{6,4},{7,5},{8,10},{9,11},{10,... | collective-permute-start | bytes 344072 | tf_op jit(solution)/shard_map/ppermute | solution.py:395
  6.3 9.3 %collective-permute-start.2 = (bf16[16,3584]{1,0:T(8,128)(2,1)}, bf16[16,3584]{1,0:T(8,128)(2,1)S(1)}, u32[]{:S(2)}, u32[]{:S(2)}) collective-permute-start(bf16[16,3584]{1,0:T(8,128)(2,1)} %refs_0_.1), channel_id=1, source_target_pairs={{0,3},{1,2},{2,1},{3,0},{4,7},{5,6},{6,5},{7,4},{8,11},{9,10},{10,... | collective-permute-start | bytes 344072 | tf_op jit(solution)/shard_map/ppermute | solution.py:395
  7.8 0.9 %copy-start = (bf16[16,3584]{1,0:T(8,128)(2,1)S(1)}, bf16[16,3584]{1,0:T(8,128)(2,1)}, u32[]{:S(2)}) copy-start(bf16[16,3584]{1,0:T(8,128)(2,1)} %refs_0_.1) | copy-start | bytes 344068
  8.7 6.9 %collective-permute-start.3 = (bf16[16,3712]{1,0:T(8,128)(2,1)S(1)}, bf16[16,3712]{1,0:T(8,128)(2,1)S(1)}, u32[]{:S(2)}, u32[]{:S(2)}) collective-permute-start(bf16[16,3712]{1,0:T(8,128)(2,1)S(1)} %pack.1.refs_7_), channel_id=1, source_target_pairs={{0,8},{4,12},{8,0},{12,4},{1,9},{5,13},{9,1},{13,5},{2,10},{6,14},... | collective-permute-start | bytes 356360 | tf_op jit(solution)/shard_map/ppermute | solution.py:395
  11.0 4.7 %copy-start.1 = (bf16[16,3584]{1,0:T(8,128)(2,1)S(1)}, bf16[16,3584]{1,0:T(8,128)(2,1)}, u32[]{:S(2)}) copy-start(bf16[16,3584]{1,0:T(8,128)(2,1)} %refs_0_.1) | copy-start | bytes 344068
  15.7 10.1 %collective-permute-start.4 = (bf16[64,3712]{1,0:T(8,128)(2,1)S(1)}, bf16[64,3712]{1,0:T(8,128)(2,1)S(1)}, u32[]{:S(2)}, u32[]{:S(2)}) collective-permute-start(bf16[64,3712]{1,0:T(8,128)(2,1)S(1)} %get-tuple-element.24.refs_1_.refs_0_), channel_id=1, source_target_pairs={{0,4},{4,0},{8,12},{12,8},{1,5},{5,1},{9,13},{13,9},{2,6},{6,2},{1... | collective-permute-start | bytes 1425416 | tf_op jit(solution)/shard_map/ppermute | solution.py:395
  15.8 11.1 %collective-permute-start.5 = (bf16[48,3712]{1,0:T(8,128)(2,1)S(1)}, bf16[48,3712]{1,0:T(8,128)(2,1)S(1)}, u32[]{:S(2)}, u32[]{:S(2)}) collective-permute-start(bf16[48,3712]{1,0:T(8,128)(2,1)S(1)} %get-tuple-element.25), channel_id=1, source_target_pairs={{0,8},{4,12},{8,0},{12,4},{1,9},{5,13},{9,1},{13,5},{2,10},{6,14},... | collective-permute-start | bytes 1069064 | tf_op jit(solution)/shard_map/ppermute | solution.py:395
  27.0 1.9 %collective-permute-start.6 = (bf16[64,3712]{1,0:T(8,128)(2,1)S(1)}, bf16[64,3712]{1,0:T(8,128)(2,1)S(1)}, u32[]{:S(2)}, u32[]{:S(2)}) collective-permute-start(bf16[64,3712]{1,0:T(8,128)(2,1)S(1)} %pass_on.1.refs_0_.refs_3_), channel_id=1, source_target_pairs={{0,4},{4,0},{8,12},{12,8},{1,5},{5,1},{9,13},{13,9},{2,6},{6,2},{1... | collective-permute-start | bytes 1425416 | tf_op jit(solution)/shard_map/ppermute | solution.py:395
  39.3 2.6 %copy-start.3 = (f32[3584]{0:T(1024)S(1)}, f32[3584]{0:T(1024)}, u32[]{:S(2)}) copy-start(f32[3584]{0:T(1024)} %param.17) | copy-start | bytes 43012
  41.7 3.1 %collective-permute-start.7 = (bf16[128,1792]{1,0:T(8,128)(2,1)S(1)}, bf16[128,1792]{1,0:T(8,128)(2,1)S(1)}, u32[]{:S(2)}, u32[]{:S(2)}) collective-permute-start(bf16[128,1792]{1,0:T(8,128)(2,1)S(1)} %slice.83), channel_id=1, source_target_pairs={{0,4},{4,0},{8,12},{12,8},{1,5},{5,1},{9,13},{13,9},{2,6},{6,2},{1... | collective-permute-start | bytes 1376264 | tf_op jit(solution)/shard_map/ppermute | solution.py:395
  44.3 2.4 %collective-permute-start.11 = (bf16[128,1792]{1,0:T(8,128)(2,1)S(1)}, bf16[128,1792]{1,0:T(8,128)(2,1)S(1)}, u32[]{:S(2)}, u32[]{:S(2)}) collective-permute-start(bf16[128,1792]{1,0:T(8,128)(2,1)S(1)} %slice.91), channel_id=1, source_target_pairs={{0,4},{4,0},{8,12},{12,8},{1,5},{5,1},{9,13},{13,9},{2,6},{6,2},{1... | collective-permute-start | bytes 1376264 | tf_op jit(solution)/shard_map/ppermute | solution.py:395
  44.8 21.4 %copy-start.2 = (s32[8]{0:T(128)S(1)}, s32[8]{0:T(128)}, u32[]{:S(2)}) copy-start(s32[8]{0:T(128)} %param.12) | copy-start | bytes 100
  44.9 7.8 %collective-permute-start.8 = (bf16[2,2,16,1792]{3,2,0,1:T(8,128)(2,1)S(1)}, bf16[2,2,16,1792]{3,2,0,1:T(8,128)(2,1)S(1)}, u32[]{:S(2)}, u32[]{:S(2)}) collective-permute-start(bf16[2,2,16,1792]{3,2,0,1:T(8,128)(2,1)S(1)} %fusion.4), channel_id=1, source_target_pairs={{0,1},{1,0},{2,3},{3,2},{4,5},{5,4},{6,7},{7,6},{8,9},{9,8},{10,11... | collective-permute-start | bytes 688136 | tf_op jit(solution)/shard_map/ppermute | solution.py:395
  46.9 7.5 %collective-permute-start.12 = (bf16[1,4,16,1792]{3,2,1,0:T(8,128)(2,1)S(1)}, bf16[1,4,16,1792]{3,2,1,0:T(8,128)(2,1)S(1)}, u32[]{:S(2)}, u32[]{:S(2)}) collective-permute-start(bf16[1,4,16,1792]{3,2,1,0:T(8,128)(2,1)S(1)} %fusion.3), channel_id=1, source_target_pairs={{0,8},{4,12},{8,0},{12,4},{1,9},{5,13},{9,1},{13,5},{2,10},{6,14},... | collective-permute-start | bytes 688136 | tf_op jit(solution)/shard_map/ppermute | solution.py:395
  52.7 4.9 %collective-permute-start.9 = (bf16[1,2,16,1792]{3,2,1,0:T(8,128)(2,1)S(1)}, bf16[1,2,16,1792]{3,2,1,0:T(8,128)(2,1)S(1)}, u32[]{:S(2)}, u32[]{:S(2)}) collective-permute-start(bf16[1,2,16,1792]{3,2,1,0:T(8,128)(2,1)S(1)} %fusion.7), channel_id=1, source_target_pairs={{0,8},{4,12},{8,0},{12,4},{1,9},{5,13},{9,1},{13,5},{2,10},{6,14},... | collective-permute-start | bytes 344072 | tf_op jit(solution)/shard_map/ppermute | solution.py:395
  54.4 6.1 %collective-permute-start.13 = (bf16[2,16,1792]{2,1,0:T(8,128)(2,1)S(1)}, bf16[2,16,1792]{2,1,0:T(8,128)(2,1)S(1)}, u32[]{:S(2)}, u32[]{:S(2)}) collective-permute-start(bf16[2,16,1792]{2,1,0:T(8,128)(2,1)S(1)} %fusion.8), channel_id=1, source_target_pairs={{0,1},{1,0},{2,3},{3,2},{4,5},{5,4},{6,7},{7,6},{8,9},{9,8},{10,11... | collective-permute-start | bytes 344072 | tf_op jit(solution)/shard_map/ppermute | solution.py:395
  57.6 6.8 %collective-permute-start.10 = (bf16[16,1792]{1,0:T(8,128)(2,1)S(1)}, bf16[16,1792]{1,0:T(8,128)(2,1)S(1)}, u32[]{:S(2)}, u32[]{:S(2)}) collective-permute-start(bf16[16,1792]{1,0:T(8,128)(2,1)S(1)} %fusion.9), channel_id=1, source_target_pairs={{0,2},{1,3},{2,0},{3,1},{4,6},{5,7},{6,4},{7,5},{8,10},{9,11},{10,... | collective-permute-start | bytes 172040 | tf_op jit(solution)/shard_map/ppermute | solution.py:395
  60.5 5.7 %collective-permute-start.14 = (bf16[16,1792]{1,0:T(8,128)(2,1)S(1)}, bf16[16,1792]{1,0:T(8,128)(2,1)S(1)}, u32[]{:S(2)}, u32[]{:S(2)}) collective-permute-start(bf16[16,1792]{1,0:T(8,128)(2,1)S(1)} %fusion.10), channel_id=1, source_target_pairs={{0,2},{1,3},{2,0},{3,1},{4,6},{5,7},{6,4},{7,5},{8,10},{9,11},{10,... | collective-permute-start | bytes 172040 | tf_op jit(solution)/shard_map/ppermute | solution.py:395

commit v7 on v6

--- a/solution.py
+++ b/solution.py
@@ -76,7 +76,7 @@
 
 def apart(packed, experts, feature_len, inner, after, shared=None):
     count = 2 * inner // 128
-    rows = feature_len // 4 if feature_len % 256 == 0 else feature_len
+    rows = feature_len // 8 if feature_len % 512 == 0 else feature_len
     chunk = 64 if rows % 64 == 0 else rows
     whole = pl.BlockSpec(memory_space=pltpu.VMEM)
     anywhere = pl.BlockSpec(memory_space=pl.ANY)
@@ -94,8 +94,8 @@
         + [jax.ShapeDtypeStruct((8, 128), jnp.float32)]
         + own,
         scratch_shapes=[
-            pltpu.VMEM((4, rows * count, 128), packed.dtype),
-            pltpu.SemaphoreType.DMA((5,)),
+            pltpu.VMEM((8, rows * count, 128), packed.dtype),
+            pltpu.SemaphoreType.DMA((9,)),
         ],
         compiler_params=pltpu.CompilerParams(vmem_limit_bytes=SMALL_VMEM),
         cost_estimate=pl.CostEstimate(flops=0, bytes_accessed=1024, transcendentals=0),
@@ -211,10 +211,49 @@
     )(*pieces, signs)
 
 
-def rest_kernel(n_first, n_chips, *refs):
+def shared_units(pieces, feature_len, shared, rows_s, out):
+    base = 0
+    for piece in pieces:
+        rows_s[base : base + piece.shape[0], :] = piece[:, :feature_len]
+        base += piece.shape[0]
+    part = shared.shape[1] // 2
+    both = jnp.dot(rows_s[...], shared[...], preferred_element_type=jnp.float32)
+    gate, up = both[:, :part], both[:, part:]
+    out[...] = (gate / (1.0 + jnp.exp(-gate)) * up).astype(jnp.bfloat16)
+
+
+def second_kernel(n_pieces, *refs):
+    pieces = refs[:n_pieces]
+    signs, shared, out, units, rows_s = refs[n_pieces:]
+    count = pieces[0].shape[0]
+    rotate(pieces[CORES:], signs, out, [n * count for n in range(n_pieces - CORES)])
+    shared_units(pieces, out.shape[1], shared, rows_s, units)
+
+
+def second_rows(pieces, signs, shared):
+    whole = pl.BlockSpec(memory_space=pltpu.VMEM)
+    feature_len = shared.shape[0]
+    count = pieces[0].shape[0]
+    rows = len(pieces) * count
+    return pl.pallas_call(
+        functools.partial(second_kernel, len(pieces)),
+        in_specs=[whole] * (len(pieces) + 2),
+        out_specs=[whole] * 2,
+        out_shape=[
+            vmem((rows - CORES * count, feature_len), jnp.bfloat16),
+            vmem((rows, shared.shape[1] // 2), jnp.bfloat16),
+        ],
+        scratch_shapes=[pltpu.VMEM((rows, feature_len), jnp.bfloat16)],
+        compiler_params=pltpu.CompilerParams(vmem_limit_bytes=HIDDEN_VMEM + 2 * rows * feature_len),
+        cost_estimate=pl.CostEstimate(flops=0, bytes_accessed=1024, transcendentals=0),
+        name="second_rows",
+    )(*pieces, signs, shared)
+
+
+def rest_kernel(n_chips, *refs):
     n_pieces = CORES * n_chips
     index, pieces = refs[0], refs[1 : 1 + n_pieces]
-    signs, first, second, shared, shared_down, *outs, rows_s, sem = refs[1 + n_pieces :]
+    signs, first, second, units, shared, shared_down, *outs, rows_s, last_s, sem = refs[1 + n_pieces :]
     deq, shared_hidden, combine, shared_out = outs
     own = shared_out.shape[0]
     own = pl.ds(pl.multiple_of(index[0] * own, own), own)
@@ -222,53 +261,57 @@
     copy.start()
     count = pieces[0].shape[0]
     feature_len = deq.shape[1]
+    last = pieces[CORES + n_chips - 1 :]
+    shared_units(last, feature_len, shared, rows_s, last_s)
     sources, bases = [], []
     for core in range(CORES):
         for chip in range(n_chips):
             base = (core * n_chips + chip) * count
+            here = slice(base, base + count)
+            at = core if chip == 0 else CORES + core * (n_chips - 1) + chip - 1
+            piece = pieces[at]
             if chip == 0:
-                piece = pieces[core]
-                deq[base : base + count, :] = first[core * count : (core + 1) * count, :]
+                deq[here, :] = first[core * count : (core + 1) * count, :]
+            elif core == 0:
+                deq[here, :] = second[(chip - 1) * count : chip * count, :]
             else:
-                piece = pieces[CORES + core * (n_chips - 1) + chip - 1]
-                if core == 0:
-                    deq[base : base + count, :] = second[(chip - 1) * count : chip * count, :]
-                else:
-                    sources.append(piece)
-                    bases.append(base)
-            rows_s[base : base + count, :] = piece[:, :feature_len]
-            combine[base : base + count, :] = piece[:, feature_len:].astype(jnp.float32)
+                sources.append(piece)
+                bases.append(base)
+            if chip and core:
+                shared_hidden[here, :] = last_s[(chip - 1) * count : chip * count, :]
+            else:
+                shared_hidden[here, :] = units[at * count : (at + 1) * count, :]
+            combine[here, :] = piece[:, feature_len:].astype(jnp.float32)
     rotate(sources, signs, deq, bases)
+    copy.wait()
+
+
+def rest_rows(index, pieces, signs, first, second, units, shared, shared_down, n_chips):
+    whole = pl.BlockSpec(memory_space=pltpu.VMEM)
+    rows = sum(piece.shape[0] for piece in pieces)
+    last = (n_chips - 1) * pieces[0].shape[0]
+    feature_len = first.shape[1]
     part = shared.shape[1] // 2
-    both = jnp.dot(rows_s[...], shared[...], preferred_element_type=jnp.float32)
-    gate, up = both[:, :part], both[:, part:]
-    shared_hidden[...] = (gate / (1.0 + jnp.exp(-gate)) * up).astype(jnp.bfloat16)
-    copy.wait()
-
-
-def rest_rows(index, pieces, signs, first, second, shared, shared_down, n_chips):
-    whole = pl.BlockSpec(memory_space=pltpu.VMEM)
-    rows = sum(piece.shape[0] for piece in pieces)
-    feature_len = first.shape[1]
-    return pl.pallas_call(
-        functools.partial(rest_kernel, len(pieces), n_chips),
+    return pl.pallas_call(
+        functools.partial(rest_kernel, n_chips),
         in_specs=[pl.BlockSpec(memory_space=pltpu.SMEM)]
-        + [whole] * (len(pieces) + 4)
+        + [whole] * (len(pieces) + 5)
         + [pl.BlockSpec(memory_space=pl.ANY)],
         out_specs=[whole] * 4,
         out_shape=[
             vmem((rows, feature_len), jnp.bfloat16),
-            vmem((rows, shared.shape[1] // 2), jnp.bfloat16),
+            vmem((rows, part), jnp.bfloat16),
             vmem((rows, pieces[0].shape[1] - feature_len), jnp.float32),
-            vmem((shared.shape[1] // 2, feature_len), shared_down.dtype),
+            vmem((part, feature_len), shared_down.dtype),
         ],
         scratch_shapes=[
-            pltpu.VMEM((rows, feature_len), jnp.bfloat16),
+            pltpu.VMEM((last, feature_len), jnp.bfloat16),
+            pltpu.VMEM((last, part), jnp.bfloat16),
             pltpu.SemaphoreType.DMA(()),
         ],
-        compiler_params=pltpu.CompilerParams(vmem_limit_bytes=HIDDEN_VMEM + 2 * rows * feature_len),
+        compiler_params=pltpu.CompilerParams(vmem_limit_bytes=HIDDEN_VMEM + 2 * last * feature_len),
         name="rest_rows",
-    )(index, *pieces, signs, first, second, shared, shared_down)
+    )(index, *pieces, signs, first, second, units, shared, shared_down)
 
 
 def hidden_kernel(experts, *refs):
@@ -475,7 +518,7 @@
     first = first_rows([along_z, near], signs, feature_len)
     from_x = [pass_on([own, part], after + [first]) for own, part in zip(own_from_x, from_x)]
     from_both = [exchange(part, "expert", 1) for part in from_x]
-    second = first_rows(from_x, signs, feature_len)
+    second, units = second_rows([along_z, near] + from_x, signs, shared_in)
 
     shared_out = pltpu.with_memory_space_constraint(shared_out, pltpu.HBM)
     deq, shared_hidden, combine, shared_out = rest_rows(
@@ -484,6 +527,7 @@
         signs,
         first,
         second,
+        units,
         shared_in,
         shared_out,
         chips,

time: 67.1 us -> 66.6 us (level)
  waiting for transfers between devices: 11.9 us -> 10.9 us
  starting transfers between devices: 20.9 us -> 21.6 us
    ppermute x15, waiting for transfers between devices: 11.9 us -> 10.9 us  [exchange(): lax.ppermute(value, axis, [(i, i ^ flip) for i in range(lax.axis_size(axi...]
    pallas_call x1 -> x2, Pallas kernels: 2.14 us -> 3.06 us  [the longest x1 2.09 us: rest_rows(): pl.pallas_call(functools.partial(rest_kernel, n_chips), in_specs=[pl.Bloc...]
    ppermute x15, starting transfers between devices: 20.9 us -> 21.6 us  [exchange(): lax.ppermute(value, axis, [(i, i ^ flip) for i in range(lax.axis_size(axi...]
    pallas_call x2 -> x1, Pallas kernels: 1.76 us -> 1.12 us  [first_rows(): pl.pallas_call(functools.partial(first_kernel, len(pieces)), in_specs=[wh...]
where the time goes in v7:
time: 66.6 us; the launch traced here: 66.3 us
  Pallas kernels  29.4 us (44%)
  starting transfers between devices  21.6 us (32%)
  waiting for transfers between devices  10.9 us (16%)
  local copies, waits for them, and re-layouts  1.99 us (3%)
  other arithmetic  1.56 us (2%)
  between operations  0.95 us (1%)
    ppermute x15, starting transfers between devices, exchange(): lax.ppermute(value, axis, [(i, i ^ flip) for i in range(lax.axis_size(axi...  21.6 us
    pallas_call x2, Pallas kernels, apart(): pl.pallas_call(functools.partial(apart_kernel, experts, rows, chunk, 1 +...  11.6 us
    ppermute x15, waiting for transfers between devices, exchange(): lax.ppermute(value, axis, [(i, i ^ flip) for i in range(lax.axis_size(axi...  10.9 us
    pallas_call x2, Pallas kernels, hidden_rows(): pl.pallas_call(functools.partial(hidden_kernel, experts), in_specs=[whole...  8.06 us
    pallas_call x2, Pallas kernels, down_rows(): pl.pallas_call(functools.partial(down_kernel, start, tile, len(hidden)),...  4.71 us
    pallas_call x1, Pallas kernels, rest_rows(): pl.pallas_call(functools.partial(rest_kernel, n_chips), in_specs=[pl.Bloc...  2.09 us
  transfers between devices with their start and end apart: 15, of which 7 were waited for; matrix products, arithmetic and copies ran while one was open for 4% of the time, Pallas kernels for 24%

profile of v7, /device:TPU:0, one launch (start us, length us, event | category | flops | bytes accessed | tf_op | source)
XLA Modules:
  0.0 66.3 jit_solution(7583998428171171841)
XLA Ops:
  0.6 3.1 %collective-permute-start = (bf16[16,3584]{1,0:T(8,128)(2,1)}, bf16[16,3584]{1,0:T(8,128)(2,1)S(1)}, u32[]{:S(2)}, u32[]{:S(2)}) collective-permute-start(bf16[16,3584]{1,0:T(8,128)(2,1)} %refs_0_.1), channel_id=1, source_target_pairs={{0,1},{1,0},{2,3},{3,2},{4,5},{5,4},{6,7},{7,6},{8,9},{9,8},{10,11... | collective-permute-start | bytes 344072 | tf_op jit(solution)/shard_map/ppermute | solution.py:438
  3.7 2.6 %collective-permute-start.1 = (bf16[16,3584]{1,0:T(8,128)(2,1)}, bf16[16,3584]{1,0:T(8,128)(2,1)S(1)}, u32[]{:S(2)}, u32[]{:S(2)}) collective-permute-start(bf16[16,3584]{1,0:T(8,128)(2,1)} %refs_0_.1), channel_id=1, source_target_pairs={{0,2},{1,3},{2,0},{3,1},{4,6},{5,7},{6,4},{7,5},{8,10},{9,11},{10,... | collective-permute-start | bytes 344072 | tf_op jit(solution)/shard_map/ppermute | solution.py:438
  6.3 0.7 %select_reduce_fusion = f32[64,16]{0,1:T(8,128)S(1)} fusion(f32[64,8]{0,1:T(8,128)} %param.11, s32[64,8]{0,1:T(8,128)} %param.10), kind=kLoop, calls=%fused_computation.27 | loop fusion | flops 23552 | bytes 8192 | tf_op jit(solution)/shard_map/reduce_sum | solution.py:462
  7.0 0.1 copy.28
  7.2 0.1 pad_maximum_fusion
  7.3 0.6 gather_fusion
  7.8 0.0 copy-start
  7.8 0.9 %copy-done = bf16[16,3584]{1,0:T(8,128)(2,1)S(1)} copy-done((bf16[16,3584]{1,0:T(8,128)(2,1)S(1)}, bf16[16,3584]{1,0:T(8,128)(2,1)}, u32[]{:S(2)}) %copy-start) | copy-done | bytes 114712
  8.7 1.8 %collective-permute-start.3 = (bf16[16,3712]{1,0:T(8,128)(2,1)S(1)}, bf16[16,3712]{1,0:T(8,128)(2,1)S(1)}, u32[]{:S(2)}, u32[]{:S(2)}) collective-permute-start(bf16[16,3712]{1,0:T(8,128)(2,1)S(1)} %pack.1.refs_7_), channel_id=1, source_target_pairs={{0,8},{4,12},{8,0},{12,4},{1,9},{5,13},{9,1},{13,5},{2,10},{6,14},... | collective-permute-start | bytes 356360 | tf_op jit(solution)/shard_map/ppermute | solution.py:438
  10.6 0.3 select_convert_fusion.refs_5_.refs_2_.refs_3_
  10.9 0.1 fusion.12.refs_4_.refs_2_
  11.0 3.8 %apart.2 = (bf16[2,3584,512]{2,1,0:T(8,128)(2,1)S(1)}, f32[8,128]{1,0:T(8,128)S(1)}, bf16[3584,1,2,128]{3,2,1,0:T(2,128)(2,1)S(1)}) custom-call(bf16[4,28672,128]{2,1,0:T(8,128)(2,1)} %bitcast.74, s32[1]{0:T(128)} %bitcast.refs_1_.refs_6_.refs_0_, bf16[3584,4,2,128]{3,2,1,0:T(2,128)(2,1)} %bitcast.76, bf16[64,128]{1,0:T(8,128)(2,1)S(1)} %bitcast.71, ...), custom_call_target="tpu_custom_call" | custom-call | bytes 1024 | tf_op jit(solution)/shard_map/apart/pallas_call | solution.py:89
  14.8 0.0 collective-permute-done.refs_1_
  14.8 0.8 %collective-permute-done.1.refs_2_ = bf16[16,3584]{1,0:T(8,128)(2,1)S(1)} collective-permute-done((bf16[16,3584]{1,0:T(8,128)(2,1)}, bf16[16,3584]{1,0:T(8,128)(2,1)S(1)}, u32[]{:S(2)}, u32[]{:S(2)}) %collective-permute-start.1) | collective-permute-done | bytes 114720 | tf_op jit(solution)/shard_map/ppermute | solution.py:438
  15.6 0.0 collective-permute-done.2.refs_3_
  15.6 0.0 collective-permute-done.3.refs_6_.refs_0_
  15.6 0.1 join.1
  15.7 0.1 collective-permute-start.4
  15.8 1.6 %collective-permute-start.5 = (bf16[48,3712]{1,0:T(8,128)(2,1)S(1)}, bf16[48,3712]{1,0:T(8,128)(2,1)S(1)}, u32[]{:S(2)}, u32[]{:S(2)}) collective-permute-start(bf16[48,3712]{1,0:T(8,128)(2,1)S(1)} %get-tuple-element.27), channel_id=1, source_target_pairs={{0,8},{4,12},{8,0},{12,4},{1,9},{5,13},{9,1},{13,5},{2,10},{6,14},... | collective-permute-start | bytes 1069064 | tf_op jit(solution)/shard_map/ppermute | solution.py:438
  17.4 0.2 copy.56
  17.6 7.8 %apart.3 = (bf16[2,3584,512]{2,1,0:T(8,128)(2,1)S(1)}, bf16[2,3584,512]{2,1,0:T(8,128)(2,1)S(1)}, bf16[2,3584,512]{2,1,0:T(8,128)(2,1)S(1)}, f32[8,128]{1,0:T(8,128)S(1)}) custom-call(bf16[4,28672,128]{2,1,0:T(8,128)(2,1)} %bitcast.75, bf16[64,3712]{1,0:T(8,128)(2,1)S(1)} %get-tuple-element.26.refs_1_.refs_0_, bf16[3584,256]{1,0:T(8,128)(2,1)S(1)} %bitcast.67), custom_call_target="tpu_custom_call" | custom-call | bytes 1024 | tf_op jit(solution)/shard_map/apart/pallas_call | solution.py:89
  25.4 1.1 %first_rows.1.refs_3_.refs_6_ = bf16[128,3584]{1,0:T(8,128)(2,1)S(1)} custom-call(bf16[64,3712]{1,0:T(8,128)(2,1)S(1)} %get-tuple-element.26.refs_1_.refs_0_, bf16[64,3712]{1,0:T(8,128)(2,1)S(1)} %collective-permute-done.4.refs_1_.refs_2_, bf16[256,256]{1,0:T(8,128)(2,1)S(1)} %select_convert_fusion.refs_5_.refs_2_.refs_3_), custom_call_target="tpu_custom_call" | custom-call | bytes 1024 | tf_op jit(solution)/shard_map/first_rows/pallas_call | solution.py:203
  26.6 0.2 collective-permute-start.6
  26.9 1.0 %second_rows.1 = (bf16[64,3584]{1,0:T(8,128)(2,1)S(1)}, bf16[192,128]{1,0:T(8,128)(2,1)S(1)}) custom-call(bf16[64,3712]{1,0:T(8,128)(2,1)S(1)} %get-tuple-element.26.refs_1_.refs_0_, bf16[64,3712]{1,0:T(8,128)(2,1)S(1)} %collective-permute-done.4.refs_1_.refs_2_, bf16[64,3712]{1,0:T(8,128)(2,1)S(1)} %pass_on.1.refs_2_.refs_3_, ...), custom_call_target="tpu_custom_call" | custom-call | bytes 1024 | tf_op jit(solution)/shard_map/second_rows/pallas_call | solution.py:238
  27.8 0.7 %collective-permute-done.6.refs_4_ = bf16[64,3712]{1,0:T(8,128)(2,1)S(1)} collective-permute-done((bf16[64,3712]{1,0:T(8,128)(2,1)S(1)}, bf16[64,3712]{1,0:T(8,128)(2,1)S(1)}, u32[]{:S(2)}, u32[]{:S(2)}) %collective-permute-start.6) | collective-permute-done | bytes 475168 | tf_op jit(solution)/shard_map/ppermute | solution.py:438
  28.5 2.1 %rest_rows.1 = (bf16[256,3584]{1,0:T(8,128)(2,1)S(1)}, bf16[256,128]{1,0:T(8,128)(2,1)S(1)}, f32[256,128]{1,0:T(8,128)S(1)}, bf16[128,3584]{1,0:T(8,128)(2,1)S(1)}) custom-call(s32[1]{0:T(128)} %bitcast.refs_1_.refs_6_.refs_0_, bf16[64,3712]{1,0:T(8,128)(2,1)S(1)} %get-tuple-element.26.refs_1_.refs_0_, ...), custom_call_target="tpu_custom_call" | custom-call | tf_op jit(solution)/shard_map/rest_rows/pallas_call | solution.py:295
  30.6 4.0 %hidden_rows.2 = (bf16[256,1024]{1,0:T(8,128)(2,1)S(1)}, bf16[512,3584]{1,0:T(8,128)(2,1)S(1)}, bf16[512,3584]{1,0:T(8,128)(2,1)S(1)}) custom-call(bf16[256,3584]{1,0:T(8,128)(2,1)S(1)} %get-tuple-element.32.refs_0_, f32[256,128]{1,0:T(8,128)S(1)} %get-tuple-element.33.refs_1_, f32[4,128]{1,0:T(4,128)S(1)} %fusion.12.refs_4_.refs_2_, ...), custom_call_target="tpu_custom_call" | custom-call | tf_op jit(solution)/shard_map/hidden_rows/pallas_call | solution.py:344
  34.7 4.0 %hidden_rows.3 = (bf16[256,1024]{1,0:T(8,128)(2,1)S(1)}, bf16[512,3584]{1,0:T(8,128)(2,1)S(1)}, bf16[512,3584]{1,0:T(8,128)(2,1)S(1)}) custom-call(bf16[256,3584]{1,0:T(8,128)(2,1)S(1)} %get-tuple-element.32.refs_0_, f32[256,128]{1,0:T(8,128)S(1)} %get-tuple-element.33.refs_1_, f32[4,128]{1,0:T(4,128)S(1)} %fusion.12.refs_4_.refs_2_, ...), custom_call_target="tpu_custom_call" | custom-call | tf_op jit(solution)/shard_map/hidden_rows/pallas_call | solution.py:344
  38.7 0.0 copy-start.3
  38.7 2.4 %down_rows.2 = bf16[256,1792]{1,0:T(8,128)(2,1)S(1)} custom-call(bf16[256,1024]{1,0:T(8,128)(2,1)S(1)} %get-tuple-element.36.refs_0_, bf16[256,1024]{1,0:T(8,128)(2,1)S(1)} %get-tuple-element.39.refs_1_, bf16[256,128]{1,0:T(8,128)(2,1)S(1)} %get-tuple-element.40.refs_2_, bf16[128,3584]{1,0:T(8,128)(2,1)S(1)} %get-tuple-element.41.refs_3_, ...), custom_call_target="tpu_custom_call" | custom-call | tf_op jit(solution)/shard_map/down_rows/pallas_call | solution.py:387
  41.1 0.2 collective-permute-start.7
  41.4 2.4 %down_rows.3 = bf16[256,1792]{1,0:T(8,128)(2,1)S(1)} custom-call(bf16[256,1024]{1,0:T(8,128)(2,1)S(1)} %get-tuple-element.36.refs_0_, bf16[256,1024]{1,0:T(8,128)(2,1)S(1)} %get-tuple-element.39.refs_1_, bf16[256,128]{1,0:T(8,128)(2,1)S(1)} %get-tuple-element.40.refs_2_, bf16[128,3584]{1,0:T(8,128)(2,1)S(1)} %get-tuple-element.41.refs_3_, ...), custom_call_target="tpu_custom_call" | custom-call | tf_op jit(solution)/shard_map/down_rows/pallas_call | solution.py:387
  43.8 0.4 collective-permute-start.11
  44.2 0.1 convert_add_fusion.1
  44.3 0.0 copy-start.2
  44.3 1.8 %collective-permute-start.8 = (bf16[2,2,16,1792]{3,2,0,1:T(8,128)(2,1)S(1)}, bf16[2,2,16,1792]{3,2,0,1:T(8,128)(2,1)S(1)}, u32[]{:S(2)}, u32[]{:S(2)}) collective-permute-start(bf16[2,2,16,1792]{3,2,0,1:T(8,128)(2,1)S(1)} %fusion.4), channel_id=1, source_target_pairs={{0,1},{1,0},{2,3},{3,2},{4,5},{5,4},{6,7},{7,6},{8,9},{9,8},{10,11... | collective-permute-start | bytes 688136 | tf_op jit(solution)/shard_map/ppermute | solution.py:438
  46.2 0.1 convert_add_fusion
  46.3 1.5 %collective-permute-start.12 = (bf16[1,4,16,1792]{3,2,1,0:T(8,128)(2,1)S(1)}, bf16[1,4,16,1792]{3,2,1,0:T(8,128)(2,1)S(1)}, u32[]{:S(2)}, u32[]{:S(2)}) collective-permute-start(bf16[1,4,16,1792]{3,2,1,0:T(8,128)(2,1)S(1)} %fusion.3), channel_id=1, source_target_pairs={{0,8},{4,12},{8,0},{12,4},{1,9},{5,13},{9,1},{13,5},{2,10},{6,14},... | collective-permute-start | bytes 688136 | tf_op jit(solution)/shard_map/ppermute | solution.py:438
  47.8 4.3 %collective-permute-done.8 = bf16[2,2,16,1792]{3,2,0,1:T(8,128)(2,1)S(1)} collective-permute-done((bf16[2,2,16,1792]{3,2,0,1:T(8,128)(2,1)S(1)}, bf16[2,2,16,1792]{3,2,0,1:T(8,128)(2,1)S(1)}, u32[]{:S(2)}, u32[]{:S(2)}) %collective-permute-start.8) | collective-permute-done | bytes 229408 | tf_op jit(solution)/shard_map/ppermute | solution.py:438
  52.2 1.5 %collective-permute-start.9 = (bf16[1,2,16,1792]{3,2,1,0:T(8,128)(2,1)S(1)}, bf16[1,2,16,1792]{3,2,1,0:T(8,128)(2,1)S(1)}, u32[]{:S(2)}, u32[]{:S(2)}) collective-permute-start(bf16[1,2,16,1792]{3,2,1,0:T(8,128)(2,1)S(1)} %fusion.7), channel_id=1, source_target_pairs={{0,8},{4,12},{8,0},{12,4},{1,9},{5,13},{9,1},{13,5},{2,10},{6,14},... | collective-permute-start | bytes 344072 | tf_op jit(solution)/shard_map/ppermute | solution.py:438
  53.6 0.1 collective-permute-done.12
  53.8 1.8 %collective-permute-start.13 = (bf16[2,16,1792]{2,1,0:T(8,128)(2,1)S(1)}, bf16[2,16,1792]{2,1,0:T(8,128)(2,1)S(1)}, u32[]{:S(2)}, u32[]{:S(2)}) collective-permute-start(bf16[2,16,1792]{2,1,0:T(8,128)(2,1)S(1)} %fusion.8), channel_id=1, source_target_pairs={{0,1},{1,0},{2,3},{3,2},{4,5},{5,4},{6,7},{7,6},{8,9},{9,8},{10,11... | collective-permute-start | bytes 344072 | tf_op jit(solution)/shard_map/ppermute | solution.py:438
  55.6 1.4 %collective-permute-done.9 = bf16[1,2,16,1792]{3,2,1,0:T(8,128)(2,1)S(1)} collective-permute-done((bf16[1,2,16,1792]{3,2,1,0:T(8,128)(2,1)S(1)}, bf16[1,2,16,1792]{3,2,1,0:T(8,128)(2,1)S(1)}, u32[]{:S(2)}, u32[]{:S(2)}) %collective-permute-start.9) | collective-permute-done | bytes 114720 | tf_op jit(solution)/shard_map/ppermute | solution.py:438
  57.1 2.8 %collective-permute-start.10 = (bf16[16,1792]{1,0:T(8,128)(2,1)S(1)}, bf16[16,1792]{1,0:T(8,128)(2,1)S(1)}, u32[]{:S(2)}, u32[]{:S(2)}) collective-permute-start(bf16[16,1792]{1,0:T(8,128)(2,1)S(1)} %fusion.9), channel_id=1, source_target_pairs={{0,2},{1,3},{2,0},{3,1},{4,6},{5,7},{6,4},{7,5},{8,10},{9,11},{10,... | collective-permute-start | bytes 172040 | tf_op jit(solution)/shard_map/ppermute | solution.py:438
  59.9 2.2 %collective-permute-start.14 = (bf16[16,1792]{1,0:T(8,128)(2,1)S(1)}, bf16[16,1792]{1,0:T(8,128)(2,1)S(1)}, u32[]{:S(2)}, u32[]{:S(2)}) collective-permute-start(bf16[16,1792]{1,0:T(8,128)(2,1)S(1)} %fusion.10), channel_id=1, source_target_pairs={{0,2},{1,3},{2,0},{3,1},{4,6},{5,7},{6,4},{7,5},{8,10},{9,11},{10,... | collective-permute-start | bytes 172040 | tf_op jit(solution)/shard_map/ppermute | solution.py:438
  62.1 1.7 %collective-permute-done.10.refs_1_ = bf16[16,1792]{1,0:T(8,128)(2,1)S(1)} collective-permute-done((bf16[16,1792]{1,0:T(8,128)(2,1)S(1)}, bf16[16,1792]{1,0:T(8,128)(2,1)S(1)}, u32[]{:S(2)}, u32[]{:S(2)}) %collective-permute-start.10) | collective-permute-done | bytes 57376 | tf_op jit(solution)/shard_map/ppermute | solution.py:438
  63.8 1.8 %collective-permute-done.14.refs_3_ = bf16[16,1792]{1,0:T(8,128)(2,1)S(1)} collective-permute-done((bf16[16,1792]{1,0:T(8,128)(2,1)S(1)}, bf16[16,1792]{1,0:T(8,128)(2,1)S(1)}, u32[]{:S(2)}, u32[]{:S(2)}) %collective-permute-start.14) | collective-permute-done | bytes 57376 | tf_op jit(solution)/shard_map/ppermute | solution.py:438
  65.6 0.7 %finish.1 = (bf16[16,3584]{1,0:T(8,128)(2,1)}, f32[1,8]{1,0:T(1,128)}) custom-call(f32[16,1792]{1,0:T(8,128)S(1)} %slice_bitcast_fusion.3.refs_0_, bf16[16,1792]{1,0:T(8,128)(2,1)S(1)} %collective-permute-done.10.refs_1_, f32[16,1792]{1,0:T(8,128)S(1)} %slice_bitcast_fusion.2.refs_2_, bf16[16,1792]{1,0:T(8,128)(2,1)S(1)} %collective-permute-done.14.refs_3_, ...), custom_call_target="tpu_custom_call" | custom-call | tf_op jit(solution)/shard_map/finish/pallas_call | solution.py:423
  (36 shorter events, 0.4 us)
Async XLA Ops:
  0.6 14.2 %collective-permute-start = (bf16[16,3584]{1,0:T(8,128)(2,1)}, bf16[16,3584]{1,0:T(8,128)(2,1)S(1)}, u32[]{:S(2)}, u32[]{:S(2)}) collective-permute-start(bf16[16,3584]{1,0:T(8,128)(2,1)} %refs_0_.1), channel_id=1, source_target_pairs={{0,1},{1,0},{2,3},{3,2},{4,5},{5,4},{6,7},{7,6},{8,9},{9,8},{10,11... | collective-permute-start | bytes 344072 | tf_op jit(solution)/shard_map/ppermute | solution.py:438
  3.7 11.9 %collective-permute-start.1 = (bf16[16,3584]{1,0:T(8,128)(2,1)}, bf16[16,3584]{1,0:T(8,128)(2,1)S(1)}, u32[]{:S(2)}, u32[]{:S(2)}) collective-permute-start(bf16[16,3584]{1,0:T(8,128)(2,1)} %refs_0_.1), channel_id=1, source_target_pairs={{0,2},{1,3},{2,0},{3,1},{4,6},{5,7},{6,4},{7,5},{8,10},{9,11},{10,... | collective-permute-start | bytes 344072 | tf_op jit(solution)/shard_map/ppermute | solution.py:438
  6.3 9.3 %collective-permute-start.2 = (bf16[16,3584]{1,0:T(8,128)(2,1)}, bf16[16,3584]{1,0:T(8,128)(2,1)S(1)}, u32[]{:S(2)}, u32[]{:S(2)}) collective-permute-start(bf16[16,3584]{1,0:T(8,128)(2,1)} %refs_0_.1), channel_id=1, source_target_pairs={{0,3},{1,2},{2,1},{3,0},{4,7},{5,6},{6,5},{7,4},{8,11},{9,10},{10,... | collective-permute-start | bytes 344072 | tf_op jit(solution)/shard_map/ppermute | solution.py:438
  7.8 0.9 %copy-start = (bf16[16,3584]{1,0:T(8,128)(2,1)S(1)}, bf16[16,3584]{1,0:T(8,128)(2,1)}, u32[]{:S(2)}) copy-start(bf16[16,3584]{1,0:T(8,128)(2,1)} %refs_0_.1) | copy-start | bytes 344068
  8.7 6.9 %collective-permute-start.3 = (bf16[16,3712]{1,0:T(8,128)(2,1)S(1)}, bf16[16,3712]{1,0:T(8,128)(2,1)S(1)}, u32[]{:S(2)}, u32[]{:S(2)}) collective-permute-start(bf16[16,3712]{1,0:T(8,128)(2,1)S(1)} %pack.1.refs_7_), channel_id=1, source_target_pairs={{0,8},{4,12},{8,0},{12,4},{1,9},{5,13},{9,1},{13,5},{2,10},{6,14},... | collective-permute-start | bytes 356360 | tf_op jit(solution)/shard_map/ppermute | solution.py:438
  11.0 4.7 %copy-start.1 = (bf16[16,3584]{1,0:T(8,128)(2,1)S(1)}, bf16[16,3584]{1,0:T(8,128)(2,1)}, u32[]{:S(2)}) copy-start(bf16[16,3584]{1,0:T(8,128)(2,1)} %refs_0_.1) | copy-start | bytes 344068
  15.7 9.7 %collective-permute-start.4 = (bf16[64,3712]{1,0:T(8,128)(2,1)S(1)}, bf16[64,3712]{1,0:T(8,128)(2,1)S(1)}, u32[]{:S(2)}, u32[]{:S(2)}) collective-permute-start(bf16[64,3712]{1,0:T(8,128)(2,1)S(1)} %get-tuple-element.26.refs_1_.refs_0_), channel_id=1, source_target_pairs={{0,4},{4,0},{8,12},{12,8},{1,5},{5,1},{9,13},{13,9},{2,6},{6,2},{1... | collective-permute-start | bytes 1425416 | tf_op jit(solution)/shard_map/ppermute | solution.py:438
  15.8 10.8 %collective-permute-start.5 = (bf16[48,3712]{1,0:T(8,128)(2,1)S(1)}, bf16[48,3712]{1,0:T(8,128)(2,1)S(1)}, u32[]{:S(2)}, u32[]{:S(2)}) collective-permute-start(bf16[48,3712]{1,0:T(8,128)(2,1)S(1)} %get-tuple-element.27), channel_id=1, source_target_pairs={{0,8},{4,12},{8,0},{12,4},{1,9},{5,13},{9,1},{13,5},{2,10},{6,14},... | collective-permute-start | bytes 1069064 | tf_op jit(solution)/shard_map/ppermute | solution.py:438
  26.6 1.9 %collective-permute-start.6 = (bf16[64,3712]{1,0:T(8,128)(2,1)S(1)}, bf16[64,3712]{1,0:T(8,128)(2,1)S(1)}, u32[]{:S(2)}, u32[]{:S(2)}) collective-permute-start(bf16[64,3712]{1,0:T(8,128)(2,1)S(1)} %pass_on.1.refs_2_.refs_3_), channel_id=1, source_target_pairs={{0,4},{4,0},{8,12},{12,8},{1,5},{5,1},{9,13},{13,9},{2,6},{6,2},{1... | collective-permute-start | bytes 1425416 | tf_op jit(solution)/shard_map/ppermute | solution.py:438
  38.7 2.6 %copy-start.3 = (f32[3584]{0:T(1024)S(1)}, f32[3584]{0:T(1024)}, u32[]{:S(2)}) copy-start(f32[3584]{0:T(1024)} %param.17) | copy-start | bytes 43012
  41.1 3.1 %collective-permute-start.7 = (bf16[128,1792]{1,0:T(8,128)(2,1)S(1)}, bf16[128,1792]{1,0:T(8,128)(2,1)S(1)}, u32[]{:S(2)}, u32[]{:S(2)}) collective-permute-start(bf16[128,1792]{1,0:T(8,128)(2,1)S(1)} %slice.83), channel_id=1, source_target_pairs={{0,4},{4,0},{8,12},{12,8},{1,5},{5,1},{9,13},{13,9},{2,6},{6,2},{1... | collective-permute-start | bytes 1376264 | tf_op jit(solution)/shard_map/ppermute | solution.py:438
  43.8 2.4 %collective-permute-start.11 = (bf16[128,1792]{1,0:T(8,128)(2,1)S(1)}, bf16[128,1792]{1,0:T(8,128)(2,1)S(1)}, u32[]{:S(2)}, u32[]{:S(2)}) collective-permute-start(bf16[128,1792]{1,0:T(8,128)(2,1)S(1)} %slice.91), channel_id=1, source_target_pairs={{0,4},{4,0},{8,12},{12,8},{1,5},{5,1},{9,13},{13,9},{2,6},{6,2},{1... | collective-permute-start | bytes 1376264 | tf_op jit(solution)/shard_map/ppermute | solution.py:438
  44.3 21.4 %copy-start.2 = (s32[8]{0:T(128)S(1)}, s32[8]{0:T(128)}, u32[]{:S(2)}) copy-start(s32[8]{0:T(128)} %param.12) | copy-start | bytes 100
  44.3 7.8 %collective-permute-start.8 = (bf16[2,2,16,1792]{3,2,0,1:T(8,128)(2,1)S(1)}, bf16[2,2,16,1792]{3,2,0,1:T(8,128)(2,1)S(1)}, u32[]{:S(2)}, u32[]{:S(2)}) collective-permute-start(bf16[2,2,16,1792]{3,2,0,1:T(8,128)(2,1)S(1)} %fusion.4), channel_id=1, source_target_pairs={{0,1},{1,0},{2,3},{3,2},{4,5},{5,4},{6,7},{7,6},{8,9},{9,8},{10,11... | collective-permute-start | bytes 688136 | tf_op jit(solution)/shard_map/ppermute | solution.py:438
  46.3 7.5 %collective-permute-start.12 = (bf16[1,4,16,1792]{3,2,1,0:T(8,128)(2,1)S(1)}, bf16[1,4,16,1792]{3,2,1,0:T(8,128)(2,1)S(1)}, u32[]{:S(2)}, u32[]{:S(2)}) collective-permute-start(bf16[1,4,16,1792]{3,2,1,0:T(8,128)(2,1)S(1)} %fusion.3), channel_id=1, source_target_pairs={{0,8},{4,12},{8,0},{12,4},{1,9},{5,13},{9,1},{13,5},{2,10},{6,14},... | collective-permute-start | bytes 688136 | tf_op jit(solution)/shard_map/ppermute | solution.py:438
  52.2 4.9 %collective-permute-start.9 = (bf16[1,2,16,1792]{3,2,1,0:T(8,128)(2,1)S(1)}, bf16[1,2,16,1792]{3,2,1,0:T(8,128)(2,1)S(1)}, u32[]{:S(2)}, u32[]{:S(2)}) collective-permute-start(bf16[1,2,16,1792]{3,2,1,0:T(8,128)(2,1)S(1)} %fusion.7), channel_id=1, source_target_pairs={{0,8},{4,12},{8,0},{12,4},{1,9},{5,13},{9,1},{13,5},{2,10},{6,14},... | collective-permute-start | bytes 344072 | tf_op jit(solution)/shard_map/ppermute | solution.py:438
  53.8 6.1 %collective-permute-start.13 = (bf16[2,16,1792]{2,1,0:T(8,128)(2,1)S(1)}, bf16[2,16,1792]{2,1,0:T(8,128)(2,1)S(1)}, u32[]{:S(2)}, u32[]{:S(2)}) collective-permute-start(bf16[2,16,1792]{2,1,0:T(8,128)(2,1)S(1)} %fusion.8), channel_id=1, source_target_pairs={{0,1},{1,0},{2,3},{3,2},{4,5},{5,4},{6,7},{7,6},{8,9},{9,8},{10,11... | collective-permute-start | bytes 344072 | tf_op jit(solution)/shard_map/ppermute | solution.py:438
  57.1 6.8 %collective-permute-start.10 = (bf16[16,1792]{1,0:T(8,128)(2,1)S(1)}, bf16[16,1792]{1,0:T(8,128)(2,1)S(1)}, u32[]{:S(2)}, u32[]{:S(2)}) collective-permute-start(bf16[16,1792]{1,0:T(8,128)(2,1)S(1)} %fusion.9), channel_id=1, source_target_pairs={{0,2},{1,3},{2,0},{3,1},{4,6},{5,7},{6,4},{7,5},{8,10},{9,11},{10,... | collective-permute-start | bytes 172040 | tf_op jit(solution)/shard_map/ppermute | solution.py:438
  59.9 5.7 %collective-permute-start.14 = (bf16[16,1792]{1,0:T(8,128)(2,1)S(1)}, bf16[16,1792]{1,0:T(8,128)(2,1)S(1)}, u32[]{:S(2)}, u32[]{:S(2)}) collective-permute-start(bf16[16,1792]{1,0:T(8,128)(2,1)S(1)} %fusion.10), channel_id=1, source_target_pairs={{0,2},{1,3},{2,0},{3,1},{4,6},{5,7},{6,4},{7,5},{8,10},{9,11},{10,... | collective-permute-start | bytes 172040 | tf_op jit(solution)/shard_map/ppermute | solution.py:438
